TPU v7x, 256 devices: a whole 4x4x8 slice. The times are simulated.
256 devices in a mesh: pair: 2 (over x_hi), row: 8 (over z), col: 16 (over y, x_lo, core).
Axes of the slice: x: 4 (x_hi: 2, x_lo: 2; x = x_hi * 2 + x_lo), y: 4, z: 8, core: 2. Of those that a mesh axis runs over, the one named last changes fastest.
Arguments:
- front_init: float32 [12288, 12288], P('row', ('pair', 'col')), may hold values from -24 to 24, as said below
- child_blocks: float32 [2, 8192, 8192], P('pair', 'row', 'col'), may hold values from -24 to 24, as said below
- tile_map: int32 [2, 64], replicated, may hold values from 0 to 95, as said below
Outputs:
- front_out: float32 [12288, 12288], P('row', ('pair', 'col'))
Inputs may be any that keep to these rules, and one draw needn't show every extreme that they name: `front_init`: symmetric positive definite in natural order, with smallest eigenvalue 0.5 or more. `child_blocks`: each sibling's block is symmetric positive definite in natural order. tile_map[s, i] mod (32) equals i mod (32); within each such residue class each sibling's map is increasing, and every parent tile is named by at least one of the two siblings.
All inputs are finite; a program needn't handle non-finite values.
Results may differ from a plain program's by a relative error of at most 0.0001.
Values sent between devices are 32-bit elements; how exact they have to be, the bound alone decides.
No kernel may reach another device: no remote copies, remote signals or barrier semaphores. Data moves between devices by JAX's collectives and lax.ppermute only.
A program may use at most 64 MiB of HBM per device.

v0:
```python
import jax
import jax.numpy as jnp
from jax import lax
from jax.sharding import PartitionSpec as P

NPIV = 1024
TILE = 128


def from_partner(block, axis, apart):
    count = lax.axis_size(axis)
    route = []
    for low in range(count):
        high = low | 1 << apart
        if high != low and high < count:
            route += [(low, high), (high, low)]
    return lax.ppermute(block, axis, route)


def from_root(shard, axis, root):
    mine = lax.axis_index(axis) == root
    return lax.psum(jnp.where(mine, shard, jnp.zeros_like(shard)), axis)


def place_tiles(contribution, row_targets, column_targets, row_count, column_count, tile_size):
    row_hot = (jnp.arange(row_count)[:, None] == row_targets[None, :]).astype(jnp.float32)
    column_hot = (jnp.arange(column_count)[:, None] == column_targets[None, :]).astype(jnp.float32)
    shaped = contribution.reshape(
        row_targets.shape[0], tile_size, column_targets.shape[0], tile_size
    )
    rows_placed = jnp.einsum("am,mxny->axny", row_hot, shaped, precision=lax.Precision.HIGHEST)
    placed = jnp.einsum("bn,axny->axby", column_hot, rows_placed, precision=lax.Precision.HIGHEST)
    return placed.reshape(row_count * tile_size, column_count * tile_size)


def lookup(table, wanted):
    hits = jnp.arange(table.shape[0])[None, :] == wanted[:, None]
    return jnp.sum(jnp.where(hits, table[None, :], 0), axis=1)


def solve_rows(leading, panel):
    return lax.linalg.triangular_solve(
        leading, panel, left_side=False, lower=True, transpose_a=True
    )


def body(front_init, child_blocks, tile_map):
    tile_size = TILE
    row_parts = lax.axis_size("row")
    col_count = lax.axis_size("col")
    column_parts = lax.axis_size("pair") * col_count
    sibling = lax.axis_index("pair")
    row_index = lax.axis_index("row")
    col_local_index = lax.axis_index("col")
    column_index = sibling * col_count + col_local_index
    own_block = child_blocks[0]
    child_rows = own_block.shape[0]
    child_columns = own_block.shape[1]
    child_row_tiles = child_rows // tile_size
    half_columns = child_columns // tile_size // 2
    paired = own_block.reshape(child_rows, half_columns, 2, tile_size)
    kept = lax.dynamic_index_in_dim(paired, sibling, 2, keepdims=False)
    handed = lax.dynamic_index_in_dim(paired, 1 - sibling, 2, keepdims=False)
    received = from_partner(handed, "pair", 0)
    front_rows, front_columns = front_init.shape
    row_tile_count = front_rows // tile_size
    column_tile_count = front_columns // tile_size
    child_row_ids = jnp.arange(child_row_tiles, dtype=jnp.int32) * row_parts + row_index
    child_column_ids = (
        2 * jnp.arange(half_columns, dtype=jnp.int32) + sibling
    ) * col_count + col_local_index
    own_map = lax.dynamic_index_in_dim(tile_map, sibling, 0, keepdims=False)
    other_map = lax.dynamic_index_in_dim(tile_map, 1 - sibling, 0, keepdims=False)

    def targets(mapping):
        row_targets = (lookup(mapping, child_row_ids) - row_index) // row_parts
        column_targets = (lookup(mapping, child_column_ids) - column_index) // column_parts
        return (row_targets, column_targets)

    own_rows, own_columns = targets(own_map)
    other_rows, other_columns = targets(other_map)
    working = front_init + place_tiles(
        kept, own_rows, own_columns, row_tile_count, column_tile_count, tile_size
    )
    working = working + place_tiles(
        received, other_rows, other_columns, row_tile_count, column_tile_count, tile_size
    )
    row_each = jnp.repeat(
        row_index + row_parts * jnp.arange(row_tile_count, dtype=jnp.int32), tile_size
    )
    column_each = jnp.repeat(
        column_index + column_parts * jnp.arange(column_tile_count, dtype=jnp.int32), tile_size
    )
    ratio = column_parts // row_parts
    first_row = column_index // row_parts

    def pick_rows(values):
        grouped = values.reshape(column_tile_count, ratio, tile_size, tile_size)
        chosen = lax.dynamic_index_in_dim(grouped, first_row, 1, keepdims=False)
        return chosen.reshape(column_tile_count * tile_size, tile_size)

    def step(current, working):
        row_local = current // row_parts
        column_local = current // column_parts
        holder = current % column_parts
        row_holder = current % row_parts
        column = lax.dynamic_slice_in_dim(working, column_local * tile_size, tile_size, 1)
        column_strip = from_root(column, ("pair", "col"), holder)
        corner = lax.dynamic_slice_in_dim(column_strip, row_local * tile_size, tile_size, 0)
        corner = from_root(corner, "row", row_holder)
        leading = jnp.linalg.cholesky(corner)
        solved = solve_rows(leading, column_strip)
        beneath = jnp.where(row_each[:, None] > current, solved, 0.0)
        across = from_root(pick_rows(solved), "row", column_index % row_parts)
        right_side = jnp.where(column_each[:, None] > current, across, 0.0)
        working = working - jnp.dot(beneath, right_side.T, precision=lax.Precision.HIGHEST)
        square = jnp.tril(leading) + jnp.triu(leading.T, 1)
        old_column = lax.dynamic_slice_in_dim(working, column_local * tile_size, tile_size, 1)
        square_rows = jnp.tile(square, (row_tile_count, 1))
        new_column = jnp.where(
            row_each[:, None] > current,
            solved,
            jnp.where(row_each[:, None] == current, square_rows, old_column),
        )
        new_column = jnp.where(holder == column_index, new_column, old_column)
        working = lax.dynamic_update_slice_in_dim(working, new_column, column_local * tile_size, 1)
        old_row = lax.dynamic_slice_in_dim(working, row_local * tile_size, tile_size, 0)
        square_columns = jnp.tile(square, (1, column_tile_count))
        new_row = jnp.where(
            column_each[None, :] > current,
            across.T,
            jnp.where(column_each[None, :] == current, square_columns, old_row),
        )
        new_row = jnp.where(row_holder == row_index, new_row, old_row)
        working = lax.dynamic_update_slice_in_dim(working, new_row, row_local * tile_size, 0)
        return working

    return lax.fori_loop(0, NPIV // TILE, step, working)


def solution(mesh):
    return jax.shard_map(
        body,
        mesh=mesh,
        in_specs=(P("row", ("pair", "col")), P("pair", "row", "col"), P()),
        out_specs=P("row", ("pair", "col")),
        check_vma=False,
    )
```

profile of v0, /device:TPU:2, one launch (start us, length us, event | category | flops | bytes accessed | tf_op | source)
XLA Modules:
  0.0 2423.1 jit_solution(13495401222883740048)
XLA Ops:
  18.8 3.6 fusion.19
  27.8 11.1 collective-permute-done
  41.7 3.6 fusion.17
  47.4 3.8 add_add_fusion
  51.2 2363.1 %while.17 = (s32[]{:T(128)}, f32[1536,384]{0,1:T(8,128)S(1)}, s32[]{:T(128)}, s32[]{:T(128)}, s32[]{:T(128)}, /*index=5*/s32[]{:T(128)}, s32[12]{0:T(128)S(1)}, ...) while((s32[]{:T(128)}, f32[1536,384]{0,1:T(8,128)S(1)}, ...), condition=%wide.region_10.11_spmd.clone, body=%wide.region_4.10_spmd.clone.sunk | while | flops 1210302720 | bytes 31994516 | solution.py:138
  52.7 119.2 %all-reduce.4.cloned.1.call-done = f32[1536,128]{0,1:T(8,128)} async-done(((f32[1536,128]{0,1:T(8,128)}), f32[1536,128]{0,1:T(8,128)}) %all-reduce.4.cloned.1.call-update) | async-done | bytes 786448 | tf_op jit(solution)/shard_map/while/body/eval_jaxpr/psum | solution.py:22
  173.6 72.1 %all-reduce.6.cloned.1.call-done = f32[128,128]{0,1:T(8,128)} async-done(((f32[128,128]{0,1:T(8,128)}), f32[128,128]{0,1:T(8,128)}) %all-reduce.6.cloned.1.call-update) | async-done | bytes 65552 | tf_op jit(solution)/shard_map/while/body/eval_jaxpr/psum | solution.py:22
  247.6 11.7 cholesky.71
  261.6 9.8 custom-call.24
  280.3 66.0 %all-reduce.8.cloned.1.call-done = f32[384,128]{1,0:T(8,128)} async-done(((f32[384,128]{1,0:T(8,128)}), f32[384,128]{1,0:T(8,128)}) %all-reduce.8.cloned.1.call-update) | async-done | bytes 196624 | tf_op jit(solution)/shard_map/while/body/eval_jaxpr/psum | solution.py:22
  352.2 114.4 %all-reduce.4.cloned.1.call-done = f32[1536,128]{0,1:T(8,128)} async-done(((f32[1536,128]{0,1:T(8,128)}), f32[1536,128]{0,1:T(8,128)}) %all-reduce.4.cloned.1.call-update) | async-done | bytes 786448 | tf_op jit(solution)/shard_map/while/body/eval_jaxpr/psum | solution.py:22
  468.3 71.9 %all-reduce.6.cloned.1.call-done = f32[128,128]{0,1:T(8,128)} async-done(((f32[128,128]{0,1:T(8,128)}), f32[128,128]{0,1:T(8,128)}) %all-reduce.6.cloned.1.call-update) | async-done | bytes 65552 | tf_op jit(solution)/shard_map/while/body/eval_jaxpr/psum | solution.py:22
  542.1 11.7 cholesky.71
  556.1 9.8 custom-call.24
  574.9 66.0 %all-reduce.8.cloned.1.call-done = f32[384,128]{1,0:T(8,128)} async-done(((f32[384,128]{1,0:T(8,128)}), f32[384,128]{1,0:T(8,128)}) %all-reduce.8.cloned.1.call-update) | async-done | bytes 196624 | tf_op jit(solution)/shard_map/while/body/eval_jaxpr/psum | solution.py:22
  646.8 114.6 %all-reduce.4.cloned.1.call-done = f32[1536,128]{0,1:T(8,128)} async-done(((f32[1536,128]{0,1:T(8,128)}), f32[1536,128]{0,1:T(8,128)}) %all-reduce.4.cloned.1.call-update) | async-done | bytes 786448 | tf_op jit(solution)/shard_map/while/body/eval_jaxpr/psum | solution.py:22
  763.1 72.1 %all-reduce.6.cloned.1.call-done = f32[128,128]{0,1:T(8,128)} async-done(((f32[128,128]{0,1:T(8,128)}), f32[128,128]{0,1:T(8,128)}) %all-reduce.6.cloned.1.call-update) | async-done | bytes 65552 | tf_op jit(solution)/shard_map/while/body/eval_jaxpr/psum | solution.py:22
  837.1 11.7 cholesky.71
  851.1 9.8 custom-call.24
  869.8 66.0 %all-reduce.8.cloned.1.call-done = f32[384,128]{1,0:T(8,128)} async-done(((f32[384,128]{1,0:T(8,128)}), f32[384,128]{1,0:T(8,128)}) %all-reduce.8.cloned.1.call-update) | async-done | bytes 196624 | tf_op jit(solution)/shard_map/while/body/eval_jaxpr/psum | solution.py:22
  941.8 114.3 %all-reduce.4.cloned.1.call-done = f32[1536,128]{0,1:T(8,128)} async-done(((f32[1536,128]{0,1:T(8,128)}), f32[1536,128]{0,1:T(8,128)}) %all-reduce.4.cloned.1.call-update) | async-done | bytes 786448 | tf_op jit(solution)/shard_map/while/body/eval_jaxpr/psum | solution.py:22
  1057.8 72.1 %all-reduce.6.cloned.1.call-done = f32[128,128]{0,1:T(8,128)} async-done(((f32[128,128]{0,1:T(8,128)}), f32[128,128]{0,1:T(8,128)}) %all-reduce.6.cloned.1.call-update) | async-done | bytes 65552 | tf_op jit(solution)/shard_map/while/body/eval_jaxpr/psum | solution.py:22
  1131.8 11.7 cholesky.71
  1145.8 9.8 custom-call.24
  1164.6 66.0 %all-reduce.8.cloned.1.call-done = f32[384,128]{1,0:T(8,128)} async-done(((f32[384,128]{1,0:T(8,128)}), f32[384,128]{1,0:T(8,128)}) %all-reduce.8.cloned.1.call-update) | async-done | bytes 196624 | tf_op jit(solution)/shard_map/while/body/eval_jaxpr/psum | solution.py:22
  1230.6 3.5 convolution_subtract_fusion.2
  1236.5 114.6 %all-reduce.4.cloned.1.call-done = f32[1536,128]{0,1:T(8,128)} async-done(((f32[1536,128]{0,1:T(8,128)}), f32[1536,128]{0,1:T(8,128)}) %all-reduce.4.cloned.1.call-update) | async-done | bytes 786448 | tf_op jit(solution)/shard_map/while/body/eval_jaxpr/psum | solution.py:22
  1352.8 71.9 %all-reduce.6.cloned.1.call-done = f32[128,128]{0,1:T(8,128)} async-done(((f32[128,128]{0,1:T(8,128)}), f32[128,128]{0,1:T(8,128)}) %all-reduce.6.cloned.1.call-update) | async-done | bytes 65552 | tf_op jit(solution)/shard_map/while/body/eval_jaxpr/psum | solution.py:22
  1426.6 11.7 cholesky.71
  1440.6 9.8 custom-call.24
  1459.3 66.0 %all-reduce.8.cloned.1.call-done = f32[384,128]{1,0:T(8,128)} async-done(((f32[384,128]{1,0:T(8,128)}), f32[384,128]{1,0:T(8,128)}) %all-reduce.8.cloned.1.call-update) | async-done | bytes 196624 | tf_op jit(solution)/shard_map/while/body/eval_jaxpr/psum | solution.py:22
  1525.4 3.5 convolution_subtract_fusion.2
  1531.3 114.3 %all-reduce.4.cloned.1.call-done = f32[1536,128]{0,1:T(8,128)} async-done(((f32[1536,128]{0,1:T(8,128)}), f32[1536,128]{0,1:T(8,128)}) %all-reduce.4.cloned.1.call-update) | async-done | bytes 786448 | tf_op jit(solution)/shard_map/while/body/eval_jaxpr/psum | solution.py:22
  1647.3 71.9 %all-reduce.6.cloned.1.call-done = f32[128,128]{0,1:T(8,128)} async-done(((f32[128,128]{0,1:T(8,128)}), f32[128,128]{0,1:T(8,128)}) %all-reduce.6.cloned.1.call-update) | async-done | bytes 65552 | tf_op jit(solution)/shard_map/while/body/eval_jaxpr/psum | solution.py:22
  1721.1 11.7 cholesky.71
  1735.1 9.8 custom-call.24
  1753.8 66.0 %all-reduce.8.cloned.1.call-done = f32[384,128]{1,0:T(8,128)} async-done(((f32[384,128]{1,0:T(8,128)}), f32[384,128]{1,0:T(8,128)}) %all-reduce.8.cloned.1.call-update) | async-done | bytes 196624 | tf_op jit(solution)/shard_map/while/body/eval_jaxpr/psum | solution.py:22
  1819.9 3.5 convolution_subtract_fusion.2
  1825.8 114.6 %all-reduce.4.cloned.1.call-done = f32[1536,128]{0,1:T(8,128)} async-done(((f32[1536,128]{0,1:T(8,128)}), f32[1536,128]{0,1:T(8,128)}) %all-reduce.4.cloned.1.call-update) | async-done | bytes 786448 | tf_op jit(solution)/shard_map/while/body/eval_jaxpr/psum | solution.py:22
  1942.1 71.9 %all-reduce.6.cloned.1.call-done = f32[128,128]{0,1:T(8,128)} async-done(((f32[128,128]{0,1:T(8,128)}), f32[128,128]{0,1:T(8,128)}) %all-reduce.6.cloned.1.call-update) | async-done | bytes 65552 | tf_op jit(solution)/shard_map/while/body/eval_jaxpr/psum | solution.py:22
  2015.9 11.7 cholesky.71
  2029.9 9.8 custom-call.24
  2048.6 66.0 %all-reduce.8.cloned.1.call-done = f32[384,128]{1,0:T(8,128)} async-done(((f32[384,128]{1,0:T(8,128)}), f32[384,128]{1,0:T(8,128)}) %all-reduce.8.cloned.1.call-update) | async-done | bytes 196624 | tf_op jit(solution)/shard_map/while/body/eval_jaxpr/psum | solution.py:22
  2120.6 114.7 %all-reduce.4.cloned.1.call-done = f32[1536,128]{0,1:T(8,128)} async-done(((f32[1536,128]{0,1:T(8,128)}), f32[1536,128]{0,1:T(8,128)}) %all-reduce.4.cloned.1.call-update) | async-done | bytes 786448 | tf_op jit(solution)/shard_map/while/body/eval_jaxpr/psum | solution.py:22
  2237.0 72.1 %all-reduce.6.cloned.1.call-done = f32[128,128]{0,1:T(8,128)} async-done(((f32[128,128]{0,1:T(8,128)}), f32[128,128]{0,1:T(8,128)}) %all-reduce.6.cloned.1.call-update) | async-done | bytes 65552 | tf_op jit(solution)/shard_map/while/body/eval_jaxpr/psum | solution.py:22
  2310.9 11.7 cholesky.71
  2324.9 9.8 custom-call.24
  2343.7 66.0 %all-reduce.8.cloned.1.call-done = f32[384,128]{1,0:T(8,128)} async-done(((f32[384,128]{1,0:T(8,128)}), f32[384,128]{1,0:T(8,128)}) %all-reduce.8.cloned.1.call-update) | async-done | bytes 196624 | tf_op jit(solution)/shard_map/while/body/eval_jaxpr/psum | solution.py:22
  (335 shorter events, 177.5 us)
Async XLA Ops:
  8.5 5.9 copy-start.3
  12.2 26.7 %collective-permute-start = (f32[1024,2,128]{2,0,1:T(8,128)}, f32[1024,2,128]{2,0,1:T(8,128)}, u32[]{:S(2)}, u32[]{:S(2)}) collective-permute-start(f32[1024,2,128]{2,0,1:T(8,128)} %bitcast.11), channel_id=1, source_target_pairs={{0,128},{128,0},{1,129},{129,1},{2,130},{130,2},{3,131},{131,3},{4... | collective-permute-start | bytes 3145736 | tf_op jit(solution)/shard_map/ppermute | solution.py:17
  51.4 120.5 %all-reduce.4.cloned.1.call-start = ((), (), s32[]{:S(2)}) async-start(), calls=%async_computation | async-start | bytes 1572864 | tf_op jit(solution)/shard_map/while/body/eval_jaxpr/psum | solution.py:22
  52.5 193.2 %all-reduce.6.cloned.1.call-start = ((), (), s32[]{:S(2)}) async-start(), calls=%async_computation.1 | async-start | bytes 131072 | tf_op jit(solution)/shard_map/while/body/eval_jaxpr/psum | solution.py:22
  173.4 173.0 %all-reduce.8.cloned.1.call-start = ((), (), s32[]{:S(2)}) async-start(), calls=%async_computation.2 | async-start | bytes 393216 | tf_op jit(solution)/shard_map/while/body/eval_jaxpr/psum | solution.py:22
  273.9 0.9 copy-start
  346.4 3.5 copy-start.1
  349.8 0.9 copy-start.2
  350.9 115.7 %all-reduce.4.cloned.1.call-start = ((), (), s32[]{:S(2)}) async-start(), calls=%async_computation | async-start | bytes 1572864 | tf_op jit(solution)/shard_map/while/body/eval_jaxpr/psum | solution.py:22
  352.0 188.2 %all-reduce.6.cloned.1.call-start = ((), (), s32[]{:S(2)}) async-start(), calls=%async_computation.1 | async-start | bytes 131072 | tf_op jit(solution)/shard_map/while/body/eval_jaxpr/psum | solution.py:22
  468.1 172.8 %all-reduce.8.cloned.1.call-start = ((), (), s32[]{:S(2)}) async-start(), calls=%async_computation.2 | async-start | bytes 393216 | tf_op jit(solution)/shard_map/while/body/eval_jaxpr/psum | solution.py:22
  568.5 0.9 copy-start
  640.9 3.5 copy-start.1
  644.4 0.9 copy-start.2
  645.5 115.9 %all-reduce.4.cloned.1.call-start = ((), (), s32[]{:S(2)}) async-start(), calls=%async_computation | async-start | bytes 1572864 | tf_op jit(solution)/shard_map/while/body/eval_jaxpr/psum | solution.py:22
  646.5 188.6 %all-reduce.6.cloned.1.call-start = ((), (), s32[]{:S(2)}) async-start(), calls=%async_computation.1 | async-start | bytes 131072 | tf_op jit(solution)/shard_map/while/body/eval_jaxpr/psum | solution.py:22
  762.9 173.0 %all-reduce.8.cloned.1.call-start = ((), (), s32[]{:S(2)}) async-start(), calls=%async_computation.2 | async-start | bytes 393216 | tf_op jit(solution)/shard_map/while/body/eval_jaxpr/psum | solution.py:22
  863.4 0.9 copy-start
  935.9 3.5 copy-start.1
  939.3 0.9 copy-start.2
  940.5 115.7 %all-reduce.4.cloned.1.call-start = ((), (), s32[]{:S(2)}) async-start(), calls=%async_computation | async-start | bytes 1572864 | tf_op jit(solution)/shard_map/while/body/eval_jaxpr/psum | solution.py:22
  941.5 188.4 %all-reduce.6.cloned.1.call-start = ((), (), s32[]{:S(2)}) async-start(), calls=%async_computation.1 | async-start | bytes 131072 | tf_op jit(solution)/shard_map/while/body/eval_jaxpr/psum | solution.py:22
  1057.6 173.0 %all-reduce.8.cloned.1.call-start = ((), (), s32[]{:S(2)}) async-start(), calls=%async_computation.2 | async-start | bytes 393216 | tf_op jit(solution)/shard_map/while/body/eval_jaxpr/psum | solution.py:22
  1158.2 0.9 copy-start
  1230.6 3.5 copy-start.1
  1234.1 0.9 copy-start.2
  1235.2 115.9 %all-reduce.4.cloned.1.call-start = ((), (), s32[]{:S(2)}) async-start(), calls=%async_computation | async-start | bytes 1572864 | tf_op jit(solution)/shard_map/while/body/eval_jaxpr/psum | solution.py:22
  1236.2 188.5 %all-reduce.6.cloned.1.call-start = ((), (), s32[]{:S(2)}) async-start(), calls=%async_computation.1 | async-start | bytes 131072 | tf_op jit(solution)/shard_map/while/body/eval_jaxpr/psum | solution.py:22
  1352.6 172.8 %all-reduce.8.cloned.1.call-start = ((), (), s32[]{:S(2)}) async-start(), calls=%async_computation.2 | async-start | bytes 393216 | tf_op jit(solution)/shard_map/while/body/eval_jaxpr/psum | solution.py:22
  1525.4 3.5 copy-start.1
  1528.9 0.9 copy-start.2
  1530.0 115.6 %all-reduce.4.cloned.1.call-start = ((), (), s32[]{:S(2)}) async-start(), calls=%async_computation | async-start | bytes 1572864 | tf_op jit(solution)/shard_map/while/body/eval_jaxpr/psum | solution.py:22
  1531.0 188.2 %all-reduce.6.cloned.1.call-start = ((), (), s32[]{:S(2)}) async-start(), calls=%async_computation.1 | async-start | bytes 131072 | tf_op jit(solution)/shard_map/while/body/eval_jaxpr/psum | solution.py:22
  1647.1 172.8 %all-reduce.8.cloned.1.call-start = ((), (), s32[]{:S(2)}) async-start(), calls=%async_computation.2 | async-start | bytes 393216 | tf_op jit(solution)/shard_map/while/body/eval_jaxpr/psum | solution.py:22
  1819.9 3.5 copy-start.1
  1823.4 0.9 copy-start.2
  1824.5 115.9 %all-reduce.4.cloned.1.call-start = ((), (), s32[]{:S(2)}) async-start(), calls=%async_computation | async-start | bytes 1572864 | tf_op jit(solution)/shard_map/while/body/eval_jaxpr/psum | solution.py:22
  1825.5 188.5 %all-reduce.6.cloned.1.call-start = ((), (), s32[]{:S(2)}) async-start(), calls=%async_computation.1 | async-start | bytes 131072 | tf_op jit(solution)/shard_map/while/body/eval_jaxpr/psum | solution.py:22
  1941.8 172.8 %all-reduce.8.cloned.1.call-start = ((), (), s32[]{:S(2)}) async-start(), calls=%async_computation.2 | async-start | bytes 393216 | tf_op jit(solution)/shard_map/while/body/eval_jaxpr/psum | solution.py:22
  2042.2 0.9 copy-start
  2114.7 3.5 copy-start.1
  2118.1 0.9 copy-start.2
  2119.2 116.0 %all-reduce.4.cloned.1.call-start = ((), (), s32[]{:S(2)}) async-start(), calls=%async_computation | async-start | bytes 1572864 | tf_op jit(solution)/shard_map/while/body/eval_jaxpr/psum | solution.py:22
  2120.3 188.7 %all-reduce.6.cloned.1.call-start = ((), (), s32[]{:S(2)}) async-start(), calls=%async_computation.1 | async-start | bytes 131072 | tf_op jit(solution)/shard_map/while/body/eval_jaxpr/psum | solution.py:22
  2236.7 173.0 %all-reduce.8.cloned.1.call-start = ((), (), s32[]{:S(2)}) async-start(), calls=%async_computation.2 | async-start | bytes 393216 | tf_op jit(solution)/shard_map/while/body/eval_jaxpr/psum | solution.py:22
  2337.3 0.9 copy-start
  2409.7 3.5 copy-start.1
  2413.2 0.9 copy-start.2
  (2 other events, 1.8 us)
Sparse Core Ops, SparseCore 0:
  55.5 116.3 all-reduce.3
  174.2 71.4 all-reduce.5
  275.6 70.6 all-reduce.7
  354.7 111.8 all-reduce.3
  468.7 71.4 all-reduce.5
  570.2 70.6 all-reduce.7
  649.6 111.7 all-reduce.3
  763.7 71.4 all-reduce.5
  865.2 70.6 all-reduce.7
  944.2 111.8 all-reduce.3
  1058.4 71.4 all-reduce.5
  1159.9 70.6 all-reduce.7
  1239.3 111.7 all-reduce.3
  1353.2 71.4 all-reduce.5
  1454.7 70.6 all-reduce.7
  1533.7 111.7 all-reduce.3
  1647.7 71.4 all-reduce.5
  1749.2 70.6 all-reduce.7
  1828.5 111.7 all-reduce.3
  1942.5 71.4 all-reduce.5
  2043.9 70.6 all-reduce.7
  2123.3 111.8 all-reduce.3
  2237.6 71.4 all-reduce.5
  2339.0 70.6 all-reduce.7
where the time goes:
time: 2430 us; the launch traced here: 2420 us
  waiting for transfers between devices  2040 us (84%)
  other arithmetic  228 us (9%)
  local copies, waits for them, and re-layouts  78.6 us (3%)
  matrix products  60.4 us (2%)
    psum x24, waiting for transfers between devices, from_root(): return lax.psum(jnp.where(mine, shard, jnp.zeros_like(shard)), axis)  2020 us
    another operation x24, other arithmetic, step(): leading = jnp.linalg.cholesky(corner)  99.8 us
    another operation x16, other arithmetic, solve_rows(): lax.linalg.triangular_solve(leading, panel, left_side=False, lower=True,...  78.6 us
  transfers between devices with their start and end apart: 25, of which 25 were waited for; matrix products, arithmetic and copies ran while one was open for 2% of the time, Pallas kernels for 0%

commit v1 on v0

v1 whole, which is shorter than its diff:
```python
import jax
import jax.numpy as jnp
from jax import lax
from jax.experimental import pallas as pl
from jax.experimental.pallas import tpu as pltpu
from jax.sharding import PartitionSpec as P

TILE = 128
PIVOT_TILES = 8
NPIV = TILE * PIVOT_TILES
STRIP = 32
EXACT = lax.Precision.HIGHEST


def exact_dot(a, b, contract=((1,), (0,))):
    return lax.dot_general(
        a, b, (contract, ((), ())), precision=EXACT, preferred_element_type=jnp.float32
    )


def split(x):
    high = x.astype(jnp.bfloat16)
    low = (x - high.astype(jnp.float32)).astype(jnp.bfloat16)
    return high, low


def split_dot(a, b, contract):
    dims = (contract, ((), ()))
    a_high, a_low = a
    b_high, b_low = b

    def one(x, y):
        return lax.dot_general(x, y, dims, preferred_element_type=jnp.float32)

    return one(a_high, b_high) + (one(a_high, b_low) + one(a_low, b_high))


def factor_tile(block):
    row = lax.broadcasted_iota(jnp.int32, (TILE, TILE), 0)
    lane = lax.broadcasted_iota(jnp.int32, (TILE, TILE), 1)
    remaining = jnp.concatenate([block, (row == lane).astype(jnp.float32)], axis=1)
    strip_row = lax.broadcasted_iota(jnp.int32, (STRIP, 1), 0)
    wide_row = lax.broadcasted_iota(jnp.int32, (STRIP, 2 * TILE), 0)
    wide_lane = lax.broadcasted_iota(jnp.int32, (STRIP, 2 * TILE), 1)
    done = []
    for first in range(0, TILE, STRIP):
        strip = remaining[:STRIP]
        for k in range(STRIP):
            at = first + k
            column = strip[:, at : at + 1]
            pivot_row = strip[k : k + 1]
            pivot = strip[k : k + 1, at : at + 1]
            factor = jnp.where(strip_row > k, column * (1.0 / pivot), 0.0)
            strip = strip - factor * pivot_row
        diagonal = jnp.sum(
            jnp.where(wide_lane == wide_row + first, strip, 0.0), axis=1, keepdims=True
        )
        root = lax.rsqrt(diagonal)
        root = root * (1.5 - 0.5 * diagonal * root * root)
        strip = strip * root
        done.append(strip)
        if first + STRIP < TILE:
            change = exact_dot(strip[:, :TILE], strip, ((0,), (0,)))
            remaining = remaining[STRIP:] - change[first + STRIP :]
    whole = jnp.concatenate(done, axis=0)
    return jnp.where(lane >= row, whole[:, :TILE], 0.0), whole[:, TILE:]


def factor_kernel(parts_ref, upper_ref, lower_ref, inverse_ref):
    for i in range(PIVOT_TILES):
        for c in range(i, PIVOT_TILES):
            for k in range(4):
                upper_ref[pl.ds(i * TILE + k * 32, 32), pl.ds(c * TILE, TILE)] = parts_ref[k, c, i]

    def step(j, carry):
        at = pl.ds(pl.multiple_of(j * TILE, TILE), TILE)
        upper, inverse = factor_tile(upper_ref[at, at])
        upper_ref[at, at] = upper
        lower_ref[at, at] = upper.T
        inverse_ref[j] = inverse
        for now in range(PIVOT_TILES - 1):

            @pl.when(j == now)
            def _():
                here = slice(now * TILE, (now + 1) * TILE)
                after = slice((now + 1) * TILE, NPIV)
                solved = exact_dot(inverse, upper_ref[here, after])
                upper_ref[here, after] = solved
                lower_ref[after, here] = solved.T
                for k in range(now + 1, PIVOT_TILES):
                    rows = slice(k * TILE, (k + 1) * TILE)
                    rest = slice(k * TILE, NPIV)
                    offset = (k - now - 1) * TILE
                    upper_ref[rows, rest] = upper_ref[rows, rest] - exact_dot(
                        solved[:, offset : offset + TILE], solved[:, offset:], ((0,), (0,))
                    )

        return carry

    lax.fori_loop(0, PIVOT_TILES, step, 0)


def factor(parts):
    return pl.pallas_call(
        factor_kernel,
        out_shape=(
            jax.ShapeDtypeStruct((NPIV, NPIV), jnp.float32),
            jax.ShapeDtypeStruct((NPIV, NPIV), jnp.float32),
            jax.ShapeDtypeStruct((PIVOT_TILES, TILE, TILE), jnp.float32),
        ),
        in_specs=[pl.BlockSpec(memory_space=pltpu.VMEM)],
        out_specs=tuple(pl.BlockSpec(memory_space=pltpu.VMEM) for _ in range(3)),
        compiler_params=pltpu.CompilerParams(vmem_limit_bytes=40 * 2**20),
        cost_estimate=pl.CostEstimate(
            flops=60 * 10**9, bytes_accessed=13 * 2**20, transcendentals=0
        ),
        name="factor_pivots",
    )(parts)


def finish_kernel(
    meta_ref,
    front_ref,
    child_ref,
    received_ref,
    across_ref,
    beneath_ref,
    upper_ref,
    lower_ref,
    inverse_ref,
    out_ref,
    solved_ref,
    column_high_ref,
    column_low_ref,
    column_ref,
):
    group = pl.program_id(0)
    sibling = meta_ref[0]
    row_index = meta_ref[1]
    column_index = meta_ref[2]

    def solve(source, target_ref):
        for j in range(PIVOT_TILES):
            rows = slice(j * TILE, (j + 1) * TILE)
            rest = source(rows)
            if j:
                rest = rest - exact_dot(lower_ref[rows, : j * TILE], target_ref[: j * TILE, :])
            target_ref[rows, :] = exact_dot(inverse_ref[j], rest)

    @pl.when(group == 0)
    def _():
        solve(lambda rows: across_ref[rows, :], column_ref)
        high, low = split(column_ref[...])
        column_high_ref[...] = high
        column_low_ref[...] = low

    solve(lambda rows: beneath_ref[0, rows, :], solved_ref)
    update = split_dot(
        split(solved_ref[...]), (column_high_ref[...], column_low_ref[...]), ((0,), (0,))
    )

    def row_slot(s, u):
        return meta_ref[4 + s * 8 + group * 2 + u]

    def column_slot(s, u):
        return meta_ref[20 + s * 2 + u]

    for m in range(3):
        for n in range(3):
            lanes = slice(n * TILE, (n + 1) * TILE)
            total = front_ref[m, 0, :, lanes]
            for u in range(2):
                for v in range(2):
                    if m - u in (0, 1) and n - v in (0, 1):
                        own = (row_slot(sibling, u) == m) & (column_slot(sibling, v) == n)
                        other = (row_slot(1 - sibling, u) == m) & (
                            column_slot(1 - sibling, v) == n
                        )
                        mine = child_ref[
                            u, 0, :, pl.ds(pl.multiple_of((2 * v + sibling) * TILE, TILE), TILE)
                        ]
                        theirs = received_ref[u, 0, :, v * TILE : (v + 1) * TILE]
                        total = total + jnp.where(own, mine, 0.0)
                        total = total + jnp.where(other, theirs, 0.0)
            out_ref[m, 0, :, lanes] = (
                total - update[m * TILE : (m + 1) * TILE, n * TILE : (n + 1) * TILE]
            )

    pivot_column = column_index < PIVOT_TILES

    @pl.when(pivot_column)
    def _():
        rows = pl.ds(pl.multiple_of(column_index * TILE, TILE), TILE)
        for m in range(3):
            out_ref[m, 0, :, :TILE] = solved_ref[rows, m * TILE : (m + 1) * TILE].T

    @pl.when(group == 0)
    def _():
        rows = pl.ds(pl.multiple_of(row_index * TILE, TILE), TILE)
        out_ref[0, 0, :, :] = column_ref[rows, :]

        @pl.when(pivot_column)
        def _():
            columns = pl.ds(pl.multiple_of(column_index * TILE, TILE), TILE)
            above = upper_ref[rows, columns]
            below = lower_ref[rows, columns]

            @pl.when(row_index < column_index)
            def _():
                out_ref[0, 0, :, :TILE] = above

            @pl.when(row_index > column_index)
            def _():
                out_ref[0, 0, :, :TILE] = below

            @pl.when(row_index == column_index)
            def _():
                row = lax.broadcasted_iota(jnp.int32, (TILE, TILE), 0)
                lane = lax.broadcasted_iota(jnp.int32, (TILE, TILE), 1)
                out_ref[0, 0, :, :TILE] = jnp.where(row > lane, below, above)


def finish(meta, front, child, received, across, beneath, upper, lower, inverse):
    width = front.shape[1]
    whole = pl.BlockSpec(memory_space=pltpu.VMEM)
    out = pl.pallas_call(
        finish_kernel,
        grid=(4,),
        out_shape=jax.ShapeDtypeStruct((3, 4, TILE, width), jnp.float32),
        in_specs=[
            pl.BlockSpec(memory_space=pltpu.SMEM),
            pl.BlockSpec((3, 1, TILE, width), lambda g: (0, g, 0, 0)),
            pl.BlockSpec((2, 1, TILE, 4 * TILE), lambda g: (0, g, 0, 0)),
            pl.BlockSpec((2, 1, TILE, 2 * TILE), lambda g: (0, g, 0, 0)),
            whole,
            pl.BlockSpec((1, NPIV, width), lambda g: (g, 0, 0)),
            whole,
            whole,
            whole,
        ],
        out_specs=pl.BlockSpec((3, 1, TILE, width), lambda g: (0, g, 0, 0)),
        scratch_shapes=[
            pltpu.VMEM((NPIV, width), jnp.float32),
            pltpu.VMEM((NPIV, width), jnp.bfloat16),
            pltpu.VMEM((NPIV, width), jnp.bfloat16),
            pltpu.VMEM((NPIV, width), jnp.float32),
        ],
        compiler_params=pltpu.CompilerParams(vmem_limit_bytes=48 * 2**20),
        cost_estimate=pl.CostEstimate(
            flops=25 * 10**9, bytes_accessed=30 * 2**20, transcendentals=0
        ),
        name="solve_and_update",
    )(
        meta,
        front.reshape(3, 4, TILE, width),
        child.reshape(2, 4, TILE, 4 * TILE),
        received.reshape(2, 4, TILE, 2 * TILE),
        across,
        beneath,
        upper,
        lower,
        inverse,
    )
    return out.reshape(front.shape)


ALL = ("pair", "row", "col")


def at(pair, row, col):
    return (pair * 8 + row) * 16 + col


def body(front_init, child_blocks, tile_map):
    sibling = lax.axis_index("pair")
    row_index = lax.axis_index("row")
    col_index = lax.axis_index("col")
    column_index = sibling * 16 + col_index
    own = child_blocks[0]
    tiled_map = tile_map.astype(jnp.int32).reshape(2, 2, 32)
    positions = tiled_map // 32
    row_positions = jnp.swapaxes(
        lax.dynamic_index_in_dim(positions.reshape(2, 2, 4, 8), row_index, 3, keepdims=False), 1, 2
    )
    column_positions = lax.dynamic_index_in_dim(positions, column_index, 2, keepdims=False)
    meta = jnp.concatenate(
        [
            jnp.stack([sibling, row_index, column_index, column_index]),
            row_positions.reshape(16),
            column_positions.reshape(4),
        ]
    ).astype(jnp.int32)

    with jax.named_scope("pivot_rows"):
        first = own[:TILE].reshape(TILE, 2, 2, TILE)
        even, odd = first[:, :, 0], first[:, :, 1]
        kept = jnp.where(sibling == 0, even, odd)
        handed = jnp.where(sibling == 0, odd, even)
        received_first = lax.ppermute(handed, "pair", [(0, 1), (1, 0)])
        pieces = []
        own_row = row_positions[sibling, 0, 0] == 0
        other_row = row_positions[1 - sibling, 0, 0] == 0
        for n in range(3):
            total = front_init[:TILE, n * TILE : (n + 1) * TILE]
            for v in range(2):
                if n - v in (0, 1):
                    hit = own_row & (column_positions[sibling, v] == n)
                    total = total + jnp.where(hit, kept[:, v], 0.0)
                    hit = other_row & (column_positions[1 - sibling, v] == n)
                    total = total + jnp.where(hit, received_first[:, v], 0.0)
            pieces.append(total)
        pivot_rows = jnp.concatenate(pieces, axis=1)

    with jax.named_scope("pivot_block"):
        tile = pieces[0].reshape(4, 32, TILE)
        mine = tile[0]
        for k in range(1, 4):
            pair, half = divmod(k, 2)
            route = [
                (at(0, i, c), at(pair, i, c + 8 * half)) for i in range(8) for c in range(8)
            ]
            came = lax.ppermute(tile[k], ALL, route)
            mine = jnp.where((sibling == pair) & (col_index // 8 == half), came, mine)
        stacked = lax.all_gather(mine, "row")
        parts = lax.all_gather(stacked, ("pair", "col"))
        parts = parts.reshape(4, 8, 8, 32, TILE)

    with jax.named_scope("panel"):
        pivot_rows, parts = lax.optimization_barrier((pivot_rows, parts))
        across = lax.all_gather(pivot_rows, "row").reshape(NPIV, -1)
        route = []
        for pair in range(2):
            for i in range(8):
                for c in range(16):
                    half, other = divmod(c, 8)
                    route.append((at(pair, i, c), at(pair, other, 8 * half + i)))
        turned = lax.ppermute(pivot_rows, ALL, route)
        beneath = lax.all_gather(turned, ("pair", "col")).reshape(4, NPIV, -1)

    with jax.named_scope("siblings"):
        rows = own.reshape(NPIV, 2, 2, TILE)
        handed = jnp.where(sibling == 0, rows[:, :, 1], rows[:, :, 0]).reshape(NPIV, 2 * TILE)
        handed, parts = lax.optimization_barrier((handed, parts))
        received = lax.ppermute(handed, "pair", [(0, 1), (1, 0)])

    with jax.named_scope("factor"):
        upper, lower, inverse = factor(parts)
    with jax.named_scope("finish"):
        return finish(
            meta, front_init, own, received, across, beneath, upper, lower, inverse
        )


def solution(mesh):
    return jax.shard_map(
        body,
        mesh=mesh,
        in_specs=(P("row", ("pair", "col")), P("pair", "row", "col"), P()),
        out_specs=P("row", ("pair", "col")),
        check_vma=False,
    )
```

time: 2430 us -> 317 us (0.13)
  waiting for transfers between devices: 2040 us -> 80 us
  other arithmetic: 228 us -> 7.84 us
  Pallas kernels: 0 us -> 143 us
  local copies, waits for them, and re-layouts: 78.6 us -> 17.4 us
  matrix products: 60.4 us -> 0 us
  blocking collectives: 0 us -> 30.2 us
    psum x24 -> x0, waiting for transfers between devices: 2020 us -> none  [from_root(): return lax.psum(jnp.where(mine, shard, jnp.zeros_like(shard)), axis)]
    another operation x40 -> x0, other arithmetic: 178 us -> none  [the longest x24 99.8 us: step(): leading = jnp.linalg.cholesky(corner)]
    pallas_call x0 -> x2, Pallas kernels: none -> 143 us  [the longest x1 101 us: factor(): pl.pallas_call(factor_kernel, out_shape=(jax.ShapeDtypeStruct((NPIV, NPIV...]
    all_gather x0 -> x3, waiting for transfers between devices: none -> 59.9 us  [the longest x1 59.9 us: body(): parts = lax.all_gather(stacked, ('pair', 'col'))]
    dot_general x12 -> x0, matrix products: 40.2 us -> none  [the longest x8 27.6 us: step(): jnp.dot(beneath, right_side.T, precision=lax.Precision.HIGHEST)]
    another operation x40 -> x2, local copies, waits for them, and re-layouts: 38.7 us -> 3.03 us  [the longest x1 2.35 us: body(): rows = own.reshape(NPIV, 2, 2, TILE)]
    all_gather x0 -> x1, blocking collectives: none -> 30.2 us  [body(): stacked = lax.all_gather(mine, 'row')]
  transfers between devices with their start and end apart: 25 -> 9, of which waited for: 25 -> 4; matrix products, arithmetic and copies ran while one was open for 2% -> 4% of each run, Pallas kernels for 0% -> 32%
where the time goes in v1:
time: 317 us; the launch traced here: 314 us
  Pallas kernels  143 us (45%)
  waiting for transfers between devices  80 us (25%)
  blocking collectives  30.2 us (10%)
  between operations  19.7 us (6%)
  local copies, waits for them, and re-layouts  17.4 us (5%)
  starting transfers between devices  16.4 us (5%)
  other arithmetic  7.84 us (2%)
    pallas_call x1, Pallas kernels, factor(): pl.pallas_call(factor_kernel, out_shape=(jax.ShapeDtypeStruct((NPIV, NPIV...  101 us
    all_gather x1, waiting for transfers between devices, body(): parts = lax.all_gather(stacked, ('pair', 'col'))  59.9 us
    pallas_call x1, Pallas kernels, finish(): pl.pallas_call(finish_kernel, grid=(4,), out_shape=jax.ShapeDtypeStruct((...  41.2 us
    all_gather x1, blocking collectives, body(): stacked = lax.all_gather(mine, 'row')  30.2 us
    ppermute x1, waiting for transfers between devices, body(): turned = lax.ppermute(pivot_rows, ALL, route)  18.6 us
    unnamed x22, local copies, waits for them, and re-layouts  11.6 us
    ppermute x3, starting transfers between devices, body(): came = lax.ppermute(tile[k], ALL, route)  8.52 us
  transfers between devices with their start and end apart: 9, of which 4 were waited for; matrix products, arithmetic and copies ran while one was open for 4% of the time, Pallas kernels for 32%

profile of v1, /device:TPU:2, one launch (start us, length us, event | category | flops | bytes accessed | tf_op | source)
XLA Modules:
  0.0 314.2 jit_solution(12217278940032038438)
XLA Ops:
  6.5 0.0 all-gather.8.cloned.1.call-start
  6.5 1.1 slice.60
  7.7 0.1 copy.13
  7.8 0.1 copy.14
  7.9 0.1 copy.15
  8.1 2.2 collective-permute-start
  10.3 0.1 reshape.117
  10.4 0.1 reshape.115
  10.5 0.7 constant_dynamic-slice_fusion.2
  16.2 0.7 constant_dynamic-slice_fusion.3
  18.3 0.0 collective-permute-done
  18.3 1.0 bitcast_add_fusion.6
  19.3 5.9 %collective-permute-start.1 = (f32[32,128]{1,0:T(8,128)S(1)}, f32[32,128]{1,0:T(8,128)S(1)}, u32[]{:S(2)}, u32[]{:S(2)}) collective-permute-start(f32[32,128]{1,0:T(8,128)S(1)} %get-tuple-element.28), channel_id=1, source_target_pairs={{0,136},{1,137},{2,138},{3,139},{4,140},{5,141},{6,142},{7,143},{1... | collective-permute-start | bytes 49160 | tf_op jit(solution)/shard_map/pivot_block/ppermute | solution.py:322
  25.2 1.3 collective-permute-start.2
  26.5 1.3 collective-permute-start.3
  27.8 0.0 collective-permute-done.1
  27.9 0.1 collective-permute-done.2
  27.9 1.3 collective-permute-done.3
  29.2 30.2 %all-gather = f32[256,128]{1,0:T(8,128)} all-gather(f32[32,128]{1,0:T(8,128)S(1)} %fusion.2), channel_id=2, replica_groups=mesh['pair'=2,'row'=8,'col'=16] {'row'}, dimensions={0}, use_global_device_ids=true | all-gather | bytes 147456 | tf_op jit(solution)/shard_map/pivot_block/all_gather | solution.py:324
  59.4 0.0 all-gather.8.cloned.1.call-update
  59.5 0.0 all-gather.10.cloned.1.call-start
  59.5 0.7 pad_maximum_fusion
  60.2 59.9 %all-gather.8.cloned.1.call-done = f32[256,32,128]{2,1,0:T(8,128)} async-done(((f32[8,32,128]{2,1,0:T(8,128)}), f32[256,32,128]{2,1,0:T(8,128)}) %all-gather.8.cloned.1.call-update) | async-done | bytes 4194320 | tf_op jit(solution)/shard_map/pivot_block/all_gather | solution.py:325
  120.1 0.0 all-gather.10.cloned.1.call-update
  120.2 0.0 all-gather.12.cloned.1.call-start
  120.2 4.8 %collective-permute-start.5 = (f32[128,384]{1,0:T(8,128)}, f32[128,384]{1,0:T(8,128)S(1)}, u32[]{:S(2)}, u32[]{:S(2)}) collective-permute-start(f32[128,384]{1,0:T(8,128)} %pad_maximum_fusion), channel_id=1, source_target_pairs={{0,0},{1,16},{2,32},{3,48},{4,64},{5,80},{6,96},{7,112},{8,8},{9,2... | collective-permute-start | bytes 589832 | tf_op jit(solution)/shard_map/panel/ppermute | solution.py:337
  125.0 18.6 %collective-permute-done.5 = f32[128,384]{1,0:T(8,128)S(1)} collective-permute-done((f32[128,384]{1,0:T(8,128)}, f32[128,384]{1,0:T(8,128)S(1)}, u32[]{:S(2)}, u32[]{:S(2)}) %collective-permute-start.5) | collective-permute-done | bytes 196640 | tf_op jit(solution)/shard_map/panel/ppermute | solution.py:337
  143.7 0.7 copy-done.7
  144.3 0.0 all-gather.12.cloned.1.call-update
  144.4 2.4 reshape_squeeze.7
  146.7 6.1 %fusion = f32[1024,2,128]{2,1,0:T(2,128)S(1)} fusion(pred[]{:T(512)S(6)} %eq.77, f32[1024,2,2,128]{3,2,1,0:T(2,128)} %reshape_squeeze.7), kind=kLoop, calls=%fused_computation.1 | loop fusion | flops 262144 | bytes 3145729 | tf_op jit(solution)/shard_map/siblings/jit(_where)/select_n | solution.py:342
  152.8 1.0 copy.18
  153.9 0.2 dynamic-slice_reduce_fusion.1
  154.1 0.1 reshape.118
  154.2 0.2 dynamic-slice_reduce_fusion
  154.4 0.1 copy.9
  154.5 0.1 reshape.116
  154.6 0.1 concatenate.6.meta_ref
  154.7 0.7 collective-permute-start.4
  155.4 2.2 copy-done.1
  157.6 101.5 %factor_pivots.1 = (f32[1024,1024]{1,0:T(8,128)S(1)}, f32[1024,1024]{1,0:T(8,128)S(1)}, f32[8,128,128]{2,1,0:T(8,128)S(1)}) custom-call(f32[4,8,8,32,128]{4,3,2,1,0:T(8,128)S(1)} %bitcast.57), custom_call_target="tpu_custom_call" | custom-call | flops 60000002048 | bytes 13631488 | tf_op jit(solution)/shard_map/factor/factor_pivots/pallas_call | solution.py:104
  259.1 2.0 copy-done.3
  261.1 2.1 copy-done.4
  263.2 0.8 copy-done.5
  264.0 0.0 collective-permute-done.4
  264.0 1.4 copy-done.2
  265.4 1.0 copy-done.6
  266.5 41.2 %solve_and_update.1 = f32[3,4,128,384]{3,2,1,0:T(8,128)} custom-call(s32[24]{0:T(128)S(1)} %concatenate.6.meta_ref, f32[3,4,128,384]{3,2,1,0:T(8,128)} %bitcast.63, f32[2,4,128,512]{3,2,1,0:T(8,128)S(1)} %bitcast.56, f32[2,4,128,256]{3,2,1,0:T(8,128)S(1)} %bitcast.58, f32[1024,384]{1,0:T(8,128)S(1)} %copy-done.2, f32[4,1024,384]{2,1,0:T(8,128)} %bitcast.65, ...), custom_call_target="tpu_custom_call" | custom-call | flops 24999999488 | bytes 31457280 | tf_op jit(solution)/shard_map/finish/solve_and_update/pallas_call | solution.py:226
  (19 shorter events, 0.1 us)
Async XLA Ops:
  6.5 3.7 %copy-start.8 = (s32[2,64]{1,0:T(2,128)S(1)}, s32[2,64]{1,0:T(2,128)}, u32[]{:S(2)}) copy-start(s32[2,64]{1,0:T(2,128)} %param.5) | copy-start | bytes 1540
  6.5 113.6 %all-gather.8.cloned.1.call-start = ((), (), s32[]{:S(2)}) async-start(), calls=%async_computation | async-start | bytes 4325376 | tf_op jit(solution)/shard_map/pivot_block/all_gather | solution.py:325
  6.5 137.8 %copy-start = (f32[1,1024,512]{2,1,0:T(8,128)S(1)}, f32[1,1024,512]{2,1,0:T(8,128)}, u32[]{:S(2)}) copy-start(f32[1,1024,512]{2,1,0:T(8,128)} %param.4) | copy-start | bytes 6291460
  8.1 10.2 %collective-permute-start = (f32[128,2,128]{2,0,1:T(8,128)S(1)}, f32[128,2,128]{2,0,1:T(8,128)S(1)}, u32[]{:S(2)}, u32[]{:S(2)}) collective-permute-start(f32[128,2,128]{2,0,1:T(8,128)S(1)} %get-tuple-element.23), channel_id=1, source_target_pairs={{0,128},{128,0},{1,129},{129,1},{2,130},{130,2},{3,131},{131,3},{4... | collective-permute-start | bytes 393224 | tf_op jit(solution)/shard_map/pivot_rows/ppermute | solution.py:299
  19.3 8.6 %collective-permute-start.1 = (f32[32,128]{1,0:T(8,128)S(1)}, f32[32,128]{1,0:T(8,128)S(1)}, u32[]{:S(2)}, u32[]{:S(2)}) collective-permute-start(f32[32,128]{1,0:T(8,128)S(1)} %get-tuple-element.28), channel_id=1, source_target_pairs={{0,136},{1,137},{2,138},{3,139},{4,140},{5,141},{6,142},{7,143},{1... | collective-permute-start | bytes 49160 | tf_op jit(solution)/shard_map/pivot_block/ppermute | solution.py:322
  25.2 2.7 collective-permute-start.2
  26.5 2.7 collective-permute-start.3
  59.5 204.6 %all-gather.10.cloned.1.call-start = ((), (), s32[]{:S(2)}) async-start(), calls=%async_computation.1 | async-start | bytes 1769472 | tf_op jit(solution)/shard_map/panel/all_gather | solution.py:330
  120.2 143.8 %all-gather.12.cloned.1.call-start = ((), (), s32[]{:S(2)}) async-start(), calls=%async_computation.2 | async-start | bytes 6488064 | tf_op jit(solution)/shard_map/panel/all_gather | solution.py:338
  120.2 23.4 %collective-permute-start.5 = (f32[128,384]{1,0:T(8,128)}, f32[128,384]{1,0:T(8,128)S(1)}, u32[]{:S(2)}, u32[]{:S(2)}) collective-permute-start(f32[128,384]{1,0:T(8,128)} %pad_maximum_fusion), channel_id=1, source_target_pairs={{0,0},{1,16},{2,32},{3,48},{4,64},{5,80},{6,96},{7,112},{8,8},{9,2... | collective-permute-start | bytes 589832 | tf_op jit(solution)/shard_map/panel/ppermute | solution.py:337
  143.7 0.7 copy-start.7
  154.7 109.3 %collective-permute-start.4 = (f32[1024,256]{1,0:T(8,128)}, f32[1024,256]{1,0:T(8,128)S(1)}, u32[]{:S(2)}, u32[]{:S(2)}) collective-permute-start(f32[1024,256]{1,0:T(8,128)} %bitcast.60), channel_id=1, source_target_pairs={{0,128},{128,0},{1,129},{129,1},{2,130},{130,2},{3,131},{131,3},{4... | collective-permute-start | bytes 3145736 | tf_op jit(solution)/shard_map/siblings/ppermute | solution.py:344
  155.4 2.2 copy-start.1
  259.1 2.1 copy-start.3
  261.1 2.1 copy-start.4
  263.2 0.8 copy-start.5
  264.0 1.4 copy-start.2
  265.4 1.0 copy-start.6
Sparse Core Ops, SparseCore 0:
  59.6 60.5 all-gather.7
  121.9 42.1 all-gather.9
  166.0 65.2 all-gather.11

commit v2 on v1

v2 whole, which is shorter than its diff:
```python
import jax
import jax.numpy as jnp
from jax import lax
from jax.experimental import pallas as pl
from jax.experimental.pallas import tpu as pltpu
from jax.sharding import PartitionSpec as P

TILE = 128
PIVOT_TILES = 8
NPIV = TILE * PIVOT_TILES
STRIP = 64
GROUP = 8
PARTS = 2
FACTOR_FLOPS = 50 * 10**9
EXACT = lax.Precision.HIGHEST


def exact_dot(a, b, contract=((1,), (0,))):
    return lax.dot_general(
        a, b, (contract, ((), ())), precision=EXACT, preferred_element_type=jnp.float32
    )


def split(x):
    parts = []
    for _ in range(PARTS):
        part = x.astype(jnp.bfloat16)
        x = x - part.astype(jnp.float32)
        parts.append(part)
    return parts


def parts_dot(a, b, contract):
    total = None
    for order in reversed(range(len(a))):
        for i in range(order + 1):
            term = lax.dot_general(
                a[i], b[order - i], (contract, ((), ())), preferred_element_type=jnp.float32
            )
            total = term if total is None else total + term
    return total


def factor_tile(block):
    row = lax.broadcasted_iota(jnp.int32, (TILE, TILE), 0)
    lane = lax.broadcasted_iota(jnp.int32, (TILE, TILE), 1)
    remaining = jnp.concatenate([block, (row == lane).astype(jnp.float32)], axis=1)
    strip_row = lax.broadcasted_iota(jnp.int32, (STRIP, TILE), 0)

    def twice(x):
        return jnp.concatenate([x, x], axis=1)

    def tall(x):
        return jnp.concatenate([x] * (STRIP // 8), axis=0)

    done = []
    for first in range(0, TILE, STRIP):
        strip = remaining[:STRIP]
        for k in range(0, STRIP, GROUP):
            at = first + k
            columns, rows, corner, inverse = [], [], {}, []
            for t in range(GROUP):
                columns.append(jnp.broadcast_to(strip[:, at + t : at + t + 1], (STRIP, TILE)))
                rows.append(jnp.broadcast_to(strip[k + t : k + t + 1], (8, 2 * TILE)))
                for r in range(t + 1):
                    corner[r, t] = jnp.broadcast_to(
                        strip[k + r : k + r + 1, at + t : at + t + 1], (8, TILE)
                    )
            for r in range(GROUP):
                inverse.append(1.0 / corner[r, r])
                for t in range(r + 1, GROUP):
                    scale = corner[r, t] * inverse[r]
                    for u in range(t, GROUP):
                        corner[t, u] = corner[t, u] - scale * corner[r, u]
                    columns[t] = columns[t] - tall(scale) * columns[r]
                    rows[t] = rows[t] - twice(scale) * rows[r]
            beneath = strip
            if k + GROUP < STRIP:
                for t in range(GROUP):
                    share = jnp.where(strip_row >= k + GROUP, columns[t] * tall(inverse[t]), 0.0)
                    beneath = beneath - twice(share) * tall(rows[t])
            for t in range(GROUP):
                root = lax.rsqrt(corner[t, t])
                root = root * (1.5 - 0.5 * corner[t, t] * root * root)
                beneath = jnp.where(
                    twice(strip_row) == k + t, tall(rows[t] * twice(root)), beneath
                )
            strip = beneath
        done.append(strip)
        if first + STRIP < TILE:
            change = exact_dot(strip[:, :TILE], strip, ((0,), (0,)))
            remaining = remaining[STRIP:] - change[first + STRIP :]
    whole = jnp.concatenate(done, axis=0)
    return jnp.where(lane >= row, whole[:, :TILE], 0.0), whole[:, TILE:]


def factor_kernel(row_ref, parts_ref, upper_ref, inverse_ref):
    for i in range(PIVOT_TILES):
        away = i ^ row_ref[0]
        place = (away & 1) * 4 + (away & 2) + (away >> 2)
        for c in range(i, PIVOT_TILES):
            for half in range(2):
                upper_ref[pl.ds(i * TILE + half * 64, 64), pl.ds(c * TILE, TILE)] = parts_ref[
                    half * 8 + c, place
                ]

    def step(j, carry):
        at = pl.ds(pl.multiple_of(j * TILE, TILE), TILE)
        upper, inverse = factor_tile(upper_ref[at, at])
        upper_ref[at, at] = upper
        inverse_ref[j] = inverse.T
        for now in range(PIVOT_TILES - 1):

            @pl.when(j == now)
            def _():
                here = slice(now * TILE, (now + 1) * TILE)
                after = slice((now + 1) * TILE, NPIV)
                solved = exact_dot(inverse, upper_ref[here, after])
                upper_ref[here, after] = solved
                for k in range(now + 1, PIVOT_TILES):
                    rows = slice(k * TILE, (k + 1) * TILE)
                    rest = slice(k * TILE, NPIV)
                    offset = (k - now - 1) * TILE
                    upper_ref[rows, rest] = upper_ref[rows, rest] - exact_dot(
                        solved[:, offset : offset + TILE], solved[:, offset:], ((0,), (0,))
                    )

        return carry

    lax.fori_loop(0, PIVOT_TILES, step, 0)


def factor(row_index, parts):
    return pl.pallas_call(
        factor_kernel,
        out_shape=(
            jax.ShapeDtypeStruct((NPIV, NPIV), jnp.float32),
            jax.ShapeDtypeStruct((PIVOT_TILES, TILE, TILE), jnp.float32),
        ),
        in_specs=[
            pl.BlockSpec(memory_space=pltpu.SMEM),
            pl.BlockSpec(memory_space=pltpu.VMEM),
        ],
        out_specs=tuple(pl.BlockSpec(memory_space=pltpu.VMEM) for _ in range(2)),
        compiler_params=pltpu.CompilerParams(vmem_limit_bytes=24 * 2**20),
        cost_estimate=pl.CostEstimate(
            flops=FACTOR_FLOPS, bytes_accessed=9 * 2**20, transcendentals=0
        ),
        name="factor_pivots",
    )(row_index.astype(jnp.int32).reshape(1), parts)


def finish_kernel(
    meta_ref,
    front_ref,
    child_ref,
    received_ref,
    across_refs,
    beneath_ref,
    upper_ref,
    inverse_ref,
    out_ref,
    upper_parts_ref,
    wide_parts_ref,
    across_ref,
    solved_ref,
    solved_parts_ref,
):
    half_step = pl.program_id(0)
    sibling = meta_ref[0]
    row_index = meta_ref[1]
    column_index = meta_ref[2]
    width = across_ref.shape[1]
    column_rows = slice(2 * width, 3 * width)

    def solve(count, source):
        for j in range(PIVOT_TILES // 2):
            columns = slice(2 * j * TILE, 2 * (j + 1) * TILE)
            rest = jnp.concatenate([source(2 * j), source(2 * j + 1)], axis=1)
            if j:
                before = slice(0, 2 * j * TILE)
                rest = rest - parts_dot(
                    [ref[:count, before] for ref in solved_parts_ref],
                    [ref[before, columns] for ref in upper_parts_ref],
                    ((1,), (0,)),
                )
            result = parts_dot(split(rest), [ref[j] for ref in wide_parts_ref], ((1,), (0,)))
            solved_ref[:count, columns] = result
            for ref, part in zip(solved_parts_ref, split(result)):
                ref[:count, columns] = part

    def panel(i):
        return [beneath_ref[i, 0], beneath_ref[8 + i, 0]]

    @pl.when(half_step == 0)
    def _():
        for j in range(PIVOT_TILES // 2):
            rows = slice(2 * j * TILE, 2 * (j + 1) * TILE)
            after = slice(2 * (j + 1) * TILE, NPIV)
            if j < PIVOT_TILES // 2 - 1:
                for ref, part in zip(upper_parts_ref, split(upper_ref[rows, after])):
                    ref[rows, after] = part
            low, high = inverse_ref[2 * j], inverse_ref[2 * j + 1]
            between = upper_ref[
                2 * j * TILE : (2 * j + 1) * TILE, (2 * j + 1) * TILE : 2 * (j + 1) * TILE
            ]
            corner = -exact_dot(low, exact_dot(between, high))
            for ref, l, h, c in zip(wide_parts_ref, split(low), split(high), split(corner)):
                ref[j, :TILE, :TILE] = l
                ref[j, TILE:, TILE:] = h
                ref[j, :TILE, TILE:] = c
                ref[j, TILE:, :TILE] = jnp.zeros((TILE, TILE), jnp.bfloat16)

        for behind, ref in zip(RING, across_refs):
            across_ref[lax.rem(row_index - behind + 8, 8)] = ref[...]
        solve(3 * width, lambda i: jnp.concatenate(panel(i) + [across_ref[i]]))

    @pl.when(half_step > 0)
    def _():
        solve(2 * width, lambda i: jnp.concatenate(panel(i)))

    update = parts_dot(
        [ref[: 2 * width] for ref in solved_parts_ref],
        [ref[column_rows] for ref in solved_parts_ref],
        ((1,), (1,)),
    )

    for half in range(2):
        group = 2 * half_step + half

        def row_slot(s, u):
            return meta_ref[4 + s * 8 + group * 2 + u]

        def column_slot(s, u):
            return meta_ref[20 + s * 2 + u]

        for m in range(3):
            for n in range(3):
                lanes = slice(n * TILE, (n + 1) * TILE)
                total = front_ref[m, half, :, lanes]
                for u in range(2):
                    for v in range(2):
                        if m - u in (0, 1) and n - v in (0, 1):
                            own = (row_slot(sibling, u) == m) & (column_slot(sibling, v) == n)
                            other = (row_slot(1 - sibling, u) == m) & (
                                column_slot(1 - sibling, v) == n
                            )
                            own_lanes = pl.ds(
                                pl.multiple_of((2 * v + sibling) * TILE, TILE), TILE
                            )
                            mine = child_ref[u, half, :, own_lanes]
                            theirs = received_ref[v, u, half]
                            total = total + jnp.where(own, mine, 0.0)
                            total = total + jnp.where(other, theirs, 0.0)
                top = half * width + m * TILE
                out_ref[m, half, :, lanes] = (
                    total - update[top : top + TILE, n * TILE : (n + 1) * TILE]
                )

    pivot_column = column_index < PIVOT_TILES
    own_column = pl.ds(pl.multiple_of(lax.rem(column_index, 8) * TILE, TILE), TILE)

    @pl.when(pivot_column)
    def _():
        for half in range(2):
            for m in range(3):
                top = half * width + m * TILE
                out_ref[m, half, :, :TILE] = solved_ref[top : top + TILE, own_column]

    @pl.when(half_step == 0)
    def _():
        own_row = pl.ds(pl.multiple_of(row_index * TILE, TILE), TILE)
        for n in range(3):
            lanes = slice(n * TILE, (n + 1) * TILE)
            top = 2 * width + n * TILE
            out_ref[0, 0, :, lanes] = solved_ref[top : top + TILE, own_row].T

        @pl.when(pivot_column)
        def _():
            @pl.when(row_index < column_index)
            def _():
                out_ref[0, 0, :, :TILE] = upper_ref[own_row, own_column]

            @pl.when(row_index > column_index)
            def _():
                out_ref[0, 0, :, :TILE] = upper_ref[own_column, own_row].T

            @pl.when(row_index == column_index)
            def _():
                row = lax.broadcasted_iota(jnp.int32, (TILE, TILE), 0)
                lane = lax.broadcasted_iota(jnp.int32, (TILE, TILE), 1)
                tile = upper_ref[own_row, own_column]
                out_ref[0, 0, :, :TILE] = jnp.where(row > lane, tile.T, tile)


def finish(meta, front, child, received, across, beneath, upper, inverse):
    width = front.shape[1]
    whole = pl.BlockSpec(memory_space=pltpu.VMEM)
    held = lambda *shape: [pltpu.VMEM(shape, jnp.bfloat16) for _ in range(PARTS)]
    out = pl.pallas_call(
        finish_kernel,
        grid=(2,),
        out_shape=jax.ShapeDtypeStruct((3, 4, TILE, width), jnp.float32),
        in_specs=[
            pl.BlockSpec(memory_space=pltpu.SMEM),
            pl.BlockSpec((3, 2, TILE, width), lambda g: (0, g, 0, 0)),
            pl.BlockSpec((2, 2, TILE, 4 * TILE), lambda g: (0, g, 0, 0)),
            pl.BlockSpec((2, 2, 2, TILE, TILE), lambda g: (0, 0, g, 0, 0)),
            [whole] * 8,
            pl.BlockSpec((16, 1, width, TILE), lambda g: (0, g, 0, 0)),
            whole,
            whole,
        ],
        out_specs=pl.BlockSpec((3, 2, TILE, width), lambda g: (0, g, 0, 0)),
        scratch_shapes=[
            held(NPIV, NPIV),
            held(PIVOT_TILES // 2, 2 * TILE, 2 * TILE),
            pltpu.VMEM((8, width, TILE), jnp.float32),
            pltpu.VMEM((3 * width, NPIV), jnp.float32),
            held(3 * width, NPIV),
        ],
        compiler_params=pltpu.CompilerParams(vmem_limit_bytes=50 * 2**20),
        cost_estimate=pl.CostEstimate(
            flops=15 * 10**9, bytes_accessed=24 * 2**20, transcendentals=0
        ),
        name="solve_and_update",
    )(
        meta,
        front.reshape(3, 4, TILE, width),
        child.reshape(2, 4, TILE, 4 * TILE),
        received.reshape(2, 2, 4, TILE, TILE),
        across,
        beneath,
        upper,
        inverse,
    )
    return out.reshape(front.shape)


ALL = ("pair", "row", "col")
SWAP = [(0, 1), (1, 0)]
RING = (0, 1, 7, 2, 6, 3, 5, 4)


def at(pair, row, col):
    return (pair * 8 + row) * 16 + col


def ring_gather(block):
    up = [(i, (i + 1) % 8) for i in range(8)]
    down = [(i, (i - 1) % 8) for i in range(8)]
    half = block.shape[0] // 2
    behind = ahead = block
    blocks = [block]
    for _ in range(3):
        behind = lax.ppermute(behind, "row", up)
        ahead = lax.ppermute(ahead, "row", down)
        blocks += [behind, ahead]
    last = [lax.ppermute(behind[:half], "row", up), lax.ppermute(ahead[half:], "row", down)]
    return blocks + [jnp.concatenate(last)]


def assemble_kernel(meta_ref, front_ref, child_ref, came_ref, out_ref):
    sibling = meta_ref[0]
    own_row = meta_ref[4 + sibling * 8] == 0
    other_row = meta_ref[4 + (1 - sibling) * 8] == 0
    for n in range(3):
        total = front_ref[:, n * TILE : (n + 1) * TILE]
        for v in range(2):
            if n - v in (0, 1):
                own = own_row & (meta_ref[20 + sibling * 2 + v] == n)
                other = other_row & (meta_ref[20 + (1 - sibling) * 2 + v] == n)
                lanes = pl.ds(pl.multiple_of((2 * v + sibling) * TILE, TILE), TILE)
                total = total + jnp.where(own, child_ref[:, lanes], 0.0)
                total = total + jnp.where(other, came_ref[v], 0.0)
        out_ref[n * TILE : (n + 1) * TILE, :] = total.T


def assemble(meta, front, child, came):
    width = front.shape[1]
    return pl.pallas_call(
        assemble_kernel,
        grid=(1,),
        out_shape=jax.ShapeDtypeStruct((width, TILE), jnp.float32),
        in_specs=[
            pl.BlockSpec(memory_space=pltpu.SMEM),
            pl.BlockSpec((TILE, width), lambda g: (0, 0)),
            pl.BlockSpec((TILE, 4 * TILE), lambda g: (0, 0)),
            pl.BlockSpec((2, TILE, TILE), lambda g: (0, 0, 0)),
        ],
        out_specs=pl.BlockSpec((width, TILE), lambda g: (0, 0)),
        compiler_params=pltpu.CompilerParams(vmem_limit_bytes=8 * 2**20),
        name="assemble_pivot_rows",
    )(meta, front, child, came)


def body(front_init, child_blocks, tile_map):
    sibling = lax.axis_index("pair")
    row_index = lax.axis_index("row")
    col_index = lax.axis_index("col")
    half_index = col_index // 8
    column_index = sibling * 16 + col_index
    own = child_blocks[0]
    positions = tile_map.astype(jnp.int32).reshape(2, 2, 32) // 32

    with jax.named_scope("pivot_block"):
        own_positions = positions[sibling, 0]
        hit = (own_positions[row_index] == 0) & (own_positions[col_index] == 0)
        tile = jnp.where(sibling == 0, front_init[:TILE, :TILE], 0.0)
        tile = tile + jnp.where(hit, own[:TILE, :TILE], 0.0)
        upper_half, lower_half = tile[: TILE // 2], tile[TILE // 2 :]
        mine = jnp.where(half_index == 0, upper_half, 0.0)
        places = [(p, i, c) for p in range(2) for i in range(8) for c in range(8)]
        mine = (
            mine
            + lax.ppermute(upper_half, ALL, [(at(p, i, c), at(1 - p, i, c)) for p, i, c in places])
            + lax.ppermute(lower_half, ALL, [(at(p, i, c), at(p, i, c + 8)) for p, i, c in places])
            + lax.ppermute(
                lower_half, ALL, [(at(p, i, c), at(1 - p, i, c + 8)) for p, i, c in places]
            )
        )
        mine = mine[None]
        for bit in (4, 2, 1):
            came = lax.ppermute(mine, "row", [(i, i ^ bit) for i in range(8)])
            mine = jnp.concatenate([mine, came])
        mine = lax.optimization_barrier(mine)
        parts = lax.all_gather(mine, "col")

    row_positions = jnp.swapaxes(
        lax.dynamic_index_in_dim(positions.reshape(2, 2, 4, 8), row_index, 3, keepdims=False), 1, 2
    )
    column_positions = lax.dynamic_index_in_dim(positions, column_index, 2, keepdims=False)
    meta = jnp.concatenate(
        [
            jnp.stack([sibling, row_index, column_index, column_index]),
            row_positions.reshape(16),
            column_positions.reshape(4),
        ]
    ).astype(jnp.int32)

    def pick(count, v, even):
        low = own[:count, 2 * v * TILE : (2 * v + 1) * TILE]
        high = own[:count, (2 * v + 1) * TILE : 2 * (v + 1) * TILE]
        return jnp.where(even, low, high)

    with jax.named_scope("pivot_rows"):
        handed = jnp.stack([pick(TILE, v, sibling != 0) for v in range(2)])
        came = lax.ppermute(handed, "pair", SWAP)
        pivot_columns = assemble(meta, front_init, own, came)

    with jax.named_scope("panel"):
        pivot_columns, mine = lax.optimization_barrier((pivot_columns, mine))
        routes = [[], []]
        for p in range(2):
            for i in range(8):
                for c in range(16):
                    half, other = divmod(c, 8)
                    for away in range(2):
                        target = at(p ^ away, other, 8 * half + i)
                        routes[away].append((at(p, i, c), target))
        same = lax.ppermute(pivot_columns, ALL, routes[0])
        crossed = lax.ppermute(pivot_columns, ALL, routes[1])
        turned = jnp.where(
            sibling == 0, jnp.stack([same, crossed]), jnp.stack([crossed, same])
        )
        beneath = lax.all_gather(turned, "col")
        pivot_columns, turned = lax.optimization_barrier((pivot_columns, turned))
        across = ring_gather(pivot_columns)
        across, parts = lax.optimization_barrier((across, parts))

    with jax.named_scope("siblings"):
        handed = jnp.stack([pick(NPIV, v, sibling != 0) for v in range(2)])
        handed, parts = lax.optimization_barrier((handed, parts))
        received = lax.ppermute(handed, "pair", SWAP)

    with jax.named_scope("factor"):
        upper, inverse = factor(row_index, parts)
    with jax.named_scope("finish"):
        return finish(meta, front_init, own, received, across, beneath, upper, inverse)


def solution(mesh):
    return jax.shard_map(
        body,
        mesh=mesh,
        in_specs=(P("row", ("pair", "col")), P("pair", "row", "col"), P()),
        out_specs=P("row", ("pair", "col")),
        check_vma=False,
    )
```

time: 317 us -> 202 us (0.64)
  Pallas kernels: 143 us -> 68.7 us
  starting transfers between devices: 16.4 us -> 47 us
  blocking collectives: 30.2 us -> 0 us
  waiting for transfers between devices: 80 us -> 54.8 us
  local copies, waits for them, and re-layouts: 17.4 us -> 10.4 us
  between operations: 19.7 us -> 14.9 us
  other arithmetic: 7.84 us -> 3.95 us
    pallas_call x1, Pallas kernels: 101 us -> 42.7 us  [factor(): pl.pallas_call(factor_kernel, out_shape=(jax.ShapeDtypeStruct((NPIV, NPIV...]
    all_gather x3 -> x2, waiting for transfers between devices: 59.9 us -> 1.98 us  [the longest x1 1.96 us: body(): beneath = lax.all_gather(turned, 'col')]
    ppermute x6 -> x18, waiting for transfers between devices: 20 us -> 52.8 us  [the longest x1 18.1 us: body(): same = lax.ppermute(pivot_columns, ALL, routes[0])]
    ppermute x6 -> x18, starting transfers between devices: 16.3 us -> 46.9 us  [the longest x3 9.82 us: body(): came = lax.ppermute(mine, 'row', [(i, i ^ bit) for i in range(8)])]
    all_gather x1 -> x0, blocking collectives: 30.2 us -> none  [body(): stacked = lax.all_gather(mine, 'row')]
    pallas_call x1 -> x2, Pallas kernels: 41.2 us -> 26 us  [the longest x1 25.3 us: finish(): pl.pallas_call(finish_kernel, grid=(2,), out_shape=jax.ShapeDtypeStruct((...]
    select_n x5 -> x2, other arithmetic: 6.17 us -> 0.8 us  [the longest x1 0.79 us: body(): jnp.where(sibling == 0, jnp.stack([same, crossed]), jnp.stack([crossed, s...]
    unnamed x22 -> x14, local copies, waits for them, and re-layouts: 11.6 us -> 8.18 us
  transfers between devices with their start and end apart: 9 -> 20, of which waited for: 4 -> 14; matrix products, arithmetic and copies ran while one was open for 4% -> 1% of each run, Pallas kernels for 32% -> 22%
where the time goes in v2:
time: 202 us; the launch traced here: 200 us
  Pallas kernels  68.7 us (34%)
  waiting for transfers between devices  54.8 us (27%)
  starting transfers between devices  47 us (23%)
  between operations  14.9 us (7%)
  local copies, waits for them, and re-layouts  10.4 us (5%)
  other arithmetic  3.95 us (2%)
    pallas_call x1, Pallas kernels, factor(): pl.pallas_call(factor_kernel, out_shape=(jax.ShapeDtypeStruct((NPIV, NPIV...  42.7 us
    pallas_call x1, Pallas kernels, finish(): pl.pallas_call(finish_kernel, grid=(2,), out_shape=jax.ShapeDtypeStruct((...  25.3 us
    ppermute x1, waiting for transfers between devices, body(): same = lax.ppermute(pivot_columns, ALL, routes[0])  18.1 us
    ppermute x3, waiting for transfers between devices, ring_gather(): behind = lax.ppermute(behind, 'row', up)  10.8 us
    ppermute x3, waiting for transfers between devices, body(): came = lax.ppermute(mine, 'row', [(i, i ^ bit) for i in range(8)])  10.4 us
    ppermute x3, starting transfers between devices, body(): came = lax.ppermute(mine, 'row', [(i, i ^ bit) for i in range(8)])  9.82 us
    unnamed x14, local copies, waits for them, and re-layouts  8.18 us
    ppermute x3, starting transfers between devices, ring_gather(): behind = lax.ppermute(behind, 'row', up)  5.77 us
  transfers between devices with their start and end apart: 20, of which 14 were waited for; matrix products, arithmetic and copies ran while one was open for 1% of the time, Pallas kernels for 22%

profile of v2, /device:TPU:2, one launch (start us, length us, event | category | flops | bytes accessed | tf_op | source)
XLA Modules:
  0.0 199.8 jit_solution(2504325589344575696)
XLA Ops:
  6.5 0.9 reshape.94
  7.5 0.7 constant_dynamic-slice_fusion
  9.4 1.0 select_add_fusion
  10.5 5.1 %collective-permute-start.2 = (f32[64,128]{1,0:T(8,128)S(1)}, f32[64,128]{1,0:T(8,128)S(1)}, u32[]{:S(2)}, u32[]{:S(2)}) collective-permute-start(f32[64,128]{1,0:T(8,128)S(1)} %get-tuple-element.39), channel_id=1, source_target_pairs={{0,8},{1,9},{2,10},{3,11},{4,12},{5,13},{6,14},{7,15},{16,24},{17,... | collective-permute-start | bytes 98312 | tf_op jit(solution)/shard_map/pivot_block/ppermute | solution.py:417
  15.6 2.9 %collective-permute-start.3 = (f32[64,128]{1,0:T(8,128)S(1)}, f32[64,128]{1,0:T(8,128)S(1)}, u32[]{:S(2)}, u32[]{:S(2)}) collective-permute-start(f32[64,128]{1,0:T(8,128)S(1)} %get-tuple-element.39), channel_id=1, source_target_pairs={{0,136},{1,137},{2,138},{3,139},{4,140},{5,141},{6,142},{7,143},{1... | collective-permute-start | bytes 98312 | tf_op jit(solution)/shard_map/pivot_block/ppermute | solution.py:418
  18.4 3.3 %collective-permute-start.1 = (f32[64,128]{1,0:T(8,128)S(1)}, f32[64,128]{1,0:T(8,128)S(1)}, u32[]{:S(2)}, u32[]{:S(2)}) collective-permute-start(f32[64,128]{1,0:T(8,128)S(1)} %get-tuple-element.38), channel_id=1, source_target_pairs={{0,128},{1,129},{2,130},{3,131},{4,132},{5,133},{6,134},{7,135},{1... | collective-permute-start | bytes 98312 | tf_op jit(solution)/shard_map/pivot_block/ppermute | solution.py:416
  21.8 4.0 %collective-permute-done.1 = f32[64,128]{1,0:T(8,128)S(1)} collective-permute-done((f32[64,128]{1,0:T(8,128)S(1)}, f32[64,128]{1,0:T(8,128)S(1)}, u32[]{:S(2)}, u32[]{:S(2)}) %collective-permute-start.1) | collective-permute-done | bytes 32800 | tf_op jit(solution)/shard_map/pivot_block/ppermute | solution.py:416
  25.8 7.3 %collective-permute-start.4 = (f32[1,64,128]{2,1,0:T(8,128)S(1)}, f32[1,64,128]{2,1,0:T(8,128)S(1)}, u32[]{:S(2)}, u32[]{:S(2)}) collective-permute-start(f32[1,64,128]{2,1,0:T(8,128)S(1)} %add_bitcast_fusion), channel_id=1, source_target_pairs={{0,64},{16,80},{32,96},{48,112},{64,0},{80,16},{96,32},{112,48},{1... | collective-permute-start | bytes 98312 | tf_op jit(solution)/shard_map/pivot_block/ppermute | solution.py:424
  33.0 1.9 collective-permute-done.4
  34.9 2.0 %collective-permute-start.5 = (f32[2,64,128]{2,1,0:T(8,128)S(1)}, f32[2,64,128]{2,1,0:T(8,128)S(1)}, u32[]{:S(2)}, u32[]{:S(2)}) collective-permute-start(f32[2,64,128]{2,1,0:T(8,128)S(1)} %pad_maximum_fusion.5), channel_id=1, source_target_pairs={{0,32},{16,48},{32,0},{48,16},{64,96},{80,112},{96,64},{112,80},{1... | collective-permute-start | bytes 196616 | tf_op jit(solution)/shard_map/pivot_block/ppermute | solution.py:424
  36.9 4.0 %collective-permute-done.5 = f32[2,64,128]{2,1,0:T(8,128)S(1)} collective-permute-done((f32[2,64,128]{2,1,0:T(8,128)S(1)}, f32[2,64,128]{2,1,0:T(8,128)S(1)}, u32[]{:S(2)}, u32[]{:S(2)}) %collective-permute-start.5) | collective-permute-done | bytes 65568 | tf_op jit(solution)/shard_map/pivot_block/ppermute | solution.py:424
  40.9 0.5 collective-permute-start.6
  41.5 4.5 %collective-permute-done.6 = f32[4,64,128]{2,1,0:T(8,128)S(1)} collective-permute-done((f32[4,64,128]{2,1,0:T(8,128)S(1)}, f32[4,64,128]{2,1,0:T(8,128)S(1)}, u32[]{:S(2)}, u32[]{:S(2)}) %collective-permute-start.6) | collective-permute-done | bytes 131104 | tf_op jit(solution)/shard_map/pivot_block/ppermute | solution.py:424
  46.0 0.7 pad_maximum_fusion.1
  46.8 1.5 collective-permute-start
  48.4 0.2 dynamic-slice_reduce_fusion
  48.7 0.2 fusion.5
  49.2 4.1 %collective-permute-done.came_ref = f32[2,128,128]{2,1,0:T(8,128)S(1)} collective-permute-done((f32[2,128,128]{2,1,0:T(8,128)S(1)}, f32[2,128,128]{2,1,0:T(8,128)S(1)}, u32[]{:S(2)}, u32[]{:S(2)}) %collective-permute-start) | collective-permute-done | bytes 131104 | tf_op jit(solution)/shard_map/pivot_rows/ppermute | solution.py:448
  53.3 1.7 copy-done.1
  55.0 0.7 assemble_pivot_rows.1.across_refs_0_
  55.7 4.5 %collective-permute-start.16 = (f32[384,128]{1,0:T(8,128)S(1)}, f32[384,128]{1,0:T(8,128)S(1)}, u32[]{:S(2)}, u32[]{:S(2)}) collective-permute-start(f32[384,128]{1,0:T(8,128)S(1)} %assemble_pivot_rows.1.across_refs_0_), channel_id=1, source_target_pairs={{0,0},{1,16},{2,32},{3,48},{4,64},{5,80},{6,96},{7,112},{8,8},{9,2... | collective-permute-start | bytes 589832 | tf_op jit(solution)/shard_map/panel/ppermute | solution.py:461
  60.3 1.2 collective-permute-start.17
  61.5 18.1 %collective-permute-done.16 = f32[384,128]{1,0:T(8,128)S(1)} collective-permute-done((f32[384,128]{1,0:T(8,128)S(1)}, f32[384,128]{1,0:T(8,128)S(1)}, u32[]{:S(2)}, u32[]{:S(2)}) %collective-permute-start.16) | collective-permute-done | bytes 196640 | tf_op jit(solution)/shard_map/panel/ppermute | solution.py:461
  79.5 2.7 %collective-permute-done.17 = f32[384,128]{1,0:T(8,128)S(1)} collective-permute-done((f32[384,128]{1,0:T(8,128)S(1)}, f32[384,128]{1,0:T(8,128)S(1)}, u32[]{:S(2)}, u32[]{:S(2)}) %collective-permute-start.17) | collective-permute-done | bytes 196640 | tf_op jit(solution)/shard_map/panel/ppermute | solution.py:462
  82.2 0.8 maximum_select_fusion
  83.0 1.8 collective-permute-start.7
  84.9 1.5 collective-permute-start.8
  86.3 3.6 %collective-permute-done.7.across_refs_1_ = f32[384,128]{1,0:T(8,128)S(1)} collective-permute-done((f32[384,128]{1,0:T(8,128)S(1)}, f32[384,128]{1,0:T(8,128)S(1)}, u32[]{:S(2)}, u32[]{:S(2)}) %collective-permute-start.7) | collective-permute-done | bytes 196640 | tf_op jit(solution)/shard_map/panel/ppermute | solution.py:356
  90.0 1.6 collective-permute-start.9
  91.6 0.3 collective-permute-done.8.across_refs_2_
  92.0 1.3 collective-permute-start.10
  93.2 3.6 %collective-permute-done.9.across_refs_3_ = f32[384,128]{1,0:T(8,128)S(1)} collective-permute-done((f32[384,128]{1,0:T(8,128)S(1)}, f32[384,128]{1,0:T(8,128)S(1)}, u32[]{:S(2)}, u32[]{:S(2)}) %collective-permute-start.9) | collective-permute-done | bytes 196640 | tf_op jit(solution)/shard_map/panel/ppermute | solution.py:356
  96.9 2.3 %collective-permute-start.11 = (f32[384,128]{1,0:T(8,128)S(1)}, f32[384,128]{1,0:T(8,128)S(1)}, u32[]{:S(2)}, u32[]{:S(2)}) collective-permute-start(f32[384,128]{1,0:T(8,128)S(1)} %collective-permute-done.9.across_refs_3_), channel_id=1, source_target_pairs={{0,16},{16,32},{32,48},{48,64},{64,80},{80,96},{96,112},{112,0},{1... | collective-permute-start | bytes 589832 | tf_op jit(solution)/shard_map/panel/ppermute | solution.py:356
  99.2 1.0 collective-permute-start.12
  100.2 3.5 %collective-permute-done.11.across_refs_5_ = f32[384,128]{1,0:T(8,128)S(1)} collective-permute-done((f32[384,128]{1,0:T(8,128)S(1)}, f32[384,128]{1,0:T(8,128)S(1)}, u32[]{:S(2)}, u32[]{:S(2)}) %collective-permute-start.11) | collective-permute-done | bytes 196640 | tf_op jit(solution)/shard_map/panel/ppermute | solution.py:356
  103.8 2.2 %collective-permute-start.13 = (f32[192,128]{1,0:T(8,128)S(1)}, f32[192,128]{1,0:T(8,128)S(1)}, u32[]{:S(2)}, u32[]{:S(2)}) collective-permute-start(f32[192,128]{1,0:T(8,128)S(1)} %slice.63), channel_id=1, source_target_pairs={{0,16},{16,32},{32,48},{48,64},{64,80},{80,96},{96,112},{112,0},{1... | collective-permute-start | bytes 294920 | tf_op jit(solution)/shard_map/panel/ppermute | solution.py:359
  106.0 1.2 collective-permute-start.14
  107.2 1.0 pad_maximum_fusion
  108.2 1.5 collective-permute-done.13
  109.7 1.0 collective-permute-done.14
  110.7 5.7 %collective-permute-start.15 = (f32[2,1024,128]{2,1,0:T(8,128)}, f32[2,1024,128]{2,1,0:T(8,128)S(1)}, u32[]{:S(2)}, u32[]{:S(2)}) collective-permute-start(f32[2,1024,128]{2,1,0:T(8,128)} %pad_maximum_fusion), channel_id=1, source_target_pairs={{0,128},{128,0},{1,129},{129,1},{2,130},{130,2},{3,131},{131,3},{4... | collective-permute-start | bytes 3145736 | tf_op jit(solution)/shard_map/siblings/ppermute | solution.py:474
  116.5 2.2 %copy-done.2 = f32[128,64,128]{2,1,0:T(8,128)S(1)} copy-done((f32[128,64,128]{2,1,0:T(8,128)S(1)}, f32[128,64,128]{2,1,0:T(8,128)}, u32[]{:S(2)}) %copy-start.2) | copy-done | bytes 4194328
  118.7 42.7 %factor_pivots.1 = (f32[1024,1024]{1,0:T(8,128)S(1)}, f32[8,128,128]{2,1,0:T(8,128)S(1)}) custom-call(s32[1]{0:T(128)} %bitcast.1.row_ref, f32[16,8,64,128]{3,2,1,0:T(8,128)S(1)} %bitcast.28), custom_call_target="tpu_custom_call" | custom-call | flops 49999998976 | bytes 9437184 | tf_op jit(solution)/shard_map/factor/factor_pivots/pallas_call | solution.py:134
  161.4 2.1 %copy-done.5 = f32[1024,1024]{1,0:T(8,128)} copy-done((f32[1024,1024]{1,0:T(8,128)}, f32[1024,1024]{1,0:T(8,128)S(1)}, u32[]{:S(2)}) %copy-start.5) | copy-done | bytes 4194328
  163.5 1.0 copy-done.3
  164.4 2.0 all-gather.4.cloned.1.call-done.beneath_ref
  166.4 1.2 copy-done.4
  167.6 25.3 %solve_and_update.1 = f32[3,4,128,384]{3,2,1,0:T(8,128)} custom-call(s32[24]{0:T(128)S(1)} %concatenate.31.meta_ref, f32[3,4,128,384]{3,2,1,0:T(8,128)} %bitcast.27, f32[2,4,128,512]{3,2,1,0:T(8,128)} %bitcast.24, f32[2,2,4,128,128]{4,3,2,1,0:T(8,128)S(1)} %bitcast.29, f32[384,128]{1,0:T(8,128)S(1)} %assemble_pivot_rows.1.across_refs_0_, ...), custom_call_target="tpu_custom_call" | custom-call | flops 15000000512 | bytes 25165824 | tf_op jit(solution)/shard_map/finish/solve_and_update/pallas_call | solution.py:300
  (36 shorter events, 0.8 us)
Async XLA Ops:
  6.5 41.7 %copy-start.6 = (s32[2,64]{1,0:T(2,128)S(1)}, s32[2,64]{1,0:T(2,128)}, u32[]{:S(2)}) copy-start(s32[2,64]{1,0:T(2,128)} %param.5) | copy-start | bytes 1540
  6.5 46.8 %copy-start = (f32[1,1024,512]{2,1,0:T(8,128)S(1)}, f32[1,1024,512]{2,1,0:T(8,128)}, u32[]{:S(2)}) copy-start(f32[1,1024,512]{2,1,0:T(8,128)} %param.4) | copy-start | bytes 6291460
  6.5 104.2 %all-gather.6.cloned.1.call-start = ((), (), s32[]{:S(2)}) async-start(), calls=%async_computation.1 | async-start | bytes 4456448 | tf_op jit(solution)/shard_map/pivot_block/all_gather | solution.py:427
  10.5 11.3 %collective-permute-start.2 = (f32[64,128]{1,0:T(8,128)S(1)}, f32[64,128]{1,0:T(8,128)S(1)}, u32[]{:S(2)}, u32[]{:S(2)}) collective-permute-start(f32[64,128]{1,0:T(8,128)S(1)} %get-tuple-element.39), channel_id=1, source_target_pairs={{0,8},{1,9},{2,10},{3,11},{4,12},{5,13},{6,14},{7,15},{16,24},{17,... | collective-permute-start | bytes 98312 | tf_op jit(solution)/shard_map/pivot_block/ppermute | solution.py:417
  15.6 6.2 %collective-permute-start.3 = (f32[64,128]{1,0:T(8,128)S(1)}, f32[64,128]{1,0:T(8,128)S(1)}, u32[]{:S(2)}, u32[]{:S(2)}) collective-permute-start(f32[64,128]{1,0:T(8,128)S(1)} %get-tuple-element.39), channel_id=1, source_target_pairs={{0,136},{1,137},{2,138},{3,139},{4,140},{5,141},{6,142},{7,143},{1... | collective-permute-start | bytes 98312 | tf_op jit(solution)/shard_map/pivot_block/ppermute | solution.py:418
  18.4 7.3 %collective-permute-start.1 = (f32[64,128]{1,0:T(8,128)S(1)}, f32[64,128]{1,0:T(8,128)S(1)}, u32[]{:S(2)}, u32[]{:S(2)}) collective-permute-start(f32[64,128]{1,0:T(8,128)S(1)} %get-tuple-element.38), channel_id=1, source_target_pairs={{0,128},{1,129},{2,130},{3,131},{4,132},{5,133},{6,134},{7,135},{1... | collective-permute-start | bytes 98312 | tf_op jit(solution)/shard_map/pivot_block/ppermute | solution.py:416
  25.8 9.2 %collective-permute-start.4 = (f32[1,64,128]{2,1,0:T(8,128)S(1)}, f32[1,64,128]{2,1,0:T(8,128)S(1)}, u32[]{:S(2)}, u32[]{:S(2)}) collective-permute-start(f32[1,64,128]{2,1,0:T(8,128)S(1)} %add_bitcast_fusion), channel_id=1, source_target_pairs={{0,64},{16,80},{32,96},{48,112},{64,0},{80,16},{96,32},{112,48},{1... | collective-permute-start | bytes 98312 | tf_op jit(solution)/shard_map/pivot_block/ppermute | solution.py:424
  34.9 6.0 %collective-permute-start.5 = (f32[2,64,128]{2,1,0:T(8,128)S(1)}, f32[2,64,128]{2,1,0:T(8,128)S(1)}, u32[]{:S(2)}, u32[]{:S(2)}) collective-permute-start(f32[2,64,128]{2,1,0:T(8,128)S(1)} %pad_maximum_fusion.5), channel_id=1, source_target_pairs={{0,32},{16,48},{32,0},{48,16},{64,96},{80,112},{96,64},{112,80},{1... | collective-permute-start | bytes 196616 | tf_op jit(solution)/shard_map/pivot_block/ppermute | solution.py:424
  40.9 5.1 %collective-permute-start.6 = (f32[4,64,128]{2,1,0:T(8,128)S(1)}, f32[4,64,128]{2,1,0:T(8,128)S(1)}, u32[]{:S(2)}, u32[]{:S(2)}) collective-permute-start(f32[4,64,128]{2,1,0:T(8,128)S(1)} %pad_maximum_fusion.4), channel_id=1, source_target_pairs={{0,16},{16,0},{32,48},{48,32},{64,80},{80,64},{96,112},{112,96},{1... | collective-permute-start | bytes 393224 | tf_op jit(solution)/shard_map/pivot_block/ppermute | solution.py:424
  46.7 119.7 %all-gather.4.cloned.1.call-start = ((), (), s32[]{:S(2)}) async-start(), calls=%async_computation | async-start | bytes 6684672 | tf_op jit(solution)/shard_map/panel/all_gather | solution.py:466
  46.8 6.6 %collective-permute-start = (f32[2,128,128]{2,1,0:T(8,128)S(1)}, f32[2,128,128]{2,1,0:T(8,128)S(1)}, u32[]{:S(2)}, u32[]{:S(2)}) collective-permute-start(f32[2,128,128]{2,1,0:T(8,128)S(1)} %pad_maximum_fusion.3), channel_id=1, source_target_pairs={{0,128},{128,0},{1,129},{129,1},{2,130},{130,2},{3,131},{131,3},{4... | collective-permute-start | bytes 393224 | tf_op jit(solution)/shard_map/pivot_rows/ppermute | solution.py:448
  53.3 1.7 copy-start.1
  55.7 23.8 %collective-permute-start.16 = (f32[384,128]{1,0:T(8,128)S(1)}, f32[384,128]{1,0:T(8,128)S(1)}, u32[]{:S(2)}, u32[]{:S(2)}) collective-permute-start(f32[384,128]{1,0:T(8,128)S(1)} %assemble_pivot_rows.1.across_refs_0_), channel_id=1, source_target_pairs={{0,0},{1,16},{2,32},{3,48},{4,64},{5,80},{6,96},{7,112},{8,8},{9,2... | collective-permute-start | bytes 589832 | tf_op jit(solution)/shard_map/panel/ppermute | solution.py:461
  60.3 22.0 %collective-permute-start.17 = (f32[384,128]{1,0:T(8,128)S(1)}, f32[384,128]{1,0:T(8,128)S(1)}, u32[]{:S(2)}, u32[]{:S(2)}) collective-permute-start(f32[384,128]{1,0:T(8,128)S(1)} %assemble_pivot_rows.1.across_refs_0_), channel_id=1, source_target_pairs={{0,128},{1,144},{2,160},{3,176},{4,192},{5,208},{6,224},{7,240},{8... | collective-permute-start | bytes 589832 | tf_op jit(solution)/shard_map/panel/ppermute | solution.py:462
  83.0 7.0 %collective-permute-start.7 = (f32[384,128]{1,0:T(8,128)S(1)}, f32[384,128]{1,0:T(8,128)S(1)}, u32[]{:S(2)}, u32[]{:S(2)}) collective-permute-start(f32[384,128]{1,0:T(8,128)S(1)} %assemble_pivot_rows.1.across_refs_0_), channel_id=1, source_target_pairs={{0,16},{16,32},{32,48},{48,64},{64,80},{80,96},{96,112},{112,0},{1... | collective-permute-start | bytes 589832 | tf_op jit(solution)/shard_map/panel/ppermute | solution.py:356
  84.9 7.1 %collective-permute-start.8 = (f32[384,128]{1,0:T(8,128)S(1)}, f32[384,128]{1,0:T(8,128)S(1)}, u32[]{:S(2)}, u32[]{:S(2)}) collective-permute-start(f32[384,128]{1,0:T(8,128)S(1)} %assemble_pivot_rows.1.across_refs_0_), channel_id=1, source_target_pairs={{0,112},{16,0},{32,16},{48,32},{64,48},{80,64},{96,80},{112,96},{1... | collective-permute-start | bytes 589832 | tf_op jit(solution)/shard_map/panel/ppermute | solution.py:357
  90.0 6.9 %collective-permute-start.9 = (f32[384,128]{1,0:T(8,128)S(1)}, f32[384,128]{1,0:T(8,128)S(1)}, u32[]{:S(2)}, u32[]{:S(2)}) collective-permute-start(f32[384,128]{1,0:T(8,128)S(1)} %collective-permute-done.7.across_refs_1_), channel_id=1, source_target_pairs={{0,16},{16,32},{32,48},{48,64},{64,80},{80,96},{96,112},{112,0},{1... | collective-permute-start | bytes 589832 | tf_op jit(solution)/shard_map/panel/ppermute | solution.py:356
  92.0 7.2 %collective-permute-start.10 = (f32[384,128]{1,0:T(8,128)S(1)}, f32[384,128]{1,0:T(8,128)S(1)}, u32[]{:S(2)}, u32[]{:S(2)}) collective-permute-start(f32[384,128]{1,0:T(8,128)S(1)} %collective-permute-done.8.across_refs_2_), channel_id=1, source_target_pairs={{0,112},{16,0},{32,16},{48,32},{64,48},{80,64},{96,80},{112,96},{1... | collective-permute-start | bytes 589832 | tf_op jit(solution)/shard_map/panel/ppermute | solution.py:357
  96.9 6.9 %collective-permute-start.11 = (f32[384,128]{1,0:T(8,128)S(1)}, f32[384,128]{1,0:T(8,128)S(1)}, u32[]{:S(2)}, u32[]{:S(2)}) collective-permute-start(f32[384,128]{1,0:T(8,128)S(1)} %collective-permute-done.9.across_refs_3_), channel_id=1, source_target_pairs={{0,16},{16,32},{32,48},{48,64},{64,80},{80,96},{96,112},{112,0},{1... | collective-permute-start | bytes 589832 | tf_op jit(solution)/shard_map/panel/ppermute | solution.py:356
  99.2 6.8 %collective-permute-start.12 = (f32[384,128]{1,0:T(8,128)S(1)}, f32[384,128]{1,0:T(8,128)S(1)}, u32[]{:S(2)}, u32[]{:S(2)}) collective-permute-start(f32[384,128]{1,0:T(8,128)S(1)} %collective-permute-done.10.across_refs_4_), channel_id=1, source_target_pairs={{0,112},{16,0},{32,16},{48,32},{64,48},{80,64},{96,80},{112,96},{1... | collective-permute-start | bytes 589832 | tf_op jit(solution)/shard_map/panel/ppermute | solution.py:357
  103.8 5.9 %collective-permute-start.13 = (f32[192,128]{1,0:T(8,128)S(1)}, f32[192,128]{1,0:T(8,128)S(1)}, u32[]{:S(2)}, u32[]{:S(2)}) collective-permute-start(f32[192,128]{1,0:T(8,128)S(1)} %slice.63), channel_id=1, source_target_pairs={{0,16},{16,32},{32,48},{48,64},{64,80},{80,96},{96,112},{112,0},{1... | collective-permute-start | bytes 294920 | tf_op jit(solution)/shard_map/panel/ppermute | solution.py:359
  106.0 4.7 %collective-permute-start.14 = (f32[192,128]{1,0:T(8,128)S(1)}, f32[192,128]{1,0:T(8,128)S(1)}, u32[]{:S(2)}, u32[]{:S(2)}) collective-permute-start(f32[192,128]{1,0:T(8,128)S(1)} %slice.64), channel_id=1, source_target_pairs={{0,112},{16,0},{32,16},{48,32},{64,48},{80,64},{96,80},{112,96},{1... | collective-permute-start | bytes 294920 | tf_op jit(solution)/shard_map/panel/ppermute | solution.py:359
  110.7 52.7 %collective-permute-start.15 = (f32[2,1024,128]{2,1,0:T(8,128)}, f32[2,1024,128]{2,1,0:T(8,128)S(1)}, u32[]{:S(2)}, u32[]{:S(2)}) collective-permute-start(f32[2,1024,128]{2,1,0:T(8,128)} %pad_maximum_fusion), channel_id=1, source_target_pairs={{0,128},{128,0},{1,129},{129,1},{2,130},{130,2},{3,131},{131,3},{4... | collective-permute-start | bytes 3145736 | tf_op jit(solution)/shard_map/siblings/ppermute | solution.py:474
  116.5 2.3 %copy-start.2 = (f32[128,64,128]{2,1,0:T(8,128)S(1)}, f32[128,64,128]{2,1,0:T(8,128)}, u32[]{:S(2)}) copy-start(f32[128,64,128]{2,1,0:T(8,128)} %all-gather.6.cloned.1.call-done) | copy-start | bytes 12582916
  161.4 2.1 %copy-start.5 = (f32[1024,1024]{1,0:T(8,128)}, f32[1024,1024]{1,0:T(8,128)S(1)}, u32[]{:S(2)}) copy-start(f32[1024,1024]{1,0:T(8,128)S(1)} %get-tuple-element.31.upper_ref) | copy-start | bytes 12582916
  163.5 1.0 copy-start.3
  166.4 1.2 copy-start.4
Sparse Core Ops, SparseCore 0:
  46.8 52.7 all-gather.5
  101.5 64.8 all-gather.3

commit v3 on v2

--- a/solution.py
+++ b/solution.py
@@ -115,14 +115,17 @@
             def _():
                 here = slice(now * TILE, (now + 1) * TILE)
                 after = slice((now + 1) * TILE, NPIV)
-                solved = exact_dot(inverse, upper_ref[here, after])
+                solved = parts_dot(split(inverse), split(upper_ref[here, after]), ((1,), (0,)))
                 upper_ref[here, after] = solved
+                solved_parts = split(solved)
                 for k in range(now + 1, PIVOT_TILES):
                     rows = slice(k * TILE, (k + 1) * TILE)
                     rest = slice(k * TILE, NPIV)
                     offset = (k - now - 1) * TILE
-                    upper_ref[rows, rest] = upper_ref[rows, rest] - exact_dot(
-                        solved[:, offset : offset + TILE], solved[:, offset:], ((0,), (0,))
+                    upper_ref[rows, rest] = upper_ref[rows, rest] - parts_dot(
+                        [part[:, offset : offset + TILE] for part in solved_parts],
+                        [part[:, offset:] for part in solved_parts],
+                        ((0,), (0,)),
                     )
 
         return carry
@@ -403,6 +406,11 @@
     own = child_blocks[0]
     positions = tile_map.astype(jnp.int32).reshape(2, 2, 32) // 32
 
+    def pick(count, v, even):
+        low = own[:count, 2 * v * TILE : (2 * v + 1) * TILE]
+        high = own[:count, (2 * v + 1) * TILE : 2 * (v + 1) * TILE]
+        return jnp.where(even, low, high)
+
     with jax.named_scope("pivot_block"):
         own_positions = positions[sibling, 0]
         hit = (own_positions[row_index] == 0) & (own_positions[col_index] == 0)
@@ -419,11 +427,20 @@
                 lower_half, ALL, [(at(p, i, c), at(1 - p, i, c + 8)) for p, i, c in places]
             )
         )
+    with jax.named_scope("siblings"):
+        first = jnp.stack([pick(TILE, v, sibling != 0) for v in range(2)])
+        first = lax.ppermute(first, "pair", SWAP)
+        handed = jnp.stack([pick(NPIV, v, sibling != 0) for v in range(2)])
+        handed, mine = lax.optimization_barrier((handed, mine))
+        received = lax.ppermute(handed, "pair", SWAP)
+
+    with jax.named_scope("pivot_gather"):
         mine = mine[None]
         for bit in (4, 2, 1):
             came = lax.ppermute(mine, "row", [(i, i ^ bit) for i in range(8)])
             mine = jnp.concatenate([mine, came])
-        mine = lax.optimization_barrier(mine)
+            if bit == 2:
+                mine, first = lax.optimization_barrier((mine, first))
         parts = lax.all_gather(mine, "col")
 
     row_positions = jnp.swapaxes(
@@ -438,15 +455,8 @@
         ]
     ).astype(jnp.int32)
 
-    def pick(count, v, even):
-        low = own[:count, 2 * v * TILE : (2 * v + 1) * TILE]
-        high = own[:count, (2 * v + 1) * TILE : 2 * (v + 1) * TILE]
-        return jnp.where(even, low, high)
-
     with jax.named_scope("pivot_rows"):
-        handed = jnp.stack([pick(TILE, v, sibling != 0) for v in range(2)])
-        came = lax.ppermute(handed, "pair", SWAP)
-        pivot_columns = assemble(meta, front_init, own, came)
+        pivot_columns = assemble(meta, front_init, own, first)
 
     with jax.named_scope("panel"):
         pivot_columns, mine = lax.optimization_barrier((pivot_columns, mine))
@@ -464,14 +474,11 @@
             sibling == 0, jnp.stack([same, crossed]), jnp.stack([crossed, same])
         )
         beneath = lax.all_gather(turned, "col")
-        pivot_columns, turned = lax.optimization_barrier((pivot_columns, turned))
+        pivot_columns, turned, received = lax.optimization_barrier(
+            (pivot_columns, turned, received)
+        )
         across = ring_gather(pivot_columns)
         across, parts = lax.optimization_barrier((across, parts))
-
-    with jax.named_scope("siblings"):
-        handed = jnp.stack([pick(NPIV, v, sibling != 0) for v in range(2)])
-        handed, parts = lax.optimization_barrier((handed, parts))
-        received = lax.ppermute(handed, "pair", SWAP)
 
     with jax.named_scope("factor"):
         upper, inverse = factor(row_index, parts)

time: 202 us -> 224 us (1.11)
  waiting for transfers between devices: 54.8 us -> 82.4 us
  Pallas kernels: 68.7 us -> 66 us
    ppermute x1, waiting for transfers between devices: 0.01 us -> 33.1 us  [body(): received = lax.ppermute(handed, 'pair', SWAP)]
    ppermute x3, starting transfers between devices: 3.7 us -> 10.5 us  [ring_gather(): ahead = lax.ppermute(ahead, 'row', down)]
    ppermute x3, starting transfers between devices: 5.77 us -> 0.01 us  [ring_gather(): behind = lax.ppermute(behind, 'row', up)]
    ppermute x3, waiting for transfers between devices: 10.4 us -> 6.64 us  [body(): came = lax.ppermute(mine, 'row', [(i, i ^ bit) for i in range(8)])]
    ppermute x1, starting transfers between devices: 5.74 us -> 2.64 us  [body(): received = lax.ppermute(handed, 'pair', SWAP)]
    pallas_call x1, Pallas kernels: 42.7 us -> 40 us  [factor(): pl.pallas_call(factor_kernel, out_shape=(jax.ShapeDtypeStruct((NPIV, NPIV...]
    ppermute x1, starting transfers between devices: 1.2 us -> 3.85 us  [ring_gather(): lax.ppermute(ahead[half:], 'row', down)]
    unnamed x14 -> x11, local copies, waits for them, and re-layouts: 8.18 us -> 6.66 us
  transfers between devices with their start and end apart: 20 -> 20, of which waited for: 14 -> 14; matrix products, arithmetic and copies ran while one was open for 1% -> 2% of each run, Pallas kernels for 22% -> 18%
where the time goes in v3:
time: 224 us; the launch traced here: 223 us
  waiting for transfers between devices  82.4 us (37%)
  Pallas kernels  66 us (29%)
  starting transfers between devices  46.8 us (21%)
  between operations  15 us (7%)
  local copies, waits for them, and re-layouts  9.44 us (4%)
  other arithmetic  3.8 us (2%)
    pallas_call x1, Pallas kernels, factor(): pl.pallas_call(factor_kernel, out_shape=(jax.ShapeDtypeStruct((NPIV, NPIV...  40 us
    ppermute x1, waiting for transfers between devices, body(): received = lax.ppermute(handed, 'pair', SWAP)  33.1 us
    pallas_call x1, Pallas kernels, finish(): pl.pallas_call(finish_kernel, grid=(2,), out_shape=jax.ShapeDtypeStruct((...  25.3 us
    ppermute x1, waiting for transfers between devices, body(): same = lax.ppermute(pivot_columns, ALL, routes[0])  18.6 us
    ppermute x3, waiting for transfers between devices, ring_gather(): behind = lax.ppermute(behind, 'row', up)  12.6 us
    ppermute x3, starting transfers between devices, body(): came = lax.ppermute(mine, 'row', [(i, i ^ bit) for i in range(8)])  11.2 us
    ppermute x3, starting transfers between devices, ring_gather(): ahead = lax.ppermute(ahead, 'row', down)  10.5 us
    unnamed x11, local copies, waits for them, and re-layouts  6.66 us
  transfers between devices with their start and end apart: 20, of which 14 were waited for; matrix products, arithmetic and copies ran while one was open for 2% of the time, Pallas kernels for 18%

profile of v3, /device:TPU:2, one launch (start us, length us, event | category | flops | bytes accessed | tf_op | source)
XLA Modules:
  0.0 223.5 jit_solution(18102105061317080409)
XLA Ops:
  6.5 0.8 reshape.94
  7.3 0.7 constant_dynamic-slice_fusion
  9.3 1.0 fusion.3
  10.3 5.1 %collective-permute-start.1 = (f32[64,128]{1,0:T(8,128)S(1)}, f32[64,128]{1,0:T(8,128)S(1)}, u32[]{:S(2)}, u32[]{:S(2)}) collective-permute-start(f32[64,128]{1,0:T(8,128)S(1)} %get-tuple-element.47), channel_id=1, source_target_pairs={{0,8},{1,9},{2,10},{3,11},{4,12},{5,13},{6,14},{7,15},{16,24},{17,... | collective-permute-start | bytes 98312 | tf_op jit(solution)/shard_map/pivot_block/ppermute | solution.py:425
  15.4 2.9 %collective-permute-start.2 = (f32[64,128]{1,0:T(8,128)S(1)}, f32[64,128]{1,0:T(8,128)S(1)}, u32[]{:S(2)}, u32[]{:S(2)}) collective-permute-start(f32[64,128]{1,0:T(8,128)S(1)} %get-tuple-element.47), channel_id=1, source_target_pairs={{0,136},{1,137},{2,138},{3,139},{4,140},{5,141},{6,142},{7,143},{1... | collective-permute-start | bytes 98312 | tf_op jit(solution)/shard_map/pivot_block/ppermute | solution.py:426
  18.3 3.3 %collective-permute-start = (f32[64,128]{1,0:T(8,128)S(1)}, f32[64,128]{1,0:T(8,128)S(1)}, u32[]{:S(2)}, u32[]{:S(2)}) collective-permute-start(f32[64,128]{1,0:T(8,128)S(1)} %get-tuple-element.46), channel_id=1, source_target_pairs={{0,128},{1,129},{2,130},{3,131},{4,132},{5,133},{6,134},{7,135},{1... | collective-permute-start | bytes 98312 | tf_op jit(solution)/shard_map/pivot_block/ppermute | solution.py:424
  21.6 1.6 fusion.1
  23.4 2.2 collective-permute-done
  25.6 7.3 %collective-permute-start.3 = (f32[1,64,128]{2,1,0:T(8,128)S(1)}, f32[1,64,128]{2,1,0:T(8,128)S(1)}, u32[]{:S(2)}, u32[]{:S(2)}) collective-permute-start(f32[1,64,128]{2,1,0:T(8,128)S(1)} %bitcast.29), channel_id=1, source_target_pairs={{0,64},{16,80},{32,96},{48,112},{64,0},{80,16},{96,32},{112,48},{1... | collective-permute-start | bytes 98312 | tf_op jit(solution)/shard_map/pivot_gather/ppermute | solution.py:440
  32.9 1.9 collective-permute-done.3
  34.8 2.0 collective-permute-start.4
  36.8 1.5 collective-permute-start.5
  38.3 2.4 %collective-permute-done.4 = f32[2,64,128]{2,1,0:T(8,128)S(1)} collective-permute-done((f32[2,64,128]{2,1,0:T(8,128)S(1)}, f32[2,64,128]{2,1,0:T(8,128)S(1)}, u32[]{:S(2)}, u32[]{:S(2)}) %collective-permute-start.4) | collective-permute-done | bytes 65568 | tf_op jit(solution)/shard_map/pivot_gather/ppermute | solution.py:440
  40.7 2.7 %collective-permute-done.5.came_ref = f32[2,128,128]{2,1,0:T(8,128)S(1)} collective-permute-done((f32[2,128,128]{2,1,0:T(8,128)S(1)}, f32[2,128,128]{2,1,0:T(8,128)S(1)}, u32[]{:S(2)}, u32[]{:S(2)}) %collective-permute-start.5) | collective-permute-done | bytes 131104 | tf_op jit(solution)/shard_map/siblings/ppermute | solution.py:432
  43.4 1.9 collective-permute-start.6
  45.3 0.7 constant_dynamic-update-slice_fusion.1
  46.0 2.4 %collective-permute-done.6 = f32[4,64,128]{2,1,0:T(8,128)S(1)} collective-permute-done((f32[4,64,128]{2,1,0:T(8,128)S(1)}, f32[4,64,128]{2,1,0:T(8,128)S(1)}, u32[]{:S(2)}, u32[]{:S(2)}) %collective-permute-start.6) | collective-permute-done | bytes 131104 | tf_op jit(solution)/shard_map/pivot_gather/ppermute | solution.py:440
  48.3 0.7 constant_dynamic-update-slice_fusion
  49.1 0.1 reshape.92
  49.2 0.2 dynamic-slice_reduce_fusion
  49.4 0.1 reshape.95
  49.5 0.2 fusion.5
  49.7 0.1 copy.6
  49.8 0.1 reshape.93
  49.9 0.1 concatenate.30.meta_ref
  50.0 1.7 copy-done.1
  51.7 0.7 assemble_pivot_rows.1.across_refs_0_
  52.4 3.7 %collective-permute-start.16 = (f32[384,128]{1,0:T(8,128)S(1)}, f32[384,128]{1,0:T(8,128)S(1)}, u32[]{:S(2)}, u32[]{:S(2)}) collective-permute-start(f32[384,128]{1,0:T(8,128)S(1)} %assemble_pivot_rows.1.across_refs_0_), channel_id=1, source_target_pairs={{0,0},{1,16},{2,32},{3,48},{4,64},{5,80},{6,96},{7,112},{8,8},{9,2... | collective-permute-start | bytes 589832 | tf_op jit(solution)/shard_map/panel/ppermute | solution.py:471
  56.1 2.1 collective-permute-start.17
  58.2 18.6 %collective-permute-done.16 = f32[384,128]{1,0:T(8,128)S(1)} collective-permute-done((f32[384,128]{1,0:T(8,128)S(1)}, f32[384,128]{1,0:T(8,128)S(1)}, u32[]{:S(2)}, u32[]{:S(2)}) %collective-permute-start.16) | collective-permute-done | bytes 196640 | tf_op jit(solution)/shard_map/panel/ppermute | solution.py:471
  76.8 4.2 %collective-permute-done.17 = f32[384,128]{1,0:T(8,128)S(1)} collective-permute-done((f32[384,128]{1,0:T(8,128)S(1)}, f32[384,128]{1,0:T(8,128)S(1)}, u32[]{:S(2)}, u32[]{:S(2)}) %collective-permute-start.17) | collective-permute-done | bytes 196640 | tf_op jit(solution)/shard_map/panel/ppermute | solution.py:472
  81.0 0.8 maximum_select_fusion
  81.8 2.6 %collective-permute-start.7 = (f32[2,1024,128]{2,1,0:T(8,128)S(1)}, f32[2,1024,128]{2,1,0:T(8,128)S(1)}, u32[]{:S(2)}, u32[]{:S(2)}) collective-permute-start(f32[2,1024,128]{2,1,0:T(8,128)S(1)} %pad_maximum_fusion), channel_id=1, source_target_pairs={{0,128},{128,0},{1,129},{129,1},{2,130},{130,2},{3,131},{131,3},{4... | collective-permute-start | bytes 3145736 | tf_op jit(solution)/shard_map/siblings/ppermute | solution.py:435
  84.5 33.1 %collective-permute-done.7 = f32[2,1024,128]{2,1,0:T(8,128)S(1)} collective-permute-done((f32[2,1024,128]{2,1,0:T(8,128)S(1)}, f32[2,1024,128]{2,1,0:T(8,128)S(1)}, u32[]{:S(2)}, u32[]{:S(2)}) %collective-permute-start.7) | collective-permute-done | bytes 1048608 | tf_op jit(solution)/shard_map/siblings/ppermute | solution.py:435
  117.6 3.2 %collective-permute-start.9 = (f32[384,128]{1,0:T(8,128)S(1)}, f32[384,128]{1,0:T(8,128)S(1)}, u32[]{:S(2)}, u32[]{:S(2)}) collective-permute-start(f32[384,128]{1,0:T(8,128)S(1)} %assemble_pivot_rows.1.across_refs_0_), channel_id=1, source_target_pairs={{0,112},{16,0},{32,16},{48,32},{64,48},{80,64},{96,80},{112,96},{1... | collective-permute-start | bytes 589832 | tf_op jit(solution)/shard_map/panel/ppermute | solution.py:360
  120.8 4.0 %collective-permute-done.8.across_refs_1_ = f32[384,128]{1,0:T(8,128)S(1)} collective-permute-done((f32[384,128]{1,0:T(8,128)S(1)}, f32[384,128]{1,0:T(8,128)S(1)}, u32[]{:S(2)}, u32[]{:S(2)}) %collective-permute-start.8) | collective-permute-done | bytes 196640 | tf_op jit(solution)/shard_map/panel/ppermute | solution.py:359
  124.8 3.5 %collective-permute-start.11 = (f32[384,128]{1,0:T(8,128)S(1)}, f32[384,128]{1,0:T(8,128)S(1)}, u32[]{:S(2)}, u32[]{:S(2)}) collective-permute-start(f32[384,128]{1,0:T(8,128)S(1)} %collective-permute-done.9.across_refs_2_), channel_id=1, source_target_pairs={{0,112},{16,0},{32,16},{48,32},{64,48},{80,64},{96,80},{112,96},{1... | collective-permute-start | bytes 589832 | tf_op jit(solution)/shard_map/panel/ppermute | solution.py:360
  128.4 4.9 %collective-permute-done.10.across_refs_3_ = f32[384,128]{1,0:T(8,128)S(1)} collective-permute-done((f32[384,128]{1,0:T(8,128)S(1)}, f32[384,128]{1,0:T(8,128)S(1)}, u32[]{:S(2)}, u32[]{:S(2)}) %collective-permute-start.10) | collective-permute-done | bytes 196640 | tf_op jit(solution)/shard_map/panel/ppermute | solution.py:359
  133.4 3.7 %collective-permute-start.13 = (f32[384,128]{1,0:T(8,128)S(1)}, f32[384,128]{1,0:T(8,128)S(1)}, u32[]{:S(2)}, u32[]{:S(2)}) collective-permute-start(f32[384,128]{1,0:T(8,128)S(1)} %collective-permute-done.11.across_refs_4_), channel_id=1, source_target_pairs={{0,112},{16,0},{32,16},{48,32},{64,48},{80,64},{96,80},{112,96},{1... | collective-permute-start | bytes 589832 | tf_op jit(solution)/shard_map/panel/ppermute | solution.py:360
  137.1 3.6 %collective-permute-done.12.across_refs_5_ = f32[384,128]{1,0:T(8,128)S(1)} collective-permute-done((f32[384,128]{1,0:T(8,128)S(1)}, f32[384,128]{1,0:T(8,128)S(1)}, u32[]{:S(2)}, u32[]{:S(2)}) %collective-permute-start.12) | collective-permute-done | bytes 196640 | tf_op jit(solution)/shard_map/panel/ppermute | solution.py:359
  140.7 0.1 collective-permute-start.14
  140.8 3.8 %collective-permute-start.15 = (f32[192,128]{1,0:T(8,128)S(1)}, f32[192,128]{1,0:T(8,128)S(1)}, u32[]{:S(2)}, u32[]{:S(2)}) collective-permute-start(f32[192,128]{1,0:T(8,128)S(1)} %slice.64), channel_id=1, source_target_pairs={{0,112},{16,0},{32,16},{48,32},{64,48},{80,64},{96,80},{112,96},{1... | collective-permute-start | bytes 294920 | tf_op jit(solution)/shard_map/panel/ppermute | solution.py:362
  144.7 1.9 collective-permute-done.14
  146.6 0.3 collective-permute-done.15
  147.0 2.3 %copy-done.2 = f32[128,64,128]{2,1,0:T(8,128)S(1)} copy-done((f32[128,64,128]{2,1,0:T(8,128)S(1)}, f32[128,64,128]{2,1,0:T(8,128)}, u32[]{:S(2)}) %copy-start.2) | copy-done | bytes 4194328
  149.2 40.0 %factor_pivots.1 = (f32[1024,1024]{1,0:T(8,128)S(1)}, f32[8,128,128]{2,1,0:T(8,128)S(1)}) custom-call(s32[1]{0:T(128)} %bitcast.1.row_ref, f32[16,8,64,128]{3,2,1,0:T(8,128)S(1)} %bitcast.27), custom_call_target="tpu_custom_call" | custom-call | flops 49999998976 | bytes 9437184 | tf_op jit(solution)/shard_map/factor/factor_pivots/pallas_call | solution.py:137
  189.3 2.0 copy-done.3
  191.3 25.3 %solve_and_update.1 = f32[3,4,128,384]{3,2,1,0:T(8,128)} custom-call(s32[24]{0:T(128)S(1)} %concatenate.30.meta_ref, f32[3,4,128,384]{3,2,1,0:T(8,128)} %bitcast.26, f32[2,4,128,512]{3,2,1,0:T(8,128)} %bitcast.24, f32[2,2,4,128,128]{4,3,2,1,0:T(8,128)S(1)} %bitcast.28, f32[384,128]{1,0:T(8,128)S(1)} %assemble_pivot_rows.1.across_refs_0_, ...), custom_call_target="tpu_custom_call" | custom-call | flops 15000000512 | bytes 25165824 | tf_op jit(solution)/shard_map/finish/solve_and_update/pallas_call | solution.py:303
  (33 shorter events, 0.4 us)
Async XLA Ops:
  6.5 140.4 %all-gather.6.cloned.1.call-start = ((), (), s32[]{:S(2)}) async-start(), calls=%async_computation.1 | async-start | bytes 4456448 | tf_op jit(solution)/shard_map/pivot_gather/all_gather | solution.py:444
  10.3 13.1 %collective-permute-start.1 = (f32[64,128]{1,0:T(8,128)S(1)}, f32[64,128]{1,0:T(8,128)S(1)}, u32[]{:S(2)}, u32[]{:S(2)}) collective-permute-start(f32[64,128]{1,0:T(8,128)S(1)} %get-tuple-element.47), channel_id=1, source_target_pairs={{0,8},{1,9},{2,10},{3,11},{4,12},{5,13},{6,14},{7,15},{16,24},{17,... | collective-permute-start | bytes 98312 | tf_op jit(solution)/shard_map/pivot_block/ppermute | solution.py:425
  15.4 8.0 %collective-permute-start.2 = (f32[64,128]{1,0:T(8,128)S(1)}, f32[64,128]{1,0:T(8,128)S(1)}, u32[]{:S(2)}, u32[]{:S(2)}) collective-permute-start(f32[64,128]{1,0:T(8,128)S(1)} %get-tuple-element.47), channel_id=1, source_target_pairs={{0,136},{1,137},{2,138},{3,139},{4,140},{5,141},{6,142},{7,143},{1... | collective-permute-start | bytes 98312 | tf_op jit(solution)/shard_map/pivot_block/ppermute | solution.py:426
  18.3 7.3 %collective-permute-start = (f32[64,128]{1,0:T(8,128)S(1)}, f32[64,128]{1,0:T(8,128)S(1)}, u32[]{:S(2)}, u32[]{:S(2)}) collective-permute-start(f32[64,128]{1,0:T(8,128)S(1)} %get-tuple-element.46), channel_id=1, source_target_pairs={{0,128},{1,129},{2,130},{3,131},{4,132},{5,133},{6,134},{7,135},{1... | collective-permute-start | bytes 98312 | tf_op jit(solution)/shard_map/pivot_block/ppermute | solution.py:424
  23.3 25.8 %copy-start.4 = (s32[2,64]{1,0:T(2,128)S(1)}, s32[2,64]{1,0:T(2,128)}, u32[]{:S(2)}) copy-start(s32[2,64]{1,0:T(2,128)} %param.5) | copy-start | bytes 1540
  23.3 26.7 %copy-start = (f32[1,1024,512]{2,1,0:T(8,128)S(1)}, f32[1,1024,512]{2,1,0:T(8,128)}, u32[]{:S(2)}) copy-start(f32[1,1024,512]{2,1,0:T(8,128)} %param.4) | copy-start | bytes 6291460
  25.6 9.2 %collective-permute-start.3 = (f32[1,64,128]{2,1,0:T(8,128)S(1)}, f32[1,64,128]{2,1,0:T(8,128)S(1)}, u32[]{:S(2)}, u32[]{:S(2)}) collective-permute-start(f32[1,64,128]{2,1,0:T(8,128)S(1)} %bitcast.29), channel_id=1, source_target_pairs={{0,64},{16,80},{32,96},{48,112},{64,0},{80,16},{96,32},{112,48},{1... | collective-permute-start | bytes 98312 | tf_op jit(solution)/shard_map/pivot_gather/ppermute | solution.py:440
  34.8 5.9 %collective-permute-start.4 = (f32[2,64,128]{2,1,0:T(8,128)S(1)}, f32[2,64,128]{2,1,0:T(8,128)S(1)}, u32[]{:S(2)}, u32[]{:S(2)}) collective-permute-start(f32[2,64,128]{2,1,0:T(8,128)S(1)} %pad_maximum_fusion.4), channel_id=1, source_target_pairs={{0,32},{16,48},{32,0},{48,16},{64,96},{80,112},{96,64},{112,80},{1... | collective-permute-start | bytes 196616 | tf_op jit(solution)/shard_map/pivot_gather/ppermute | solution.py:440
  36.8 6.6 %collective-permute-start.5 = (f32[2,128,128]{2,1,0:T(8,128)S(1)}, f32[2,128,128]{2,1,0:T(8,128)S(1)}, u32[]{:S(2)}, u32[]{:S(2)}) collective-permute-start(f32[2,128,128]{2,1,0:T(8,128)S(1)} %pad_maximum_fusion.3), channel_id=1, source_target_pairs={{0,128},{128,0},{1,129},{129,1},{2,130},{130,2},{3,131},{131,3},{4... | collective-permute-start | bytes 393224 | tf_op jit(solution)/shard_map/siblings/ppermute | solution.py:432
  43.4 5.0 %collective-permute-start.6 = (f32[4,64,128]{2,1,0:T(8,128)S(1)}, f32[4,64,128]{2,1,0:T(8,128)S(1)}, u32[]{:S(2)}, u32[]{:S(2)}) collective-permute-start(f32[4,64,128]{2,1,0:T(8,128)S(1)} %pad_maximum_fusion.2), channel_id=1, source_target_pairs={{0,16},{16,0},{32,48},{48,32},{64,80},{80,64},{96,112},{112,96},{1... | collective-permute-start | bytes 393224 | tf_op jit(solution)/shard_map/pivot_gather/ppermute | solution.py:440
  49.0 142.3 %all-gather.4.cloned.1.call-start = ((), (), s32[]{:S(2)}) async-start(), calls=%async_computation | async-start | bytes 6684672 | tf_op jit(solution)/shard_map/panel/all_gather | solution.py:476
  50.0 1.7 copy-start.1
  52.4 24.4 %collective-permute-start.16 = (f32[384,128]{1,0:T(8,128)S(1)}, f32[384,128]{1,0:T(8,128)S(1)}, u32[]{:S(2)}, u32[]{:S(2)}) collective-permute-start(f32[384,128]{1,0:T(8,128)S(1)} %assemble_pivot_rows.1.across_refs_0_), channel_id=1, source_target_pairs={{0,0},{1,16},{2,32},{3,48},{4,64},{5,80},{6,96},{7,112},{8,8},{9,2... | collective-permute-start | bytes 589832 | tf_op jit(solution)/shard_map/panel/ppermute | solution.py:471
  56.1 24.9 %collective-permute-start.17 = (f32[384,128]{1,0:T(8,128)S(1)}, f32[384,128]{1,0:T(8,128)S(1)}, u32[]{:S(2)}, u32[]{:S(2)}) collective-permute-start(f32[384,128]{1,0:T(8,128)S(1)} %assemble_pivot_rows.1.across_refs_0_), channel_id=1, source_target_pairs={{0,128},{1,144},{2,160},{3,176},{4,192},{5,208},{6,224},{7,240},{8... | collective-permute-start | bytes 589832 | tf_op jit(solution)/shard_map/panel/ppermute | solution.py:472
  81.8 35.8 %collective-permute-start.7 = (f32[2,1024,128]{2,1,0:T(8,128)S(1)}, f32[2,1024,128]{2,1,0:T(8,128)S(1)}, u32[]{:S(2)}, u32[]{:S(2)}) collective-permute-start(f32[2,1024,128]{2,1,0:T(8,128)S(1)} %pad_maximum_fusion), channel_id=1, source_target_pairs={{0,128},{128,0},{1,129},{129,1},{2,130},{130,2},{3,131},{131,3},{4... | collective-permute-start | bytes 3145736 | tf_op jit(solution)/shard_map/siblings/ppermute | solution.py:435
  117.6 7.3 %collective-permute-start.8 = (f32[384,128]{1,0:T(8,128)S(1)}, f32[384,128]{1,0:T(8,128)S(1)}, u32[]{:S(2)}, u32[]{:S(2)}) collective-permute-start(f32[384,128]{1,0:T(8,128)S(1)} %assemble_pivot_rows.1.across_refs_0_), channel_id=1, source_target_pairs={{0,16},{16,32},{32,48},{48,64},{64,80},{80,96},{96,112},{112,0},{1... | collective-permute-start | bytes 589832 | tf_op jit(solution)/shard_map/panel/ppermute | solution.py:359
  117.6 7.3 %collective-permute-start.9 = (f32[384,128]{1,0:T(8,128)S(1)}, f32[384,128]{1,0:T(8,128)S(1)}, u32[]{:S(2)}, u32[]{:S(2)}) collective-permute-start(f32[384,128]{1,0:T(8,128)S(1)} %assemble_pivot_rows.1.across_refs_0_), channel_id=1, source_target_pairs={{0,112},{16,0},{32,16},{48,32},{64,48},{80,64},{96,80},{112,96},{1... | collective-permute-start | bytes 589832 | tf_op jit(solution)/shard_map/panel/ppermute | solution.py:360
  124.8 8.5 %collective-permute-start.10 = (f32[384,128]{1,0:T(8,128)S(1)}, f32[384,128]{1,0:T(8,128)S(1)}, u32[]{:S(2)}, u32[]{:S(2)}) collective-permute-start(f32[384,128]{1,0:T(8,128)S(1)} %collective-permute-done.8.across_refs_1_), channel_id=1, source_target_pairs={{0,16},{16,32},{32,48},{48,64},{64,80},{80,96},{96,112},{112,0},{1... | collective-permute-start | bytes 589832 | tf_op jit(solution)/shard_map/panel/ppermute | solution.py:359
  124.8 8.5 %collective-permute-start.11 = (f32[384,128]{1,0:T(8,128)S(1)}, f32[384,128]{1,0:T(8,128)S(1)}, u32[]{:S(2)}, u32[]{:S(2)}) collective-permute-start(f32[384,128]{1,0:T(8,128)S(1)} %collective-permute-done.9.across_refs_2_), channel_id=1, source_target_pairs={{0,112},{16,0},{32,16},{48,32},{64,48},{80,64},{96,80},{112,96},{1... | collective-permute-start | bytes 589832 | tf_op jit(solution)/shard_map/panel/ppermute | solution.py:360
  133.3 7.4 %collective-permute-start.12 = (f32[384,128]{1,0:T(8,128)S(1)}, f32[384,128]{1,0:T(8,128)S(1)}, u32[]{:S(2)}, u32[]{:S(2)}) collective-permute-start(f32[384,128]{1,0:T(8,128)S(1)} %collective-permute-done.10.across_refs_3_), channel_id=1, source_target_pairs={{0,16},{16,32},{32,48},{48,64},{64,80},{80,96},{96,112},{112,0},{1... | collective-permute-start | bytes 589832 | tf_op jit(solution)/shard_map/panel/ppermute | solution.py:359
  133.4 7.4 %collective-permute-start.13 = (f32[384,128]{1,0:T(8,128)S(1)}, f32[384,128]{1,0:T(8,128)S(1)}, u32[]{:S(2)}, u32[]{:S(2)}) collective-permute-start(f32[384,128]{1,0:T(8,128)S(1)} %collective-permute-done.11.across_refs_4_), channel_id=1, source_target_pairs={{0,112},{16,0},{32,16},{48,32},{64,48},{80,64},{96,80},{112,96},{1... | collective-permute-start | bytes 589832 | tf_op jit(solution)/shard_map/panel/ppermute | solution.py:360
  140.7 5.9 %collective-permute-start.14 = (f32[192,128]{1,0:T(8,128)S(1)}, f32[192,128]{1,0:T(8,128)S(1)}, u32[]{:S(2)}, u32[]{:S(2)}) collective-permute-start(f32[192,128]{1,0:T(8,128)S(1)} %slice.63), channel_id=1, source_target_pairs={{0,16},{16,32},{32,48},{48,64},{64,80},{80,96},{96,112},{112,0},{1... | collective-permute-start | bytes 294920 | tf_op jit(solution)/shard_map/panel/ppermute | solution.py:362
  140.8 6.1 %collective-permute-start.15 = (f32[192,128]{1,0:T(8,128)S(1)}, f32[192,128]{1,0:T(8,128)S(1)}, u32[]{:S(2)}, u32[]{:S(2)}) collective-permute-start(f32[192,128]{1,0:T(8,128)S(1)} %slice.64), channel_id=1, source_target_pairs={{0,112},{16,0},{32,16},{48,32},{64,48},{80,64},{96,80},{112,96},{1... | collective-permute-start | bytes 294920 | tf_op jit(solution)/shard_map/panel/ppermute | solution.py:362
  147.0 2.3 %copy-start.2 = (f32[128,64,128]{2,1,0:T(8,128)S(1)}, f32[128,64,128]{2,1,0:T(8,128)}, u32[]{:S(2)}) copy-start(f32[128,64,128]{2,1,0:T(8,128)} %all-gather.6.cloned.1.call-done) | copy-start | bytes 12582916
  189.3 2.1 copy-start.3
Sparse Core Ops, SparseCore 0:
  49.2 63.2 all-gather.5
  114.3 41.8 all-gather.3

commit v4 on v3

--- a/solution.py
+++ b/solution.py
@@ -349,15 +349,17 @@
     return (pair * 8 + row) * 16 + col
 
 
-def ring_gather(block):
+def ring_gather(block, beside):
     up = [(i, (i + 1) % 8) for i in range(8)]
     down = [(i, (i - 1) % 8) for i in range(8)]
     half = block.shape[0] // 2
     behind = ahead = block
     blocks = [block]
-    for _ in range(3):
+    for turn in range(3):
         behind = lax.ppermute(behind, "row", up)
         ahead = lax.ppermute(ahead, "row", down)
+        if turn < len(beside):
+            behind, ahead, beside[turn] = lax.optimization_barrier((behind, ahead, beside[turn]))
         blocks += [behind, ahead]
     last = [lax.ppermute(behind[:half], "row", up), lax.ppermute(ahead[half:], "row", down)]
     return blocks + [jnp.concatenate(last)]
@@ -428,8 +430,6 @@
             )
         )
     with jax.named_scope("siblings"):
-        first = jnp.stack([pick(TILE, v, sibling != 0) for v in range(2)])
-        first = lax.ppermute(first, "pair", SWAP)
         handed = jnp.stack([pick(NPIV, v, sibling != 0) for v in range(2)])
         handed, mine = lax.optimization_barrier((handed, mine))
         received = lax.ppermute(handed, "pair", SWAP)
@@ -439,8 +439,7 @@
         for bit in (4, 2, 1):
             came = lax.ppermute(mine, "row", [(i, i ^ bit) for i in range(8)])
             mine = jnp.concatenate([mine, came])
-            if bit == 2:
-                mine, first = lax.optimization_barrier((mine, first))
+        mine, received = lax.optimization_barrier((mine, received))
         parts = lax.all_gather(mine, "col")
 
     row_positions = jnp.swapaxes(
@@ -456,7 +455,7 @@
     ).astype(jnp.int32)
 
     with jax.named_scope("pivot_rows"):
-        pivot_columns = assemble(meta, front_init, own, first)
+        pivot_columns = assemble(meta, front_init, own, received)
 
     with jax.named_scope("panel"):
         pivot_columns, mine = lax.optimization_barrier((pivot_columns, mine))
@@ -468,16 +467,13 @@
                     for away in range(2):
                         target = at(p ^ away, other, 8 * half + i)
                         routes[away].append((at(p, i, c), target))
-        same = lax.ppermute(pivot_columns, ALL, routes[0])
-        crossed = lax.ppermute(pivot_columns, ALL, routes[1])
+        beside = [lax.ppermute(pivot_columns, ALL, route) for route in routes]
+        across = ring_gather(pivot_columns, beside)
+        same, crossed = beside
         turned = jnp.where(
             sibling == 0, jnp.stack([same, crossed]), jnp.stack([crossed, same])
         )
         beneath = lax.all_gather(turned, "col")
-        pivot_columns, turned, received = lax.optimization_barrier(
-            (pivot_columns, turned, received)
-        )
-        across = ring_gather(pivot_columns)
         across, parts = lax.optimization_barrier((across, parts))
 
     with jax.named_scope("factor"):

time: 224 us -> 188 us (0.84)
  waiting for transfers between devices: 82.4 us -> 46.4 us
    ppermute x1, waiting for transfers between devices: 33.1 us -> 3.72 us  [body(): received = lax.ppermute(handed, 'pair', SWAP)]
    ppermute x3 -> x2, waiting for transfers between devices: 25.6 us -> 21.3 us  [body(): beside = [lax.ppermute(pivot_columns, ALL, route) for route in routes]]
    ppermute x3, waiting for transfers between devices: 12.6 us -> 8.58 us  [ring_gather(): behind = lax.ppermute(behind, 'row', up)]
    ppermute x3 -> x2, starting transfers between devices: 7.25 us -> 6.08 us  [body(): beside = [lax.ppermute(pivot_columns, ALL, route) for route in routes]]
    unnamed x11 -> x10, local copies, waits for them, and re-layouts: 6.66 us -> 5.93 us
  transfers between devices with their start and end apart: 20 -> 19, of which waited for: 14 -> 10; matrix products, arithmetic and copies ran while one was open for 2% -> 3% of each run, Pallas kernels for 18% -> 22%
where the time goes in v4:
time: 188 us; the launch traced here: 186 us
  Pallas kernels  66 us (35%)
  waiting for transfers between devices  46.4 us (25%)
  starting transfers between devices  45.5 us (24%)
  between operations  14.9 us (8%)
  local copies, waits for them, and re-layouts  8.02 us (4%)
  other arithmetic  5.36 us (3%)
    pallas_call x1, Pallas kernels, factor(): pl.pallas_call(factor_kernel, out_shape=(jax.ShapeDtypeStruct((NPIV, NPIV...  40 us
    pallas_call x1, Pallas kernels, finish(): pl.pallas_call(finish_kernel, grid=(2,), out_shape=jax.ShapeDtypeStruct((...  25.3 us
    ppermute x2, waiting for transfers between devices, body(): beside = [lax.ppermute(pivot_columns, ALL, route) for route in routes]  21.3 us
    ppermute x3, starting transfers between devices, ring_gather(): ahead = lax.ppermute(ahead, 'row', down)  10.9 us
    ppermute x3, starting transfers between devices, body(): came = lax.ppermute(mine, 'row', [(i, i ^ bit) for i in range(8)])  10.5 us
    ppermute x3, waiting for transfers between devices, body(): came = lax.ppermute(mine, 'row', [(i, i ^ bit) for i in range(8)])  8.77 us
    ppermute x3, waiting for transfers between devices, ring_gather(): behind = lax.ppermute(behind, 'row', up)  8.58 us
    ppermute x2, starting transfers between devices, body(): beside = [lax.ppermute(pivot_columns, ALL, route) for route in routes]  6.08 us
  transfers between devices with their start and end apart: 19, of which 10 were waited for; matrix products, arithmetic and copies ran while one was open for 3% of the time, Pallas kernels for 22%

profile of v4, /device:TPU:2, one launch (start us, length us, event | category | flops | bytes accessed | tf_op | source)
XLA Modules:
  0.0 186.3 jit_solution(11724117142410498998)
XLA Ops:
  6.5 0.8 reshape.94
  7.3 0.7 constant_dynamic-slice_fusion
  9.3 0.9 fusion.2
  10.2 5.1 %collective-permute-start.1 = (f32[64,128]{1,0:T(8,128)S(1)}, f32[64,128]{1,0:T(8,128)S(1)}, u32[]{:S(2)}, u32[]{:S(2)}) collective-permute-start(f32[64,128]{1,0:T(8,128)S(1)} %get-tuple-element.52), channel_id=1, source_target_pairs={{0,8},{1,9},{2,10},{3,11},{4,12},{5,13},{6,14},{7,15},{16,24},{17,... | collective-permute-start | bytes 98312 | tf_op jit(solution)/shard_map/pivot_block/ppermute | solution.py:427
  15.3 2.9 %collective-permute-start.2 = (f32[64,128]{1,0:T(8,128)S(1)}, f32[64,128]{1,0:T(8,128)S(1)}, u32[]{:S(2)}, u32[]{:S(2)}) collective-permute-start(f32[64,128]{1,0:T(8,128)S(1)} %get-tuple-element.52), channel_id=1, source_target_pairs={{0,136},{1,137},{2,138},{3,139},{4,140},{5,141},{6,142},{7,143},{1... | collective-permute-start | bytes 98312 | tf_op jit(solution)/shard_map/pivot_block/ppermute | solution.py:428
  18.2 3.3 %collective-permute-start = (f32[64,128]{1,0:T(8,128)S(1)}, f32[64,128]{1,0:T(8,128)S(1)}, u32[]{:S(2)}, u32[]{:S(2)}) collective-permute-start(f32[64,128]{1,0:T(8,128)S(1)} %get-tuple-element.51), channel_id=1, source_target_pairs={{0,128},{1,129},{2,130},{3,131},{4,132},{5,133},{6,134},{7,135},{1... | collective-permute-start | bytes 98312 | tf_op jit(solution)/shard_map/pivot_block/ppermute | solution.py:426
  21.5 1.6 fusion.1
  23.2 1.0 pad_maximum_fusion
  24.2 1.3 collective-permute-done
  25.5 1.5 collective-permute-start.6
  27.0 7.2 %collective-permute-start.3 = (f32[1,64,128]{2,1,0:T(8,128)S(1)}, f32[1,64,128]{2,1,0:T(8,128)S(1)}, u32[]{:S(2)}, u32[]{:S(2)}) collective-permute-start(f32[1,64,128]{2,1,0:T(8,128)S(1)} %bitcast.25), channel_id=1, source_target_pairs={{0,64},{16,80},{32,96},{48,112},{64,0},{80,16},{96,32},{112,48},{1... | collective-permute-start | bytes 98312 | tf_op jit(solution)/shard_map/pivot_gather/ppermute | solution.py:440
  34.2 1.9 %collective-permute-done.3 = f32[1,64,128]{2,1,0:T(8,128)S(1)} collective-permute-done((f32[1,64,128]{2,1,0:T(8,128)S(1)}, f32[1,64,128]{2,1,0:T(8,128)S(1)}, u32[]{:S(2)}, u32[]{:S(2)}) %collective-permute-start.3) | collective-permute-done | bytes 32800 | tf_op jit(solution)/shard_map/pivot_gather/ppermute | solution.py:440
  36.1 2.0 %collective-permute-start.4 = (f32[2,64,128]{2,1,0:T(8,128)S(1)}, f32[2,64,128]{2,1,0:T(8,128)S(1)}, u32[]{:S(2)}, u32[]{:S(2)}) collective-permute-start(f32[2,64,128]{2,1,0:T(8,128)S(1)} %pad_maximum_fusion.4), channel_id=1, source_target_pairs={{0,32},{16,48},{32,0},{48,16},{64,96},{80,112},{96,64},{112,80},{1... | collective-permute-start | bytes 196616 | tf_op jit(solution)/shard_map/pivot_gather/ppermute | solution.py:440
  38.1 3.2 %collective-permute-done.4 = f32[2,64,128]{2,1,0:T(8,128)S(1)} collective-permute-done((f32[2,64,128]{2,1,0:T(8,128)S(1)}, f32[2,64,128]{2,1,0:T(8,128)S(1)}, u32[]{:S(2)}, u32[]{:S(2)}) %collective-permute-start.4) | collective-permute-done | bytes 65568 | tf_op jit(solution)/shard_map/pivot_gather/ppermute | solution.py:440
  41.3 1.3 collective-permute-start.5
  42.6 3.7 %collective-permute-done.5 = f32[4,64,128]{2,1,0:T(8,128)S(1)} collective-permute-done((f32[4,64,128]{2,1,0:T(8,128)S(1)}, f32[4,64,128]{2,1,0:T(8,128)S(1)}, u32[]{:S(2)}, u32[]{:S(2)}) %collective-permute-start.5) | collective-permute-done | bytes 131104 | tf_op jit(solution)/shard_map/pivot_gather/ppermute | solution.py:440
  46.3 0.7 pad_maximum_fusion.1
  47.0 3.7 %collective-permute-done.6.came_ref = f32[2,1024,128]{2,1,0:T(8,128)S(1)} collective-permute-done((f32[2,1024,128]{2,1,0:T(8,128)}, f32[2,1024,128]{2,1,0:T(8,128)S(1)}, u32[]{:S(2)}, u32[]{:S(2)}) %collective-permute-start.6) | collective-permute-done | bytes 1048608 | tf_op jit(solution)/shard_map/siblings/ppermute | solution.py:435
  50.8 0.0 all-gather.4.cloned.1.call-start
  50.9 0.1 reshape.92
  50.9 0.2 dynamic-slice_reduce_fusion
  51.2 0.1 reshape.95
  51.3 0.2 fusion.4
  51.5 0.1 copy.6
  51.6 0.1 reshape.93
  51.7 0.1 concatenate.31.meta_ref
  51.8 1.7 copy-done.1
  53.5 0.7 assemble_pivot_rows.1.across_refs_0_
  54.1 2.0 %collective-permute-start.7 = (f32[384,128]{1,0:T(8,128)S(1)}, f32[384,128]{1,0:T(8,128)S(1)}, u32[]{:S(2)}, u32[]{:S(2)}) collective-permute-start(f32[384,128]{1,0:T(8,128)S(1)} %assemble_pivot_rows.1.across_refs_0_), channel_id=1, source_target_pairs={{0,16},{16,32},{32,48},{48,64},{64,80},{80,96},{96,112},{112,0},{1... | collective-permute-start | bytes 589832 | tf_op jit(solution)/shard_map/panel/ppermute | solution.py:359
  56.1 4.0 %collective-permute-start.8 = (f32[384,128]{1,0:T(8,128)S(1)}, f32[384,128]{1,0:T(8,128)S(1)}, u32[]{:S(2)}, u32[]{:S(2)}) collective-permute-start(f32[384,128]{1,0:T(8,128)S(1)} %assemble_pivot_rows.1.across_refs_0_), channel_id=1, source_target_pairs={{0,112},{16,0},{32,16},{48,32},{64,48},{80,64},{96,80},{112,96},{1... | collective-permute-start | bytes 589832 | tf_op jit(solution)/shard_map/panel/ppermute | solution.py:360
  60.2 2.1 %collective-permute-start.9 = (f32[384,128]{1,0:T(8,128)S(1)}, f32[384,128]{1,0:T(8,128)S(1)}, u32[]{:S(2)}, u32[]{:S(2)}) collective-permute-start(f32[384,128]{1,0:T(8,128)S(1)} %assemble_pivot_rows.1.across_refs_0_), channel_id=1, source_target_pairs={{0,0},{1,16},{2,32},{3,48},{4,64},{5,80},{6,96},{7,112},{8,8},{9,2... | collective-permute-start | bytes 589832 | tf_op jit(solution)/shard_map/panel/ppermute | solution.py:470
  62.3 4.0 %collective-permute-start.12 = (f32[384,128]{1,0:T(8,128)S(1)}, f32[384,128]{1,0:T(8,128)S(1)}, u32[]{:S(2)}, u32[]{:S(2)}) collective-permute-start(f32[384,128]{1,0:T(8,128)S(1)} %assemble_pivot_rows.1.across_refs_0_), channel_id=1, source_target_pairs={{0,128},{1,144},{2,160},{3,176},{4,192},{5,208},{6,224},{7,240},{8... | collective-permute-start | bytes 589832 | tf_op jit(solution)/shard_map/panel/ppermute | solution.py:470
  66.3 21.2 %collective-permute-done.9 = f32[384,128]{1,0:T(8,128)S(1)} collective-permute-done((f32[384,128]{1,0:T(8,128)S(1)}, f32[384,128]{1,0:T(8,128)S(1)}, u32[]{:S(2)}, u32[]{:S(2)}) %collective-permute-start.9) | collective-permute-done | bytes 196640 | tf_op jit(solution)/shard_map/panel/ppermute | solution.py:470
  87.5 3.2 %collective-permute-start.11 = (f32[384,128]{1,0:T(8,128)S(1)}, f32[384,128]{1,0:T(8,128)S(1)}, u32[]{:S(2)}, u32[]{:S(2)}) collective-permute-start(f32[384,128]{1,0:T(8,128)S(1)} %collective-permute-done.8.across_refs_2_), channel_id=1, source_target_pairs={{0,112},{16,0},{32,16},{48,32},{64,48},{80,64},{96,80},{112,96},{1... | collective-permute-start | bytes 589832 | tf_op jit(solution)/shard_map/panel/ppermute | solution.py:360
  90.7 0.0 collective-permute-done.12
  90.8 5.0 %collective-permute-done.10.across_refs_3_ = f32[384,128]{1,0:T(8,128)S(1)} collective-permute-done((f32[384,128]{1,0:T(8,128)S(1)}, f32[384,128]{1,0:T(8,128)S(1)}, u32[]{:S(2)}, u32[]{:S(2)}) %collective-permute-start.10) | collective-permute-done | bytes 196640 | tf_op jit(solution)/shard_map/panel/ppermute | solution.py:359
  95.8 0.8 maximum_select_fusion
  96.6 0.1 collective-permute-start.13
  96.7 3.6 %collective-permute-start.14 = (f32[384,128]{1,0:T(8,128)S(1)}, f32[384,128]{1,0:T(8,128)S(1)}, u32[]{:S(2)}, u32[]{:S(2)}) collective-permute-start(f32[384,128]{1,0:T(8,128)S(1)} %collective-permute-done.11.across_refs_4_), channel_id=1, source_target_pairs={{0,112},{16,0},{32,16},{48,32},{64,48},{80,64},{96,80},{112,96},{1... | collective-permute-start | bytes 589832 | tf_op jit(solution)/shard_map/panel/ppermute | solution.py:360
  100.3 3.6 %collective-permute-done.13.across_refs_5_ = f32[384,128]{1,0:T(8,128)S(1)} collective-permute-done((f32[384,128]{1,0:T(8,128)S(1)}, f32[384,128]{1,0:T(8,128)S(1)}, u32[]{:S(2)}, u32[]{:S(2)}) %collective-permute-start.13) | collective-permute-done | bytes 196640 | tf_op jit(solution)/shard_map/panel/ppermute | solution.py:359
  103.9 0.3 collective-permute-start.15
  104.2 0.4 collective-permute-done.14.across_refs_6_
  104.7 2.8 %collective-permute-start.16 = (f32[192,128]{1,0:T(8,128)S(1)}, f32[192,128]{1,0:T(8,128)S(1)}, u32[]{:S(2)}, u32[]{:S(2)}) collective-permute-start(f32[192,128]{1,0:T(8,128)S(1)} %slice.48), channel_id=1, source_target_pairs={{0,112},{16,0},{32,16},{48,32},{64,48},{80,64},{96,80},{112,96},{1... | collective-permute-start | bytes 294920 | tf_op jit(solution)/shard_map/panel/ppermute | solution.py:364
  107.4 2.3 %collective-permute-done.15 = f32[192,128]{1,0:T(8,128)S(1)} collective-permute-done((f32[192,128]{1,0:T(8,128)S(1)}, f32[192,128]{1,0:T(8,128)S(1)}, u32[]{:S(2)}, u32[]{:S(2)}) %collective-permute-start.15) | collective-permute-done | bytes 98336 | tf_op jit(solution)/shard_map/panel/ppermute | solution.py:364
  109.8 2.2 %copy-done.2 = f32[128,64,128]{2,1,0:T(8,128)S(1)} copy-done((f32[128,64,128]{2,1,0:T(8,128)S(1)}, f32[128,64,128]{2,1,0:T(8,128)}, u32[]{:S(2)}) %copy-start.2) | copy-done | bytes 4194328
  112.0 40.0 %factor_pivots.1 = (f32[1024,1024]{1,0:T(8,128)S(1)}, f32[8,128,128]{2,1,0:T(8,128)S(1)}) custom-call(s32[1]{0:T(128)} %bitcast.1.row_ref, f32[16,8,64,128]{3,2,1,0:T(8,128)S(1)} %bitcast.24), custom_call_target="tpu_custom_call" | custom-call | flops 49999998976 | bytes 9437184 | tf_op jit(solution)/shard_map/factor/factor_pivots/pallas_call | solution.py:137
  152.0 2.1 %copy-done.3 = f32[1024,1024]{1,0:T(8,128)} copy-done((f32[1024,1024]{1,0:T(8,128)}, f32[1024,1024]{1,0:T(8,128)S(1)}, u32[]{:S(2)}) %copy-start.3) | copy-done | bytes 4194328
  154.1 25.3 %solve_and_update.1 = f32[3,4,128,384]{3,2,1,0:T(8,128)} custom-call(s32[24]{0:T(128)S(1)} %concatenate.31.meta_ref, f32[3,4,128,384]{3,2,1,0:T(8,128)} %bitcast.22, f32[2,4,128,512]{3,2,1,0:T(8,128)} %bitcast.20, f32[2,2,4,128,128]{4,3,2,1,0:T(8,128)S(1)} %bitcast.23, f32[384,128]{1,0:T(8,128)S(1)} %assemble_pivot_rows.1.across_refs_0_, ...), custom_call_target="tpu_custom_call" | custom-call | flops 15000000512 | bytes 25165824 | tf_op jit(solution)/shard_map/finish/solve_and_update/pallas_call | solution.py:303
  (29 shorter events, 0.2 us)
Async XLA Ops:
  6.5 103.3 %all-gather.6.cloned.1.call-start = ((), (), s32[]{:S(2)}) async-start(), calls=%async_computation.1 | async-start | bytes 4456448 | tf_op jit(solution)/shard_map/pivot_gather/all_gather | solution.py:443
  10.2 14.0 %collective-permute-start.1 = (f32[64,128]{1,0:T(8,128)S(1)}, f32[64,128]{1,0:T(8,128)S(1)}, u32[]{:S(2)}, u32[]{:S(2)}) collective-permute-start(f32[64,128]{1,0:T(8,128)S(1)} %get-tuple-element.52), channel_id=1, source_target_pairs={{0,8},{1,9},{2,10},{3,11},{4,12},{5,13},{6,14},{7,15},{16,24},{17,... | collective-permute-start | bytes 98312 | tf_op jit(solution)/shard_map/pivot_block/ppermute | solution.py:427
  15.3 8.9 %collective-permute-start.2 = (f32[64,128]{1,0:T(8,128)S(1)}, f32[64,128]{1,0:T(8,128)S(1)}, u32[]{:S(2)}, u32[]{:S(2)}) collective-permute-start(f32[64,128]{1,0:T(8,128)S(1)} %get-tuple-element.52), channel_id=1, source_target_pairs={{0,136},{1,137},{2,138},{3,139},{4,140},{5,141},{6,142},{7,143},{1... | collective-permute-start | bytes 98312 | tf_op jit(solution)/shard_map/pivot_block/ppermute | solution.py:428
  18.2 7.3 %collective-permute-start = (f32[64,128]{1,0:T(8,128)S(1)}, f32[64,128]{1,0:T(8,128)S(1)}, u32[]{:S(2)}, u32[]{:S(2)}) collective-permute-start(f32[64,128]{1,0:T(8,128)S(1)} %get-tuple-element.51), channel_id=1, source_target_pairs={{0,128},{1,129},{2,130},{3,131},{4,132},{5,133},{6,134},{7,135},{1... | collective-permute-start | bytes 98312 | tf_op jit(solution)/shard_map/pivot_block/ppermute | solution.py:426
  23.1 27.7 %copy-start.4 = (s32[2,64]{1,0:T(2,128)S(1)}, s32[2,64]{1,0:T(2,128)}, u32[]{:S(2)}) copy-start(s32[2,64]{1,0:T(2,128)} %param.5) | copy-start | bytes 1540
  23.2 28.6 %copy-start = (f32[1,1024,512]{2,1,0:T(8,128)S(1)}, f32[1,1024,512]{2,1,0:T(8,128)}, u32[]{:S(2)}) copy-start(f32[1,1024,512]{2,1,0:T(8,128)} %param.4) | copy-start | bytes 6291460
  25.5 25.3 %collective-permute-start.6 = (f32[2,1024,128]{2,1,0:T(8,128)}, f32[2,1024,128]{2,1,0:T(8,128)S(1)}, u32[]{:S(2)}, u32[]{:S(2)}) collective-permute-start(f32[2,1024,128]{2,1,0:T(8,128)} %pad_maximum_fusion), channel_id=1, source_target_pairs={{0,128},{128,0},{1,129},{129,1},{2,130},{130,2},{3,131},{131,3},{4... | collective-permute-start | bytes 3145736 | tf_op jit(solution)/shard_map/siblings/ppermute | solution.py:435
  27.0 9.1 %collective-permute-start.3 = (f32[1,64,128]{2,1,0:T(8,128)S(1)}, f32[1,64,128]{2,1,0:T(8,128)S(1)}, u32[]{:S(2)}, u32[]{:S(2)}) collective-permute-start(f32[1,64,128]{2,1,0:T(8,128)S(1)} %bitcast.25), channel_id=1, source_target_pairs={{0,64},{16,80},{32,96},{48,112},{64,0},{80,16},{96,32},{112,48},{1... | collective-permute-start | bytes 98312 | tf_op jit(solution)/shard_map/pivot_gather/ppermute | solution.py:440
  36.1 5.2 %collective-permute-start.4 = (f32[2,64,128]{2,1,0:T(8,128)S(1)}, f32[2,64,128]{2,1,0:T(8,128)S(1)}, u32[]{:S(2)}, u32[]{:S(2)}) collective-permute-start(f32[2,64,128]{2,1,0:T(8,128)S(1)} %pad_maximum_fusion.4), channel_id=1, source_target_pairs={{0,32},{16,48},{32,0},{48,16},{64,96},{80,112},{96,64},{112,80},{1... | collective-permute-start | bytes 196616 | tf_op jit(solution)/shard_map/pivot_gather/ppermute | solution.py:440
  41.3 5.1 %collective-permute-start.5 = (f32[4,64,128]{2,1,0:T(8,128)S(1)}, f32[4,64,128]{2,1,0:T(8,128)S(1)}, u32[]{:S(2)}, u32[]{:S(2)}) collective-permute-start(f32[4,64,128]{2,1,0:T(8,128)S(1)} %pad_maximum_fusion.3), channel_id=1, source_target_pairs={{0,16},{16,0},{32,48},{48,32},{64,80},{80,64},{96,112},{112,96},{1... | collective-permute-start | bytes 393224 | tf_op jit(solution)/shard_map/pivot_gather/ppermute | solution.py:440
  50.8 103.3 %all-gather.4.cloned.1.call-start = ((), (), s32[]{:S(2)}) async-start(), calls=%async_computation | async-start | bytes 6684672 | tf_op jit(solution)/shard_map/panel/all_gather | solution.py:476
  51.8 1.7 copy-start.1
  54.1 12.1 %collective-permute-start.7 = (f32[384,128]{1,0:T(8,128)S(1)}, f32[384,128]{1,0:T(8,128)S(1)}, u32[]{:S(2)}, u32[]{:S(2)}) collective-permute-start(f32[384,128]{1,0:T(8,128)S(1)} %assemble_pivot_rows.1.across_refs_0_), channel_id=1, source_target_pairs={{0,16},{16,32},{32,48},{48,64},{64,80},{80,96},{96,112},{112,0},{1... | collective-permute-start | bytes 589832 | tf_op jit(solution)/shard_map/panel/ppermute | solution.py:359
  56.1 10.1 %collective-permute-start.8 = (f32[384,128]{1,0:T(8,128)S(1)}, f32[384,128]{1,0:T(8,128)S(1)}, u32[]{:S(2)}, u32[]{:S(2)}) collective-permute-start(f32[384,128]{1,0:T(8,128)S(1)} %assemble_pivot_rows.1.across_refs_0_), channel_id=1, source_target_pairs={{0,112},{16,0},{32,16},{48,32},{64,48},{80,64},{96,80},{112,96},{1... | collective-permute-start | bytes 589832 | tf_op jit(solution)/shard_map/panel/ppermute | solution.py:360
  60.2 27.3 %collective-permute-start.9 = (f32[384,128]{1,0:T(8,128)S(1)}, f32[384,128]{1,0:T(8,128)S(1)}, u32[]{:S(2)}, u32[]{:S(2)}) collective-permute-start(f32[384,128]{1,0:T(8,128)S(1)} %assemble_pivot_rows.1.across_refs_0_), channel_id=1, source_target_pairs={{0,0},{1,16},{2,32},{3,48},{4,64},{5,80},{6,96},{7,112},{8,8},{9,2... | collective-permute-start | bytes 589832 | tf_op jit(solution)/shard_map/panel/ppermute | solution.py:470
  62.3 28.5 %collective-permute-start.12 = (f32[384,128]{1,0:T(8,128)S(1)}, f32[384,128]{1,0:T(8,128)S(1)}, u32[]{:S(2)}, u32[]{:S(2)}) collective-permute-start(f32[384,128]{1,0:T(8,128)S(1)} %assemble_pivot_rows.1.across_refs_0_), channel_id=1, source_target_pairs={{0,128},{1,144},{2,160},{3,176},{4,192},{5,208},{6,224},{7,240},{8... | collective-permute-start | bytes 589832 | tf_op jit(solution)/shard_map/panel/ppermute | solution.py:470
  87.5 8.3 %collective-permute-start.10 = (f32[384,128]{1,0:T(8,128)S(1)}, f32[384,128]{1,0:T(8,128)S(1)}, u32[]{:S(2)}, u32[]{:S(2)}) collective-permute-start(f32[384,128]{1,0:T(8,128)S(1)} %collective-permute-done.7.across_refs_1_), channel_id=1, source_target_pairs={{0,16},{16,32},{32,48},{48,64},{64,80},{80,96},{96,112},{112,0},{1... | collective-permute-start | bytes 589832 | tf_op jit(solution)/shard_map/panel/ppermute | solution.py:359
  87.5 8.3 %collective-permute-start.11 = (f32[384,128]{1,0:T(8,128)S(1)}, f32[384,128]{1,0:T(8,128)S(1)}, u32[]{:S(2)}, u32[]{:S(2)}) collective-permute-start(f32[384,128]{1,0:T(8,128)S(1)} %collective-permute-done.8.across_refs_2_), channel_id=1, source_target_pairs={{0,112},{16,0},{32,16},{48,32},{64,48},{80,64},{96,80},{112,96},{1... | collective-permute-start | bytes 589832 | tf_op jit(solution)/shard_map/panel/ppermute | solution.py:360
  96.6 7.3 %collective-permute-start.13 = (f32[384,128]{1,0:T(8,128)S(1)}, f32[384,128]{1,0:T(8,128)S(1)}, u32[]{:S(2)}, u32[]{:S(2)}) collective-permute-start(f32[384,128]{1,0:T(8,128)S(1)} %collective-permute-done.10.across_refs_3_), channel_id=1, source_target_pairs={{0,16},{16,32},{32,48},{48,64},{64,80},{80,96},{96,112},{112,0},{1... | collective-permute-start | bytes 589832 | tf_op jit(solution)/shard_map/panel/ppermute | solution.py:359
  96.7 8.0 %collective-permute-start.14 = (f32[384,128]{1,0:T(8,128)S(1)}, f32[384,128]{1,0:T(8,128)S(1)}, u32[]{:S(2)}, u32[]{:S(2)}) collective-permute-start(f32[384,128]{1,0:T(8,128)S(1)} %collective-permute-done.11.across_refs_4_), channel_id=1, source_target_pairs={{0,112},{16,0},{32,16},{48,32},{64,48},{80,64},{96,80},{112,96},{1... | collective-permute-start | bytes 589832 | tf_op jit(solution)/shard_map/panel/ppermute | solution.py:360
  103.9 5.9 %collective-permute-start.15 = (f32[192,128]{1,0:T(8,128)S(1)}, f32[192,128]{1,0:T(8,128)S(1)}, u32[]{:S(2)}, u32[]{:S(2)}) collective-permute-start(f32[192,128]{1,0:T(8,128)S(1)} %slice.47), channel_id=1, source_target_pairs={{0,16},{16,32},{32,48},{48,64},{64,80},{80,96},{96,112},{112,0},{1... | collective-permute-start | bytes 294920 | tf_op jit(solution)/shard_map/panel/ppermute | solution.py:364
  104.7 5.1 %collective-permute-start.16 = (f32[192,128]{1,0:T(8,128)S(1)}, f32[192,128]{1,0:T(8,128)S(1)}, u32[]{:S(2)}, u32[]{:S(2)}) collective-permute-start(f32[192,128]{1,0:T(8,128)S(1)} %slice.48), channel_id=1, source_target_pairs={{0,112},{16,0},{32,16},{48,32},{64,48},{80,64},{96,80},{112,96},{1... | collective-permute-start | bytes 294920 | tf_op jit(solution)/shard_map/panel/ppermute | solution.py:364
  109.8 2.2 %copy-start.2 = (f32[128,64,128]{2,1,0:T(8,128)S(1)}, f32[128,64,128]{2,1,0:T(8,128)}, u32[]{:S(2)}) copy-start(f32[128,64,128]{2,1,0:T(8,128)} %all-gather.6.cloned.1.call-done) | copy-start | bytes 12582916
  152.0 2.1 %copy-start.3 = (f32[1024,1024]{1,0:T(8,128)}, f32[1024,1024]{1,0:T(8,128)S(1)}, u32[]{:S(2)}) copy-start(f32[1024,1024]{1,0:T(8,128)S(1)} %get-tuple-element.47.upper_ref) | copy-start | bytes 12582916
Sparse Core Ops, SparseCore 0:
  50.9 54.3 all-gather.5
  107.1 41.3 all-gather.3

commit v5 on v4

--- a/solution.py
+++ b/solution.py
@@ -31,61 +31,67 @@
 
 
 def parts_dot(a, b, contract):
-    total = None
-    for order in reversed(range(len(a))):
-        for i in range(order + 1):
-            term = lax.dot_general(
-                a[i], b[order - i], (contract, ((), ())), preferred_element_type=jnp.float32
-            )
-            total = term if total is None else total + term
-    return total
+    pairs = [(i, order - i) for order in range(len(a)) for i in range(order + 1)]
+    return lax.dot_general(
+        jnp.concatenate([a[i] for i, _ in pairs], axis=contract[0][0]),
+        jnp.concatenate([b[j] for _, j in pairs], axis=contract[1][0]),
+        (contract, ((), ())),
+        preferred_element_type=jnp.float32,
+    )
 
 
 def factor_tile(block):
     row = lax.broadcasted_iota(jnp.int32, (TILE, TILE), 0)
     lane = lax.broadcasted_iota(jnp.int32, (TILE, TILE), 1)
     remaining = jnp.concatenate([block, (row == lane).astype(jnp.float32)], axis=1)
-    strip_row = lax.broadcasted_iota(jnp.int32, (STRIP, TILE), 0)
+    group_row = lax.broadcasted_iota(jnp.int32, (GROUP, 2 * TILE), 0)
 
     def twice(x):
         return jnp.concatenate([x, x], axis=1)
 
-    def tall(x):
-        return jnp.concatenate([x] * (STRIP // 8), axis=0)
+    def tall(x, count):
+        return jnp.concatenate([x] * (count // GROUP), axis=0)
 
     done = []
     for first in range(0, TILE, STRIP):
         strip = remaining[:STRIP]
+        finished = []
         for k in range(0, STRIP, GROUP):
             at = first + k
+            count = STRIP - k - GROUP
+            top, beneath = strip[:GROUP], strip[GROUP:]
             columns, rows, corner, inverse = [], [], {}, []
             for t in range(GROUP):
-                columns.append(jnp.broadcast_to(strip[:, at + t : at + t + 1], (STRIP, TILE)))
-                rows.append(jnp.broadcast_to(strip[k + t : k + t + 1], (8, 2 * TILE)))
+                if count:
+                    columns.append(jnp.broadcast_to(beneath[:, at + t : at + t + 1], (count, TILE)))
+                rows.append(jnp.broadcast_to(top[t : t + 1], (GROUP, 2 * TILE)))
                 for r in range(t + 1):
                     corner[r, t] = jnp.broadcast_to(
-                        strip[k + r : k + r + 1, at + t : at + t + 1], (8, TILE)
+                        top[r : r + 1, at + t : at + t + 1], (GROUP, TILE)
                     )
             for r in range(GROUP):
                 inverse.append(1.0 / corner[r, r])
                 for t in range(r + 1, GROUP):
                     scale = corner[r, t] * inverse[r]
                     for u in range(t, GROUP):
-                        corner[t, u] = corner[t, u] - scale * corner[r, u]
-                    columns[t] = columns[t] - tall(scale) * columns[r]
+                        product = corner[r, t] * corner[r, u]
+                        corner[t, u] = corner[t, u] - product * inverse[r]
+                    if count:
+                        columns[t] = columns[t] - tall(scale, count) * columns[r]
                     rows[t] = rows[t] - twice(scale) * rows[r]
-            beneath = strip
-            if k + GROUP < STRIP:
+            if count:
                 for t in range(GROUP):
-                    share = jnp.where(strip_row >= k + GROUP, columns[t] * tall(inverse[t]), 0.0)
-                    beneath = beneath - twice(share) * tall(rows[t])
+                    share = columns[t] * tall(inverse[t], count)
+                    beneath = beneath - twice(share) * tall(rows[t], count)
+            result = None
             for t in range(GROUP):
                 root = lax.rsqrt(corner[t, t])
                 root = root * (1.5 - 0.5 * corner[t, t] * root * root)
-                beneath = jnp.where(
-                    twice(strip_row) == k + t, tall(rows[t] * twice(root)), beneath
-                )
+                scaled = rows[t] * twice(root)
+                result = scaled if t == 0 else jnp.where(group_row == t, scaled, result)
+            finished.append(result)
             strip = beneath
+        strip = jnp.concatenate(finished, axis=0)
         done.append(strip)
         if first + STRIP < TILE:
             change = exact_dot(strip[:, :TILE], strip, ((0,), (0,)))
@@ -358,8 +364,10 @@
     for turn in range(3):
         behind = lax.ppermute(behind, "row", up)
         ahead = lax.ppermute(ahead, "row", down)
-        if turn < len(beside):
-            behind, ahead, beside[turn] = lax.optimization_barrier((behind, ahead, beside[turn]))
+        if turn:
+            behind, ahead, beside[turn - 1] = lax.optimization_barrier(
+                (behind, ahead, beside[turn - 1])
+            )
         blocks += [behind, ahead]
     last = [lax.ppermute(behind[:half], "row", up), lax.ppermute(ahead[half:], "row", down)]
     return blocks + [jnp.concatenate(last)]
@@ -455,7 +463,7 @@
     ).astype(jnp.int32)
 
     with jax.named_scope("pivot_rows"):
-        pivot_columns = assemble(meta, front_init, own, received)
+        pivot_columns = assemble(meta, front_init[:TILE], own[:TILE], received)
 
     with jax.named_scope("panel"):
         pivot_columns, mine = lax.optimization_barrier((pivot_columns, mine))

time: 188 us -> 187 us (level)
  waiting for transfers between devices: 46.4 us -> 49.7 us
    ppermute x3, waiting for transfers between devices: 8.58 us -> 2.14 us  [ring_gather(): behind = lax.ppermute(behind, 'row', up)]
    all_gather x1, waiting for transfers between devices: 0.01 us -> 5.35 us  [body(): beneath = lax.all_gather(turned, 'col')]
    ppermute x1, starting transfers between devices: 0.34 us -> 4.94 us  [ring_gather(): lax.ppermute(behind[:half], 'row', up)]
    ppermute x2, starting transfers between devices: 6.08 us -> 2.21 us  [body(): beside = [lax.ppermute(pivot_columns, ALL, route) for route in routes]]
    ppermute x1, waiting for transfers between devices: 0.01 us -> 3 us  [ring_gather(): lax.ppermute(ahead[half:], 'row', down)]
    ppermute x1, starting transfers between devices: 2.78 us -> 0.26 us  [ring_gather(): lax.ppermute(ahead[half:], 'row', down)]
    ppermute x3, waiting for transfers between devices: 0.45 us -> 2.61 us  [ring_gather(): ahead = lax.ppermute(ahead, 'row', down)]
    slice x0 -> x2, local copies, waits for them, and re-layouts: none -> 1.93 us  [body(): pivot_columns = assemble(meta, front_init[:TILE], own[:TILE], received)]
  transfers between devices with their start and end apart: 19 -> 19, of which waited for: 10 -> 14; matrix products, arithmetic and copies ran while one was open for 3% -> 3% of each run, Pallas kernels for 22% -> 21%
where the time goes in v5:
time: 187 us; the launch traced here: 185 us
  Pallas kernels  64.2 us (34%)
  waiting for transfers between devices  49.7 us (27%)
  starting transfers between devices  43.7 us (23%)
  between operations  14.9 us (8%)
  local copies, waits for them, and re-layouts  8.29 us (4%)
  other arithmetic  4.39 us (2%)
    pallas_call x1, Pallas kernels, factor(): pl.pallas_call(factor_kernel, out_shape=(jax.ShapeDtypeStruct((NPIV, NPIV...  38.3 us
    pallas_call x1, Pallas kernels, finish(): pl.pallas_call(finish_kernel, grid=(2,), out_shape=jax.ShapeDtypeStruct((...  25.3 us
    ppermute x2, waiting for transfers between devices, body(): beside = [lax.ppermute(pivot_columns, ALL, route) for route in routes]  19.4 us
    ppermute x3, starting transfers between devices, ring_gather(): ahead = lax.ppermute(ahead, 'row', down)  12.7 us
    ppermute x3, starting transfers between devices, body(): came = lax.ppermute(mine, 'row', [(i, i ^ bit) for i in range(8)])  10.6 us
    ppermute x3, waiting for transfers between devices, body(): came = lax.ppermute(mine, 'row', [(i, i ^ bit) for i in range(8)])  8.66 us
    all_gather x1, waiting for transfers between devices, body(): beneath = lax.all_gather(turned, 'col')  5.35 us
    ppermute x1, starting transfers between devices, body(): lax.ppermute(lower_half, ALL, [(at(p, i, c), at(p, i, c + 8)) for p, i, c...  5.1 us
  transfers between devices with their start and end apart: 19, of which 14 were waited for; matrix products, arithmetic and copies ran while one was open for 3% of the time, Pallas kernels for 21%

profile of v5, /device:TPU:2, one launch (start us, length us, event | category | flops | bytes accessed | tf_op | source)
XLA Modules:
  0.0 185.3 jit_solution(14109510336161700173)
XLA Ops:
  6.5 0.8 reshape.95
  7.3 0.7 constant_dynamic-slice_fusion
  9.3 0.9 fusion.2
  10.2 5.1 %collective-permute-start.1 = (f32[64,128]{1,0:T(8,128)S(1)}, f32[64,128]{1,0:T(8,128)S(1)}, u32[]{:S(2)}, u32[]{:S(2)}) collective-permute-start(f32[64,128]{1,0:T(8,128)S(1)} %get-tuple-element.52), channel_id=1, source_target_pairs={{0,8},{1,9},{2,10},{3,11},{4,12},{5,13},{6,14},{7,15},{16,24},{17,... | collective-permute-start | bytes 98312 | tf_op jit(solution)/shard_map/pivot_block/ppermute | solution.py:435
  15.3 2.9 %collective-permute-start.2 = (f32[64,128]{1,0:T(8,128)S(1)}, f32[64,128]{1,0:T(8,128)S(1)}, u32[]{:S(2)}, u32[]{:S(2)}) collective-permute-start(f32[64,128]{1,0:T(8,128)S(1)} %get-tuple-element.52), channel_id=1, source_target_pairs={{0,136},{1,137},{2,138},{3,139},{4,140},{5,141},{6,142},{7,143},{1... | collective-permute-start | bytes 98312 | tf_op jit(solution)/shard_map/pivot_block/ppermute | solution.py:436
  18.2 3.3 %collective-permute-start = (f32[64,128]{1,0:T(8,128)S(1)}, f32[64,128]{1,0:T(8,128)S(1)}, u32[]{:S(2)}, u32[]{:S(2)}) collective-permute-start(f32[64,128]{1,0:T(8,128)S(1)} %get-tuple-element.51), channel_id=1, source_target_pairs={{0,128},{1,129},{2,130},{3,131},{4,132},{5,133},{6,134},{7,135},{1... | collective-permute-start | bytes 98312 | tf_op jit(solution)/shard_map/pivot_block/ppermute | solution.py:434
  21.5 1.6 fusion.1
  23.3 2.2 %collective-permute-done = f32[64,128]{1,0:T(8,128)S(1)} collective-permute-done((f32[64,128]{1,0:T(8,128)S(1)}, f32[64,128]{1,0:T(8,128)S(1)}, u32[]{:S(2)}, u32[]{:S(2)}) %collective-permute-start) | collective-permute-done | bytes 32800 | tf_op jit(solution)/shard_map/pivot_block/ppermute | solution.py:434
  25.5 1.5 collective-permute-start.6
  27.0 7.2 %collective-permute-start.3 = (f32[1,64,128]{2,1,0:T(8,128)S(1)}, f32[1,64,128]{2,1,0:T(8,128)S(1)}, u32[]{:S(2)}, u32[]{:S(2)}) collective-permute-start(f32[1,64,128]{2,1,0:T(8,128)S(1)} %bitcast.25), channel_id=1, source_target_pairs={{0,64},{16,80},{32,96},{48,112},{64,0},{80,16},{96,32},{112,48},{1... | collective-permute-start | bytes 98312 | tf_op jit(solution)/shard_map/pivot_gather/ppermute | solution.py:448
  34.2 1.9 %collective-permute-done.3 = f32[1,64,128]{2,1,0:T(8,128)S(1)} collective-permute-done((f32[1,64,128]{2,1,0:T(8,128)S(1)}, f32[1,64,128]{2,1,0:T(8,128)S(1)}, u32[]{:S(2)}, u32[]{:S(2)}) %collective-permute-start.3) | collective-permute-done | bytes 32800 | tf_op jit(solution)/shard_map/pivot_gather/ppermute | solution.py:448
  36.1 2.0 %collective-permute-start.4 = (f32[2,64,128]{2,1,0:T(8,128)S(1)}, f32[2,64,128]{2,1,0:T(8,128)S(1)}, u32[]{:S(2)}, u32[]{:S(2)}) collective-permute-start(f32[2,64,128]{2,1,0:T(8,128)S(1)} %pad_maximum_fusion.4), channel_id=1, source_target_pairs={{0,32},{16,48},{32,0},{48,16},{64,96},{80,112},{96,64},{112,80},{1... | collective-permute-start | bytes 196616 | tf_op jit(solution)/shard_map/pivot_gather/ppermute | solution.py:448
  38.1 3.2 %collective-permute-done.4 = f32[2,64,128]{2,1,0:T(8,128)S(1)} collective-permute-done((f32[2,64,128]{2,1,0:T(8,128)S(1)}, f32[2,64,128]{2,1,0:T(8,128)S(1)}, u32[]{:S(2)}, u32[]{:S(2)}) %collective-permute-start.4) | collective-permute-done | bytes 65568 | tf_op jit(solution)/shard_map/pivot_gather/ppermute | solution.py:448
  41.3 1.4 collective-permute-start.5
  42.7 3.6 %collective-permute-done.5 = f32[4,64,128]{2,1,0:T(8,128)S(1)} collective-permute-done((f32[4,64,128]{2,1,0:T(8,128)S(1)}, f32[4,64,128]{2,1,0:T(8,128)S(1)}, u32[]{:S(2)}, u32[]{:S(2)}) %collective-permute-start.5) | collective-permute-done | bytes 131104 | tf_op jit(solution)/shard_map/pivot_gather/ppermute | solution.py:448
  46.3 0.7 pad_maximum_fusion.1
  47.0 3.5 %collective-permute-done.6.came_ref = f32[2,1024,128]{2,1,0:T(8,128)S(1)} collective-permute-done((f32[2,1024,128]{2,1,0:T(8,128)S(1)}, f32[2,1024,128]{2,1,0:T(8,128)S(1)}, u32[]{:S(2)}, u32[]{:S(2)}) %collective-permute-start.6) | collective-permute-done | bytes 1048608 | tf_op jit(solution)/shard_map/siblings/ppermute | solution.py:443
  50.7 0.1 reshape.93
  50.7 0.9 slice.47.front_ref
  51.7 0.2 dynamic-slice_reduce_fusion
  51.9 0.1 reshape.96
  52.0 0.2 fusion.4
  52.2 0.1 copy.6
  52.3 0.1 reshape.94
  52.4 0.1 concatenate.31.meta_ref
  52.5 1.0 slice_bitcast_fusion.child_ref
  53.5 0.7 assemble_pivot_rows.1.across_refs_0_
  54.2 5.9 %collective-permute-start.8 = (f32[384,128]{1,0:T(8,128)S(1)}, f32[384,128]{1,0:T(8,128)S(1)}, u32[]{:S(2)}, u32[]{:S(2)}) collective-permute-start(f32[384,128]{1,0:T(8,128)S(1)} %assemble_pivot_rows.1.across_refs_0_), channel_id=1, source_target_pairs={{0,112},{16,0},{32,16},{48,32},{64,48},{80,64},{96,80},{112,96},{1... | collective-permute-start | bytes 589832 | tf_op jit(solution)/shard_map/panel/ppermute | solution.py:366
  60.1 2.2 %collective-permute-start.11 = (f32[384,128]{1,0:T(8,128)S(1)}, f32[384,128]{1,0:T(8,128)S(1)}, u32[]{:S(2)}, u32[]{:S(2)}) collective-permute-start(f32[384,128]{1,0:T(8,128)S(1)} %assemble_pivot_rows.1.across_refs_0_), channel_id=1, source_target_pairs={{0,0},{1,16},{2,32},{3,48},{4,64},{5,80},{6,96},{7,112},{8,8},{9,2... | collective-permute-start | bytes 589832 | tf_op jit(solution)/shard_map/panel/ppermute | solution.py:478
  62.3 1.0 collective-permute-done.8.across_refs_2_
  63.3 3.7 %collective-permute-start.10 = (f32[384,128]{1,0:T(8,128)S(1)}, f32[384,128]{1,0:T(8,128)S(1)}, u32[]{:S(2)}, u32[]{:S(2)}) collective-permute-start(f32[384,128]{1,0:T(8,128)S(1)} %collective-permute-done.8.across_refs_2_), channel_id=1, source_target_pairs={{0,112},{16,0},{32,16},{48,32},{64,48},{80,64},{96,80},{112,96},{1... | collective-permute-start | bytes 589832 | tf_op jit(solution)/shard_map/panel/ppermute | solution.py:366
  67.0 2.1 %collective-permute-done.7.across_refs_1_ = f32[384,128]{1,0:T(8,128)S(1)} collective-permute-done((f32[384,128]{1,0:T(8,128)S(1)}, f32[384,128]{1,0:T(8,128)S(1)}, u32[]{:S(2)}, u32[]{:S(2)}) %collective-permute-start.7) | collective-permute-done | bytes 196640 | tf_op jit(solution)/shard_map/panel/ppermute | solution.py:365
  69.2 12.9 %collective-permute-done.11 = f32[384,128]{1,0:T(8,128)S(1)} collective-permute-done((f32[384,128]{1,0:T(8,128)S(1)}, f32[384,128]{1,0:T(8,128)S(1)}, u32[]{:S(2)}, u32[]{:S(2)}) %collective-permute-start.11) | collective-permute-done | bytes 196640 | tf_op jit(solution)/shard_map/panel/ppermute | solution.py:478
  82.1 0.2 collective-permute-start.12
  82.3 3.1 %collective-permute-start.13 = (f32[384,128]{1,0:T(8,128)S(1)}, f32[384,128]{1,0:T(8,128)S(1)}, u32[]{:S(2)}, u32[]{:S(2)}) collective-permute-start(f32[384,128]{1,0:T(8,128)S(1)} %collective-permute-done.10.across_refs_4_), channel_id=1, source_target_pairs={{0,112},{16,0},{32,16},{48,32},{64,48},{80,64},{96,80},{112,96},{1... | collective-permute-start | bytes 589832 | tf_op jit(solution)/shard_map/panel/ppermute | solution.py:366
  85.3 6.5 %collective-permute-done.14 = f32[384,128]{1,0:T(8,128)S(1)} collective-permute-done((f32[384,128]{1,0:T(8,128)S(1)}, f32[384,128]{1,0:T(8,128)S(1)}, u32[]{:S(2)}, u32[]{:S(2)}) %collective-permute-start.14) | collective-permute-done | bytes 196640 | tf_op jit(solution)/shard_map/panel/ppermute | solution.py:478
  91.8 1.6 collective-permute-done.13.across_refs_6_
  93.5 0.8 maximum_select_fusion
  94.3 4.9 %collective-permute-start.15 = (f32[192,128]{1,0:T(8,128)S(1)}, f32[192,128]{1,0:T(8,128)S(1)}, u32[]{:S(2)}, u32[]{:S(2)}) collective-permute-start(f32[192,128]{1,0:T(8,128)S(1)} %slice.50), channel_id=1, source_target_pairs={{0,16},{16,32},{32,48},{48,64},{64,80},{80,96},{96,112},{112,0},{1... | collective-permute-start | bytes 294920 | tf_op jit(solution)/shard_map/panel/ppermute | solution.py:372
  99.2 0.3 collective-permute-start.16
  99.5 1.9 %collective-permute-done.15 = f32[192,128]{1,0:T(8,128)S(1)} collective-permute-done((f32[192,128]{1,0:T(8,128)S(1)}, f32[192,128]{1,0:T(8,128)S(1)}, u32[]{:S(2)}, u32[]{:S(2)}) %collective-permute-start.15) | collective-permute-done | bytes 98336 | tf_op jit(solution)/shard_map/panel/ppermute | solution.py:372
  101.5 3.0 %collective-permute-done.16 = f32[192,128]{1,0:T(8,128)S(1)} collective-permute-done((f32[192,128]{1,0:T(8,128)S(1)}, f32[192,128]{1,0:T(8,128)S(1)}, u32[]{:S(2)}, u32[]{:S(2)}) %collective-permute-start.16) | collective-permute-done | bytes 98336 | tf_op jit(solution)/shard_map/panel/ppermute | solution.py:372
  104.5 0.8 all-gather.6.cloned.1.call-done
  105.3 2.2 %copy-done = f32[128,64,128]{2,1,0:T(8,128)S(1)} copy-done((f32[128,64,128]{2,1,0:T(8,128)S(1)}, f32[128,64,128]{2,1,0:T(8,128)}, u32[]{:S(2)}) %copy-start) | copy-done | bytes 4194328
  107.5 38.3 %factor_pivots.1 = (f32[1024,1024]{1,0:T(8,128)S(1)}, f32[8,128,128]{2,1,0:T(8,128)S(1)}) custom-call(s32[1]{0:T(128)} %bitcast.1.row_ref, f32[16,8,64,128]{3,2,1,0:T(8,128)S(1)} %bitcast.21), custom_call_target="tpu_custom_call" | custom-call | flops 49999998976 | bytes 9437184 | tf_op jit(solution)/shard_map/factor/factor_pivots/pallas_call | solution.py:143
  145.8 2.0 %copy-done.1 = f32[1024,1024]{1,0:T(8,128)} copy-done((f32[1024,1024]{1,0:T(8,128)}, f32[1024,1024]{1,0:T(8,128)S(1)}, u32[]{:S(2)}) %copy-start.1) | copy-done | bytes 4194328
  147.8 5.4 %all-gather.4.cloned.1.call-done.beneath_ref = f32[16,2,384,128]{3,2,1,0:T(8,128)} async-done(((f32[1,2,384,128]{3,2,1,0:T(8,128)}), f32[16,2,384,128]{3,2,1,0:T(8,128)}) %all-gather.4.cloned.1.call-update) | async-done | bytes 6291472 | tf_op jit(solution)/shard_map/panel/all_gather | solution.py:484
  153.2 25.3 %solve_and_update.1 = f32[3,4,128,384]{3,2,1,0:T(8,128)} custom-call(s32[24]{0:T(128)S(1)} %concatenate.31.meta_ref, f32[3,4,128,384]{3,2,1,0:T(8,128)} %bitcast.31, f32[2,4,128,512]{3,2,1,0:T(8,128)} %bitcast.24, f32[2,2,4,128,128]{4,3,2,1,0:T(8,128)S(1)} %bitcast.20, f32[384,128]{1,0:T(8,128)S(1)} %assemble_pivot_rows.1.across_refs_0_, ...), custom_call_target="tpu_custom_call" | custom-call | flops 15000000512 | bytes 25165824 | tf_op jit(solution)/shard_map/finish/solve_and_update/pallas_call | solution.py:309
  (27 shorter events, 0.3 us)
Async XLA Ops:
  6.5 98.8 %all-gather.6.cloned.1.call-start = ((), (), s32[]{:S(2)}) async-start(), calls=%async_computation.1 | async-start | bytes 4456448 | tf_op jit(solution)/shard_map/pivot_gather/all_gather | solution.py:451
  10.2 13.1 %collective-permute-start.1 = (f32[64,128]{1,0:T(8,128)S(1)}, f32[64,128]{1,0:T(8,128)S(1)}, u32[]{:S(2)}, u32[]{:S(2)}) collective-permute-start(f32[64,128]{1,0:T(8,128)S(1)} %get-tuple-element.52), channel_id=1, source_target_pairs={{0,8},{1,9},{2,10},{3,11},{4,12},{5,13},{6,14},{7,15},{16,24},{17,... | collective-permute-start | bytes 98312 | tf_op jit(solution)/shard_map/pivot_block/ppermute | solution.py:435
  15.3 8.0 %collective-permute-start.2 = (f32[64,128]{1,0:T(8,128)S(1)}, f32[64,128]{1,0:T(8,128)S(1)}, u32[]{:S(2)}, u32[]{:S(2)}) collective-permute-start(f32[64,128]{1,0:T(8,128)S(1)} %get-tuple-element.52), channel_id=1, source_target_pairs={{0,136},{1,137},{2,138},{3,139},{4,140},{5,141},{6,142},{7,143},{1... | collective-permute-start | bytes 98312 | tf_op jit(solution)/shard_map/pivot_block/ppermute | solution.py:436
  18.2 7.3 %collective-permute-start = (f32[64,128]{1,0:T(8,128)S(1)}, f32[64,128]{1,0:T(8,128)S(1)}, u32[]{:S(2)}, u32[]{:S(2)}) collective-permute-start(f32[64,128]{1,0:T(8,128)S(1)} %get-tuple-element.51), channel_id=1, source_target_pairs={{0,128},{1,129},{2,130},{3,131},{4,132},{5,133},{6,134},{7,135},{1... | collective-permute-start | bytes 98312 | tf_op jit(solution)/shard_map/pivot_block/ppermute | solution.py:434
  23.2 27.5 %copy-start.2 = (s32[2,64]{1,0:T(2,128)S(1)}, s32[2,64]{1,0:T(2,128)}, u32[]{:S(2)}) copy-start(s32[2,64]{1,0:T(2,128)} %param.5) | copy-start | bytes 1540
  25.5 25.1 %collective-permute-start.6 = (f32[2,1024,128]{2,1,0:T(8,128)S(1)}, f32[2,1024,128]{2,1,0:T(8,128)S(1)}, u32[]{:S(2)}, u32[]{:S(2)}) collective-permute-start(f32[2,1024,128]{2,1,0:T(8,128)S(1)} %pad_maximum_fusion), channel_id=1, source_target_pairs={{0,128},{128,0},{1,129},{129,1},{2,130},{130,2},{3,131},{131,3},{4... | collective-permute-start | bytes 3145736 | tf_op jit(solution)/shard_map/siblings/ppermute | solution.py:443
  27.0 9.1 %collective-permute-start.3 = (f32[1,64,128]{2,1,0:T(8,128)S(1)}, f32[1,64,128]{2,1,0:T(8,128)S(1)}, u32[]{:S(2)}, u32[]{:S(2)}) collective-permute-start(f32[1,64,128]{2,1,0:T(8,128)S(1)} %bitcast.25), channel_id=1, source_target_pairs={{0,64},{16,80},{32,96},{48,112},{64,0},{80,16},{96,32},{112,48},{1... | collective-permute-start | bytes 98312 | tf_op jit(solution)/shard_map/pivot_gather/ppermute | solution.py:448
  36.1 5.2 %collective-permute-start.4 = (f32[2,64,128]{2,1,0:T(8,128)S(1)}, f32[2,64,128]{2,1,0:T(8,128)S(1)}, u32[]{:S(2)}, u32[]{:S(2)}) collective-permute-start(f32[2,64,128]{2,1,0:T(8,128)S(1)} %pad_maximum_fusion.4), channel_id=1, source_target_pairs={{0,32},{16,48},{32,0},{48,16},{64,96},{80,112},{96,64},{112,80},{1... | collective-permute-start | bytes 196616 | tf_op jit(solution)/shard_map/pivot_gather/ppermute | solution.py:448
  41.3 5.1 %collective-permute-start.5 = (f32[4,64,128]{2,1,0:T(8,128)S(1)}, f32[4,64,128]{2,1,0:T(8,128)S(1)}, u32[]{:S(2)}, u32[]{:S(2)}) collective-permute-start(f32[4,64,128]{2,1,0:T(8,128)S(1)} %pad_maximum_fusion.3), channel_id=1, source_target_pairs={{0,16},{16,0},{32,48},{48,32},{64,80},{80,64},{96,112},{112,96},{1... | collective-permute-start | bytes 393224 | tf_op jit(solution)/shard_map/pivot_gather/ppermute | solution.py:448
  50.6 102.6 %all-gather.4.cloned.1.call-start = ((), (), s32[]{:S(2)}) async-start(), calls=%async_computation | async-start | bytes 6684672 | tf_op jit(solution)/shard_map/panel/all_gather | solution.py:484
  54.2 9.1 %collective-permute-start.8 = (f32[384,128]{1,0:T(8,128)S(1)}, f32[384,128]{1,0:T(8,128)S(1)}, u32[]{:S(2)}, u32[]{:S(2)}) collective-permute-start(f32[384,128]{1,0:T(8,128)S(1)} %assemble_pivot_rows.1.across_refs_0_), channel_id=1, source_target_pairs={{0,112},{16,0},{32,16},{48,32},{64,48},{80,64},{96,80},{112,96},{1... | collective-permute-start | bytes 589832 | tf_op jit(solution)/shard_map/panel/ppermute | solution.py:366
  60.1 9.0 %collective-permute-start.7 = (f32[384,128]{1,0:T(8,128)S(1)}, f32[384,128]{1,0:T(8,128)S(1)}, u32[]{:S(2)}, u32[]{:S(2)}) collective-permute-start(f32[384,128]{1,0:T(8,128)S(1)} %assemble_pivot_rows.1.across_refs_0_), channel_id=1, source_target_pairs={{0,16},{16,32},{32,48},{48,64},{64,80},{80,96},{96,112},{112,0},{1... | collective-permute-start | bytes 589832 | tf_op jit(solution)/shard_map/panel/ppermute | solution.py:365
  60.1 21.9 %collective-permute-start.11 = (f32[384,128]{1,0:T(8,128)S(1)}, f32[384,128]{1,0:T(8,128)S(1)}, u32[]{:S(2)}, u32[]{:S(2)}) collective-permute-start(f32[384,128]{1,0:T(8,128)S(1)} %assemble_pivot_rows.1.across_refs_0_), channel_id=1, source_target_pairs={{0,0},{1,16},{2,32},{3,48},{4,64},{5,80},{6,96},{7,112},{8,8},{9,2... | collective-permute-start | bytes 589832 | tf_op jit(solution)/shard_map/panel/ppermute | solution.py:478
  63.3 18.8 %collective-permute-start.10 = (f32[384,128]{1,0:T(8,128)S(1)}, f32[384,128]{1,0:T(8,128)S(1)}, u32[]{:S(2)}, u32[]{:S(2)}) collective-permute-start(f32[384,128]{1,0:T(8,128)S(1)} %collective-permute-done.8.across_refs_2_), channel_id=1, source_target_pairs={{0,112},{16,0},{32,16},{48,32},{64,48},{80,64},{96,80},{112,96},{1... | collective-permute-start | bytes 589832 | tf_op jit(solution)/shard_map/panel/ppermute | solution.py:366
  69.1 12.9 %collective-permute-start.9 = (f32[384,128]{1,0:T(8,128)S(1)}, f32[384,128]{1,0:T(8,128)S(1)}, u32[]{:S(2)}, u32[]{:S(2)}) collective-permute-start(f32[384,128]{1,0:T(8,128)S(1)} %collective-permute-done.7.across_refs_1_), channel_id=1, source_target_pairs={{0,16},{16,32},{32,48},{48,64},{64,80},{80,96},{96,112},{112,0},{1... | collective-permute-start | bytes 589832 | tf_op jit(solution)/shard_map/panel/ppermute | solution.py:365
  69.1 22.7 %collective-permute-start.14 = (f32[384,128]{1,0:T(8,128)S(1)}, f32[384,128]{1,0:T(8,128)S(1)}, u32[]{:S(2)}, u32[]{:S(2)}) collective-permute-start(f32[384,128]{1,0:T(8,128)S(1)} %assemble_pivot_rows.1.across_refs_0_), channel_id=1, source_target_pairs={{0,128},{1,144},{2,160},{3,176},{4,192},{5,208},{6,224},{7,240},{8... | collective-permute-start | bytes 589832 | tf_op jit(solution)/shard_map/panel/ppermute | solution.py:478
  82.1 9.8 %collective-permute-start.12 = (f32[384,128]{1,0:T(8,128)S(1)}, f32[384,128]{1,0:T(8,128)S(1)}, u32[]{:S(2)}, u32[]{:S(2)}) collective-permute-start(f32[384,128]{1,0:T(8,128)S(1)} %collective-permute-done.9.across_refs_3_), channel_id=1, source_target_pairs={{0,16},{16,32},{32,48},{48,64},{64,80},{80,96},{96,112},{112,0},{1... | collective-permute-start | bytes 589832 | tf_op jit(solution)/shard_map/panel/ppermute | solution.py:365
  82.3 11.2 %collective-permute-start.13 = (f32[384,128]{1,0:T(8,128)S(1)}, f32[384,128]{1,0:T(8,128)S(1)}, u32[]{:S(2)}, u32[]{:S(2)}) collective-permute-start(f32[384,128]{1,0:T(8,128)S(1)} %collective-permute-done.10.across_refs_4_), channel_id=1, source_target_pairs={{0,112},{16,0},{32,16},{48,32},{64,48},{80,64},{96,80},{112,96},{1... | collective-permute-start | bytes 589832 | tf_op jit(solution)/shard_map/panel/ppermute | solution.py:366
  94.3 7.2 %collective-permute-start.15 = (f32[192,128]{1,0:T(8,128)S(1)}, f32[192,128]{1,0:T(8,128)S(1)}, u32[]{:S(2)}, u32[]{:S(2)}) collective-permute-start(f32[192,128]{1,0:T(8,128)S(1)} %slice.50), channel_id=1, source_target_pairs={{0,16},{16,32},{32,48},{48,64},{64,80},{80,96},{96,112},{112,0},{1... | collective-permute-start | bytes 294920 | tf_op jit(solution)/shard_map/panel/ppermute | solution.py:372
  99.2 5.2 %collective-permute-start.16 = (f32[192,128]{1,0:T(8,128)S(1)}, f32[192,128]{1,0:T(8,128)S(1)}, u32[]{:S(2)}, u32[]{:S(2)}) collective-permute-start(f32[192,128]{1,0:T(8,128)S(1)} %slice.51), channel_id=1, source_target_pairs={{0,112},{16,0},{32,16},{48,32},{64,48},{80,64},{96,80},{112,96},{1... | collective-permute-start | bytes 294920 | tf_op jit(solution)/shard_map/panel/ppermute | solution.py:372
  105.3 2.2 %copy-start = (f32[128,64,128]{2,1,0:T(8,128)S(1)}, f32[128,64,128]{2,1,0:T(8,128)}, u32[]{:S(2)}) copy-start(f32[128,64,128]{2,1,0:T(8,128)} %all-gather.6.cloned.1.call-done) | copy-start | bytes 12582916
  145.7 2.1 %copy-start.1 = (f32[1024,1024]{1,0:T(8,128)}, f32[1024,1024]{1,0:T(8,128)S(1)}, u32[]{:S(2)}) copy-start(f32[1024,1024]{1,0:T(8,128)S(1)} %get-tuple-element.47.upper_ref) | copy-start | bytes 12582916
Sparse Core Ops, SparseCore 0:
  50.7 54.5 all-gather.5
  107.1 45.9 all-gather.3

commit v6 on v5

--- a/solution.py
+++ b/solution.py
@@ -100,9 +100,40 @@
     return jnp.where(lane >= row, whole[:, :TILE], 0.0), whole[:, TILE:]
 
 
-def factor_kernel(row_ref, parts_ref, upper_ref, inverse_ref):
+def solve(source, upper_parts_ref, wide_parts_ref, solved_ref, solved_parts_ref):
+    for j in range(PIVOT_TILES // 2):
+        columns = slice(2 * j * TILE, 2 * (j + 1) * TILE)
+        rest = jnp.concatenate([source(2 * j), source(2 * j + 1)], axis=1)
+        if j:
+            before = slice(0, 2 * j * TILE)
+            rest = rest - parts_dot(
+                [ref[:, before] for ref in solved_parts_ref],
+                [ref[before, columns] for ref in upper_parts_ref],
+                ((1,), (0,)),
+            )
+        result = parts_dot(split(rest), [ref[j] for ref in wide_parts_ref], ((1,), (0,)))
+        solved_ref[:, columns] = result
+        for ref, part in zip(solved_parts_ref, split(result)):
+            ref[:, columns] = part
+
+
+def factor_kernel(
+    meta_ref,
+    parts_ref,
+    across_refs,
+    upper_parts_ref,
+    wide_parts_ref,
+    column_parts_ref,
+    pivot_ref,
+    upper_ref,
+    inverse_ref,
+    across_ref,
+    solved_ref,
+):
+    row_index = meta_ref[1]
+    column_index = meta_ref[2]
     for i in range(PIVOT_TILES):
-        away = i ^ row_ref[0]
+        away = i ^ row_index
         place = (away & 1) * 4 + (away & 2) + (away >> 2)
         for c in range(i, PIVOT_TILES):
             for half in range(2):
@@ -138,25 +169,79 @@
 
     lax.fori_loop(0, PIVOT_TILES, step, 0)
 
-
-def factor(row_index, parts):
+    for j in range(PIVOT_TILES // 2):
+        rows = slice(2 * j * TILE, 2 * (j + 1) * TILE)
+        after = slice(2 * (j + 1) * TILE, NPIV)
+        if j < PIVOT_TILES // 2 - 1:
+            for ref, part in zip(upper_parts_ref, split(upper_ref[rows, after])):
+                ref[rows, after] = part
+        low, high = inverse_ref[2 * j], inverse_ref[2 * j + 1]
+        between = upper_ref[
+            2 * j * TILE : (2 * j + 1) * TILE, (2 * j + 1) * TILE : 2 * (j + 1) * TILE
+        ]
+        corner = -exact_dot(low, exact_dot(between, high))
+        for ref, l, h, c in zip(wide_parts_ref, split(low), split(high), split(corner)):
+            ref[j, :TILE, :TILE] = l
+            ref[j, TILE:, TILE:] = h
+            ref[j, :TILE, TILE:] = c
+            ref[j, TILE:, :TILE] = jnp.zeros((TILE, TILE), jnp.bfloat16)
+
+    for behind, ref in zip(RING, across_refs):
+        across_ref[lax.rem(row_index - behind + 8, 8)] = ref[...]
+    solve(
+        lambda i: across_ref[i], upper_parts_ref, wide_parts_ref, solved_ref, column_parts_ref
+    )
+
+    own_row = pl.ds(pl.multiple_of(row_index * TILE, TILE), TILE)
+    own_column = pl.ds(pl.multiple_of(lax.rem(column_index, 8) * TILE, TILE), TILE)
+    for n in range(3):
+        lanes = slice(n * TILE, (n + 1) * TILE)
+        pivot_ref[:, lanes] = solved_ref[lanes, own_row].T
+
+    @pl.when(column_index < PIVOT_TILES)
+    def _():
+        @pl.when(row_index < column_index)
+        def _():
+            pivot_ref[:, :TILE] = upper_ref[own_row, own_column]
+
+        @pl.when(row_index > column_index)
+        def _():
+            pivot_ref[:, :TILE] = upper_ref[own_column, own_row].T
+
+        @pl.when(row_index == column_index)
+        def _():
+            row = lax.broadcasted_iota(jnp.int32, (TILE, TILE), 0)
+            lane = lax.broadcasted_iota(jnp.int32, (TILE, TILE), 1)
+            tile = upper_ref[own_row, own_column]
+            pivot_ref[:, :TILE] = jnp.where(row > lane, tile.T, tile)
+
+
+def factor(meta, parts, across):
+    width = across[0].shape[0]
+    whole = pl.BlockSpec(memory_space=pltpu.VMEM)
+    halves = lambda *shape: [jax.ShapeDtypeStruct(shape, jnp.bfloat16) for _ in range(PARTS)]
     return pl.pallas_call(
         factor_kernel,
         out_shape=(
-            jax.ShapeDtypeStruct((NPIV, NPIV), jnp.float32),
-            jax.ShapeDtypeStruct((PIVOT_TILES, TILE, TILE), jnp.float32),
+            halves(NPIV, NPIV),
+            halves(PIVOT_TILES // 2, 2 * TILE, 2 * TILE),
+            halves(width, NPIV),
+            jax.ShapeDtypeStruct((TILE, width), jnp.float32),
         ),
-        in_specs=[
-            pl.BlockSpec(memory_space=pltpu.SMEM),
-            pl.BlockSpec(memory_space=pltpu.VMEM),
+        in_specs=[pl.BlockSpec(memory_space=pltpu.SMEM), whole, [whole] * 8],
+        out_specs=([whole] * PARTS, [whole] * PARTS, [whole] * PARTS, whole),
+        scratch_shapes=[
+            pltpu.VMEM((NPIV, NPIV), jnp.float32),
+            pltpu.VMEM((PIVOT_TILES, TILE, TILE), jnp.float32),
+            pltpu.VMEM((8, width, TILE), jnp.float32),
+            pltpu.VMEM((width, NPIV), jnp.float32),
         ],
-        out_specs=tuple(pl.BlockSpec(memory_space=pltpu.VMEM) for _ in range(2)),
-        compiler_params=pltpu.CompilerParams(vmem_limit_bytes=24 * 2**20),
+        compiler_params=pltpu.CompilerParams(vmem_limit_bytes=36 * 2**20),
         cost_estimate=pl.CostEstimate(
             flops=FACTOR_FLOPS, bytes_accessed=9 * 2**20, transcendentals=0
         ),
         name="factor_pivots",
-    )(row_index.astype(jnp.int32).reshape(1), parts)
+    )(meta, parts, across)
 
 
 def finish_kernel(
@@ -164,73 +249,30 @@
     front_ref,
     child_ref,
     received_ref,
-    across_refs,
     beneath_ref,
-    upper_ref,
-    inverse_ref,
-    out_ref,
     upper_parts_ref,
     wide_parts_ref,
-    across_ref,
+    column_parts_ref,
+    pivot_ref,
+    out_ref,
     solved_ref,
     solved_parts_ref,
 ):
     half_step = pl.program_id(0)
     sibling = meta_ref[0]
-    row_index = meta_ref[1]
     column_index = meta_ref[2]
-    width = across_ref.shape[1]
-    column_rows = slice(2 * width, 3 * width)
-
-    def solve(count, source):
-        for j in range(PIVOT_TILES // 2):
-            columns = slice(2 * j * TILE, 2 * (j + 1) * TILE)
-            rest = jnp.concatenate([source(2 * j), source(2 * j + 1)], axis=1)
-            if j:
-                before = slice(0, 2 * j * TILE)
-                rest = rest - parts_dot(
-                    [ref[:count, before] for ref in solved_parts_ref],
-                    [ref[before, columns] for ref in upper_parts_ref],
-                    ((1,), (0,)),
-                )
-            result = parts_dot(split(rest), [ref[j] for ref in wide_parts_ref], ((1,), (0,)))
-            solved_ref[:count, columns] = result
-            for ref, part in zip(solved_parts_ref, split(result)):
-                ref[:count, columns] = part
-
-    def panel(i):
-        return [beneath_ref[i, 0], beneath_ref[8 + i, 0]]
-
-    @pl.when(half_step == 0)
-    def _():
-        for j in range(PIVOT_TILES // 2):
-            rows = slice(2 * j * TILE, 2 * (j + 1) * TILE)
-            after = slice(2 * (j + 1) * TILE, NPIV)
-            if j < PIVOT_TILES // 2 - 1:
-                for ref, part in zip(upper_parts_ref, split(upper_ref[rows, after])):
-                    ref[rows, after] = part
-            low, high = inverse_ref[2 * j], inverse_ref[2 * j + 1]
-            between = upper_ref[
-                2 * j * TILE : (2 * j + 1) * TILE, (2 * j + 1) * TILE : 2 * (j + 1) * TILE
-            ]
-            corner = -exact_dot(low, exact_dot(between, high))
-            for ref, l, h, c in zip(wide_parts_ref, split(low), split(high), split(corner)):
-                ref[j, :TILE, :TILE] = l
-                ref[j, TILE:, TILE:] = h
-                ref[j, :TILE, TILE:] = c
-                ref[j, TILE:, :TILE] = jnp.zeros((TILE, TILE), jnp.bfloat16)
-
-        for behind, ref in zip(RING, across_refs):
-            across_ref[lax.rem(row_index - behind + 8, 8)] = ref[...]
-        solve(3 * width, lambda i: jnp.concatenate(panel(i) + [across_ref[i]]))
-
-    @pl.when(half_step > 0)
-    def _():
-        solve(2 * width, lambda i: jnp.concatenate(panel(i)))
-
+    width = pivot_ref.shape[1]
+
+    solve(
+        lambda i: jnp.concatenate([beneath_ref[i, 0], beneath_ref[8 + i, 0]]),
+        upper_parts_ref,
+        wide_parts_ref,
+        solved_ref,
+        solved_parts_ref,
+    )
     update = parts_dot(
-        [ref[: 2 * width] for ref in solved_parts_ref],
-        [ref[column_rows] for ref in solved_parts_ref],
+        [ref[...] for ref in solved_parts_ref],
+        [ref[...] for ref in column_parts_ref],
         ((1,), (1,)),
     )
 
@@ -278,31 +320,10 @@
 
     @pl.when(half_step == 0)
     def _():
-        own_row = pl.ds(pl.multiple_of(row_index * TILE, TILE), TILE)
-        for n in range(3):
-            lanes = slice(n * TILE, (n + 1) * TILE)
-            top = 2 * width + n * TILE
-            out_ref[0, 0, :, lanes] = solved_ref[top : top + TILE, own_row].T
-
-        @pl.when(pivot_column)
-        def _():
-            @pl.when(row_index < column_index)
-            def _():
-                out_ref[0, 0, :, :TILE] = upper_ref[own_row, own_column]
-
-            @pl.when(row_index > column_index)
-            def _():
-                out_ref[0, 0, :, :TILE] = upper_ref[own_column, own_row].T
-
-            @pl.when(row_index == column_index)
-            def _():
-                row = lax.broadcasted_iota(jnp.int32, (TILE, TILE), 0)
-                lane = lax.broadcasted_iota(jnp.int32, (TILE, TILE), 1)
-                tile = upper_ref[own_row, own_column]
-                out_ref[0, 0, :, :TILE] = jnp.where(row > lane, tile.T, tile)
-
-
-def finish(meta, front, child, received, across, beneath, upper, inverse):
+        out_ref[0, 0, :, :] = pivot_ref[...]
+
+
+def finish(meta, front, child, received, beneath, upper, wide, column, pivot):
     width = front.shape[1]
     whole = pl.BlockSpec(memory_space=pltpu.VMEM)
     held = lambda *shape: [pltpu.VMEM(shape, jnp.bfloat16) for _ in range(PARTS)]
@@ -315,18 +336,16 @@
             pl.BlockSpec((3, 2, TILE, width), lambda g: (0, g, 0, 0)),
             pl.BlockSpec((2, 2, TILE, 4 * TILE), lambda g: (0, g, 0, 0)),
             pl.BlockSpec((2, 2, 2, TILE, TILE), lambda g: (0, 0, g, 0, 0)),
-            [whole] * 8,
             pl.BlockSpec((16, 1, width, TILE), lambda g: (0, g, 0, 0)),
-            whole,
+            [whole] * PARTS,
+            [whole] * PARTS,
+            [whole] * PARTS,
             whole,
         ],
         out_specs=pl.BlockSpec((3, 2, TILE, width), lambda g: (0, g, 0, 0)),
         scratch_shapes=[
-            held(NPIV, NPIV),
-            held(PIVOT_TILES // 2, 2 * TILE, 2 * TILE),
-            pltpu.VMEM((8, width, TILE), jnp.float32),
-            pltpu.VMEM((3 * width, NPIV), jnp.float32),
-            held(3 * width, NPIV),
+            pltpu.VMEM((2 * width, NPIV), jnp.float32),
+            held(2 * width, NPIV),
         ],
         compiler_params=pltpu.CompilerParams(vmem_limit_bytes=50 * 2**20),
         cost_estimate=pl.CostEstimate(
@@ -338,10 +357,11 @@
         front.reshape(3, 4, TILE, width),
         child.reshape(2, 4, TILE, 4 * TILE),
         received.reshape(2, 2, 4, TILE, TILE),
-        across,
         beneath,
         upper,
-        inverse,
+        wide,
+        column,
+        pivot,
     )
     return out.reshape(front.shape)
 
@@ -485,9 +505,9 @@
         across, parts = lax.optimization_barrier((across, parts))
 
     with jax.named_scope("factor"):
-        upper, inverse = factor(row_index, parts)
+        factors = factor(meta, parts, across)
     with jax.named_scope("finish"):
-        return finish(meta, front_init, own, received, across, beneath, upper, inverse)
+        return finish(meta, front_init, own, received, beneath, *factors)
 
 
 def solution(mesh):

time: 187 us -> 192 us (1.027)
  local copies, waits for them, and re-layouts: 8.29 us -> 16.2 us
  waiting for transfers between devices: 49.7 us -> 44.4 us
    unnamed x6 -> x24, local copies, waits for them, and re-layouts: 4.25 us -> 12.2 us
    all_gather x1, waiting for transfers between devices: 5.35 us -> 0.01 us  [body(): beneath = lax.all_gather(turned, 'col')]
    pallas_call x1, Pallas kernels: 38.3 us -> 43.1 us  [factor(): pl.pallas_call(factor_kernel, out_shape=(halves(NPIV, NPIV), halves(PIVOT...]
    pallas_call x1, Pallas kernels: 25.3 us -> 21.4 us  [finish(): pl.pallas_call(finish_kernel, grid=(2,), out_shape=jax.ShapeDtypeStruct((...]
  transfers between devices with their start and end apart: 19 -> 19, of which waited for: 14 -> 13; matrix products, arithmetic and copies ran while one was open for 3% -> 3% of each run, Pallas kernels for 21% -> 23%
where the time goes in v6:
time: 192 us; the launch traced here: 189 us
  Pallas kernels  65.1 us (34%)
  waiting for transfers between devices  44.4 us (23%)
  starting transfers between devices  43.7 us (23%)
  local copies, waits for them, and re-layouts  16.2 us (8%)
  between operations  14.8 us (8%)
  other arithmetic  4.38 us (2%)
    pallas_call x1, Pallas kernels, factor(): pl.pallas_call(factor_kernel, out_shape=(halves(NPIV, NPIV), halves(PIVOT...  43.1 us
    pallas_call x1, Pallas kernels, finish(): pl.pallas_call(finish_kernel, grid=(2,), out_shape=jax.ShapeDtypeStruct((...  21.4 us
    ppermute x2, waiting for transfers between devices, body(): beside = [lax.ppermute(pivot_columns, ALL, route) for route in routes]  19.4 us
    ppermute x3, starting transfers between devices, ring_gather(): ahead = lax.ppermute(ahead, 'row', down)  12.7 us
    unnamed x24, local copies, waits for them, and re-layouts  12.2 us
    ppermute x3, starting transfers between devices, body(): came = lax.ppermute(mine, 'row', [(i, i ^ bit) for i in range(8)])  10.6 us
    ppermute x3, waiting for transfers between devices, body(): came = lax.ppermute(mine, 'row', [(i, i ^ bit) for i in range(8)])  8.66 us
    ppermute x1, starting transfers between devices, body(): lax.ppermute(lower_half, ALL, [(at(p, i, c), at(p, i, c + 8)) for p, i, c...  5.1 us
  transfers between devices with their start and end apart: 19, of which 13 were waited for; matrix products, arithmetic and copies ran while one was open for 3% of the time, Pallas kernels for 23%

profile of v6, /device:TPU:2, one launch (start us, length us, event | category | flops | bytes accessed | tf_op | source)
XLA Modules:
  0.0 188.6 jit_solution(16933539463245194200)
XLA Ops:
  6.5 0.8 reshape.94
  7.3 0.6 constant_dynamic-slice_fusion
  9.1 0.9 fusion.2
  10.0 5.1 %collective-permute-start.1 = (f32[64,128]{1,0:T(8,128)S(1)}, f32[64,128]{1,0:T(8,128)S(1)}, u32[]{:S(2)}, u32[]{:S(2)}) collective-permute-start(f32[64,128]{1,0:T(8,128)S(1)} %get-tuple-element.62), channel_id=1, source_target_pairs={{0,8},{1,9},{2,10},{3,11},{4,12},{5,13},{6,14},{7,15},{16,24},{17,... | collective-permute-start | bytes 98312 | tf_op jit(solution)/shard_map/pivot_block/ppermute | solution.py:455
  15.1 2.9 %collective-permute-start.2 = (f32[64,128]{1,0:T(8,128)S(1)}, f32[64,128]{1,0:T(8,128)S(1)}, u32[]{:S(2)}, u32[]{:S(2)}) collective-permute-start(f32[64,128]{1,0:T(8,128)S(1)} %get-tuple-element.62), channel_id=1, source_target_pairs={{0,136},{1,137},{2,138},{3,139},{4,140},{5,141},{6,142},{7,143},{1... | collective-permute-start | bytes 98312 | tf_op jit(solution)/shard_map/pivot_block/ppermute | solution.py:456
  18.0 3.3 %collective-permute-start = (f32[64,128]{1,0:T(8,128)S(1)}, f32[64,128]{1,0:T(8,128)S(1)}, u32[]{:S(2)}, u32[]{:S(2)}) collective-permute-start(f32[64,128]{1,0:T(8,128)S(1)} %get-tuple-element.61), channel_id=1, source_target_pairs={{0,128},{1,129},{2,130},{3,131},{4,132},{5,133},{6,134},{7,135},{1... | collective-permute-start | bytes 98312 | tf_op jit(solution)/shard_map/pivot_block/ppermute | solution.py:454
  21.3 1.6 fusion.1
  23.1 2.2 %collective-permute-done = f32[64,128]{1,0:T(8,128)S(1)} collective-permute-done((f32[64,128]{1,0:T(8,128)S(1)}, f32[64,128]{1,0:T(8,128)S(1)}, u32[]{:S(2)}, u32[]{:S(2)}) %collective-permute-start) | collective-permute-done | bytes 32800 | tf_op jit(solution)/shard_map/pivot_block/ppermute | solution.py:454
  25.3 1.5 collective-permute-start.6
  26.8 7.2 %collective-permute-start.3 = (f32[1,64,128]{2,1,0:T(8,128)S(1)}, f32[1,64,128]{2,1,0:T(8,128)S(1)}, u32[]{:S(2)}, u32[]{:S(2)}) collective-permute-start(f32[1,64,128]{2,1,0:T(8,128)S(1)} %bitcast.25), channel_id=1, source_target_pairs={{0,64},{16,80},{32,96},{48,112},{64,0},{80,16},{96,32},{112,48},{1... | collective-permute-start | bytes 98312 | tf_op jit(solution)/shard_map/pivot_gather/ppermute | solution.py:468
  34.0 1.9 %collective-permute-done.3 = f32[1,64,128]{2,1,0:T(8,128)S(1)} collective-permute-done((f32[1,64,128]{2,1,0:T(8,128)S(1)}, f32[1,64,128]{2,1,0:T(8,128)S(1)}, u32[]{:S(2)}, u32[]{:S(2)}) %collective-permute-start.3) | collective-permute-done | bytes 32800 | tf_op jit(solution)/shard_map/pivot_gather/ppermute | solution.py:468
  35.9 2.0 %collective-permute-start.4 = (f32[2,64,128]{2,1,0:T(8,128)S(1)}, f32[2,64,128]{2,1,0:T(8,128)S(1)}, u32[]{:S(2)}, u32[]{:S(2)}) collective-permute-start(f32[2,64,128]{2,1,0:T(8,128)S(1)} %pad_maximum_fusion.4), channel_id=1, source_target_pairs={{0,32},{16,48},{32,0},{48,16},{64,96},{80,112},{96,64},{112,80},{1... | collective-permute-start | bytes 196616 | tf_op jit(solution)/shard_map/pivot_gather/ppermute | solution.py:468
  37.9 3.2 %collective-permute-done.4 = f32[2,64,128]{2,1,0:T(8,128)S(1)} collective-permute-done((f32[2,64,128]{2,1,0:T(8,128)S(1)}, f32[2,64,128]{2,1,0:T(8,128)S(1)}, u32[]{:S(2)}, u32[]{:S(2)}) %collective-permute-start.4) | collective-permute-done | bytes 65568 | tf_op jit(solution)/shard_map/pivot_gather/ppermute | solution.py:468
  41.1 1.4 collective-permute-start.5
  42.5 3.6 %collective-permute-done.5 = f32[4,64,128]{2,1,0:T(8,128)S(1)} collective-permute-done((f32[4,64,128]{2,1,0:T(8,128)S(1)}, f32[4,64,128]{2,1,0:T(8,128)S(1)}, u32[]{:S(2)}, u32[]{:S(2)}) %collective-permute-start.5) | collective-permute-done | bytes 131104 | tf_op jit(solution)/shard_map/pivot_gather/ppermute | solution.py:468
  46.1 0.7 pad_maximum_fusion.1
  46.9 3.5 %collective-permute-done.6.came_ref = f32[2,1024,128]{2,1,0:T(8,128)S(1)} collective-permute-done((f32[2,1024,128]{2,1,0:T(8,128)S(1)}, f32[2,1024,128]{2,1,0:T(8,128)S(1)}, u32[]{:S(2)}, u32[]{:S(2)}) %collective-permute-start.6) | collective-permute-done | bytes 1048608 | tf_op jit(solution)/shard_map/siblings/ppermute | solution.py:463
  50.6 0.9 slice.47.front_ref
  52.3 1.0 slice_bitcast_fusion.child_ref
  53.3 0.7 assemble_pivot_rows.1.across_refs_0_
  54.0 5.9 %collective-permute-start.9 = (f32[384,128]{1,0:T(8,128)S(1)}, f32[384,128]{1,0:T(8,128)S(1)}, u32[]{:S(2)}, u32[]{:S(2)}) collective-permute-start(f32[384,128]{1,0:T(8,128)S(1)} %assemble_pivot_rows.1.across_refs_0_), channel_id=1, source_target_pairs={{0,112},{16,0},{32,16},{48,32},{64,48},{80,64},{96,80},{112,96},{1... | collective-permute-start | bytes 589832 | tf_op jit(solution)/shard_map/panel/ppermute | solution.py:386
  59.9 2.2 %collective-permute-start.11 = (f32[384,128]{1,0:T(8,128)S(1)}, f32[384,128]{1,0:T(8,128)S(1)}, u32[]{:S(2)}, u32[]{:S(2)}) collective-permute-start(f32[384,128]{1,0:T(8,128)S(1)} %assemble_pivot_rows.1.across_refs_0_), channel_id=1, source_target_pairs={{0,0},{1,16},{2,32},{3,48},{4,64},{5,80},{6,96},{7,112},{8,8},{9,2... | collective-permute-start | bytes 589832 | tf_op jit(solution)/shard_map/panel/ppermute | solution.py:498
  62.2 1.0 collective-permute-done.9.across_refs_2_
  63.1 3.7 %collective-permute-start.10 = (f32[384,128]{1,0:T(8,128)S(1)}, f32[384,128]{1,0:T(8,128)S(1)}, u32[]{:S(2)}, u32[]{:S(2)}) collective-permute-start(f32[384,128]{1,0:T(8,128)S(1)} %collective-permute-done.9.across_refs_2_), channel_id=1, source_target_pairs={{0,112},{16,0},{32,16},{48,32},{64,48},{80,64},{96,80},{112,96},{1... | collective-permute-start | bytes 589832 | tf_op jit(solution)/shard_map/panel/ppermute | solution.py:386
  66.8 2.1 %collective-permute-done.7.across_refs_1_ = f32[384,128]{1,0:T(8,128)S(1)} collective-permute-done((f32[384,128]{1,0:T(8,128)S(1)}, f32[384,128]{1,0:T(8,128)S(1)}, u32[]{:S(2)}, u32[]{:S(2)}) %collective-permute-start.7) | collective-permute-done | bytes 196640 | tf_op jit(solution)/shard_map/panel/ppermute | solution.py:385
  69.0 12.9 %collective-permute-done.11 = f32[384,128]{1,0:T(8,128)S(1)} collective-permute-done((f32[384,128]{1,0:T(8,128)S(1)}, f32[384,128]{1,0:T(8,128)S(1)}, u32[]{:S(2)}, u32[]{:S(2)}) %collective-permute-start.11) | collective-permute-done | bytes 196640 | tf_op jit(solution)/shard_map/panel/ppermute | solution.py:498
  82.1 3.1 %collective-permute-start.13 = (f32[384,128]{1,0:T(8,128)S(1)}, f32[384,128]{1,0:T(8,128)S(1)}, u32[]{:S(2)}, u32[]{:S(2)}) collective-permute-start(f32[384,128]{1,0:T(8,128)S(1)} %collective-permute-done.10.across_refs_4_), channel_id=1, source_target_pairs={{0,112},{16,0},{32,16},{48,32},{64,48},{80,64},{96,80},{112,96},{1... | collective-permute-start | bytes 589832 | tf_op jit(solution)/shard_map/panel/ppermute | solution.py:386
  85.1 6.5 %collective-permute-done.14 = f32[384,128]{1,0:T(8,128)S(1)} collective-permute-done((f32[384,128]{1,0:T(8,128)S(1)}, f32[384,128]{1,0:T(8,128)S(1)}, u32[]{:S(2)}, u32[]{:S(2)}) %collective-permute-start.14) | collective-permute-done | bytes 196640 | tf_op jit(solution)/shard_map/panel/ppermute | solution.py:498
  91.7 1.6 collective-permute-done.13.across_refs_6_
  93.3 0.8 maximum_select_fusion
  94.1 4.9 %collective-permute-start.15 = (f32[192,128]{1,0:T(8,128)S(1)}, f32[192,128]{1,0:T(8,128)S(1)}, u32[]{:S(2)}, u32[]{:S(2)}) collective-permute-start(f32[192,128]{1,0:T(8,128)S(1)} %slice.50), channel_id=1, source_target_pairs={{0,16},{16,32},{32,48},{48,64},{64,80},{80,96},{96,112},{112,0},{1... | collective-permute-start | bytes 294920 | tf_op jit(solution)/shard_map/panel/ppermute | solution.py:392
  99.0 0.3 collective-permute-start.16
  99.3 1.9 %collective-permute-done.15 = f32[192,128]{1,0:T(8,128)S(1)} collective-permute-done((f32[192,128]{1,0:T(8,128)S(1)}, f32[192,128]{1,0:T(8,128)S(1)}, u32[]{:S(2)}, u32[]{:S(2)}) %collective-permute-start.15) | collective-permute-done | bytes 98336 | tf_op jit(solution)/shard_map/panel/ppermute | solution.py:392
  101.2 3.0 %collective-permute-done.16 = f32[192,128]{1,0:T(8,128)S(1)} collective-permute-done((f32[192,128]{1,0:T(8,128)S(1)}, f32[192,128]{1,0:T(8,128)S(1)}, u32[]{:S(2)}, u32[]{:S(2)}) %collective-permute-start.16) | collective-permute-done | bytes 98336 | tf_op jit(solution)/shard_map/panel/ppermute | solution.py:392
  104.3 0.8 all-gather.6.cloned.1.call-done
  105.1 2.2 %copy-done = f32[128,64,128]{2,1,0:T(8,128)S(1)} copy-done((f32[128,64,128]{2,1,0:T(8,128)S(1)}, f32[128,64,128]{2,1,0:T(8,128)}, u32[]{:S(2)}) %copy-start) | copy-done | bytes 4194328
  107.3 43.1 %factor_pivots.1 = (bf16[1024,1024]{1,0:T(8,128)(2,1)S(1)}, bf16[1024,1024]{1,0:T(8,128)(2,1)S(1)}, bf16[4,256,256]{2,1,0:T(8,128)(2,1)S(1)}, bf16[4,256,256]{2,...) custom-call(s32[24]{0:T(128)S(1)} %concatenate.31.meta_ref, ...), custom_call_target="tpu_custom_call" | custom-call | flops 49999998976 | bytes 9437184 | tf_op jit(solution)/shard_map/factor/factor_pivots/pallas_call | solution.py:223
  150.4 1.4 copy-done.1
  151.8 1.4 copy-done.2
  153.1 0.9 copy-done.3
  154.0 0.8 copy-done.5
  154.8 0.8 copy-done.7
  155.6 0.7 copy-done.9
  156.3 1.1 copy-done.4
  157.4 1.0 copy-done.6
  158.4 1.0 copy-done.8
  159.5 0.9 copy-done.10
  160.4 21.4 %solve_and_update.1 = f32[3,4,128,384]{3,2,1,0:T(8,128)} custom-call(s32[24]{0:T(128)S(1)} %concatenate.31.meta_ref, f32[3,4,128,384]{3,2,1,0:T(8,128)} %bitcast.31, f32[2,4,128,512]{3,2,1,0:T(8,128)} %bitcast.24, f32[2,2,4,128,128]{4,3,2,1,0:T(8,128)S(1)} %bitcast.20, f32[16,2,384,128]{3,2,1,0:T(8,128)} %all-gather.4.cloned.1.call-done.beneath_ref, ...), custom_call_target="tpu_custom_call" | custom-call | flops 15000000512 | bytes 25165824 | tf_op jit(solution)/shard_map/finish/solve_and_update/pallas_call | solution.py:330
  (45 shorter events, 1.4 us)
Async XLA Ops:
  6.5 98.6 %all-gather.6.cloned.1.call-start = ((), (), s32[]{:S(2)}) async-start(), calls=%async_computation.1 | async-start | bytes 4456448 | tf_op jit(solution)/shard_map/pivot_gather/all_gather | solution.py:471
  10.0 13.1 %collective-permute-start.1 = (f32[64,128]{1,0:T(8,128)S(1)}, f32[64,128]{1,0:T(8,128)S(1)}, u32[]{:S(2)}, u32[]{:S(2)}) collective-permute-start(f32[64,128]{1,0:T(8,128)S(1)} %get-tuple-element.62), channel_id=1, source_target_pairs={{0,8},{1,9},{2,10},{3,11},{4,12},{5,13},{6,14},{7,15},{16,24},{17,... | collective-permute-start | bytes 98312 | tf_op jit(solution)/shard_map/pivot_block/ppermute | solution.py:455
  15.1 8.0 %collective-permute-start.2 = (f32[64,128]{1,0:T(8,128)S(1)}, f32[64,128]{1,0:T(8,128)S(1)}, u32[]{:S(2)}, u32[]{:S(2)}) collective-permute-start(f32[64,128]{1,0:T(8,128)S(1)} %get-tuple-element.62), channel_id=1, source_target_pairs={{0,136},{1,137},{2,138},{3,139},{4,140},{5,141},{6,142},{7,143},{1... | collective-permute-start | bytes 98312 | tf_op jit(solution)/shard_map/pivot_block/ppermute | solution.py:456
  18.0 7.3 %collective-permute-start = (f32[64,128]{1,0:T(8,128)S(1)}, f32[64,128]{1,0:T(8,128)S(1)}, u32[]{:S(2)}, u32[]{:S(2)}) collective-permute-start(f32[64,128]{1,0:T(8,128)S(1)} %get-tuple-element.61), channel_id=1, source_target_pairs={{0,128},{1,129},{2,130},{3,131},{4,132},{5,133},{6,134},{7,135},{1... | collective-permute-start | bytes 98312 | tf_op jit(solution)/shard_map/pivot_block/ppermute | solution.py:454
  23.0 27.5 %copy-start.11 = (s32[2,64]{1,0:T(2,128)S(1)}, s32[2,64]{1,0:T(2,128)}, u32[]{:S(2)}) copy-start(s32[2,64]{1,0:T(2,128)} %param.5) | copy-start | bytes 1540
  25.3 25.1 %collective-permute-start.6 = (f32[2,1024,128]{2,1,0:T(8,128)S(1)}, f32[2,1024,128]{2,1,0:T(8,128)S(1)}, u32[]{:S(2)}, u32[]{:S(2)}) collective-permute-start(f32[2,1024,128]{2,1,0:T(8,128)S(1)} %pad_maximum_fusion), channel_id=1, source_target_pairs={{0,128},{128,0},{1,129},{129,1},{2,130},{130,2},{3,131},{131,3},{4... | collective-permute-start | bytes 3145736 | tf_op jit(solution)/shard_map/siblings/ppermute | solution.py:463
  26.8 9.1 %collective-permute-start.3 = (f32[1,64,128]{2,1,0:T(8,128)S(1)}, f32[1,64,128]{2,1,0:T(8,128)S(1)}, u32[]{:S(2)}, u32[]{:S(2)}) collective-permute-start(f32[1,64,128]{2,1,0:T(8,128)S(1)} %bitcast.25), channel_id=1, source_target_pairs={{0,64},{16,80},{32,96},{48,112},{64,0},{80,16},{96,32},{112,48},{1... | collective-permute-start | bytes 98312 | tf_op jit(solution)/shard_map/pivot_gather/ppermute | solution.py:468
  35.9 5.2 %collective-permute-start.4 = (f32[2,64,128]{2,1,0:T(8,128)S(1)}, f32[2,64,128]{2,1,0:T(8,128)S(1)}, u32[]{:S(2)}, u32[]{:S(2)}) collective-permute-start(f32[2,64,128]{2,1,0:T(8,128)S(1)} %pad_maximum_fusion.4), channel_id=1, source_target_pairs={{0,32},{16,48},{32,0},{48,16},{64,96},{80,112},{96,64},{112,80},{1... | collective-permute-start | bytes 196616 | tf_op jit(solution)/shard_map/pivot_gather/ppermute | solution.py:468
  41.1 5.1 %collective-permute-start.5 = (f32[4,64,128]{2,1,0:T(8,128)S(1)}, f32[4,64,128]{2,1,0:T(8,128)S(1)}, u32[]{:S(2)}, u32[]{:S(2)}) collective-permute-start(f32[4,64,128]{2,1,0:T(8,128)S(1)} %pad_maximum_fusion.3), channel_id=1, source_target_pairs={{0,16},{16,0},{32,48},{48,32},{64,80},{80,64},{96,112},{112,96},{1... | collective-permute-start | bytes 393224 | tf_op jit(solution)/shard_map/pivot_gather/ppermute | solution.py:468
  50.4 105.9 %all-gather.4.cloned.1.call-start = ((), (), s32[]{:S(2)}) async-start(), calls=%async_computation | async-start | bytes 6684672 | tf_op jit(solution)/shard_map/panel/all_gather | solution.py:504
  54.0 9.1 %collective-permute-start.9 = (f32[384,128]{1,0:T(8,128)S(1)}, f32[384,128]{1,0:T(8,128)S(1)}, u32[]{:S(2)}, u32[]{:S(2)}) collective-permute-start(f32[384,128]{1,0:T(8,128)S(1)} %assemble_pivot_rows.1.across_refs_0_), channel_id=1, source_target_pairs={{0,112},{16,0},{32,16},{48,32},{64,48},{80,64},{96,80},{112,96},{1... | collective-permute-start | bytes 589832 | tf_op jit(solution)/shard_map/panel/ppermute | solution.py:386
  59.9 9.0 %collective-permute-start.7 = (f32[384,128]{1,0:T(8,128)S(1)}, f32[384,128]{1,0:T(8,128)S(1)}, u32[]{:S(2)}, u32[]{:S(2)}) collective-permute-start(f32[384,128]{1,0:T(8,128)S(1)} %assemble_pivot_rows.1.across_refs_0_), channel_id=1, source_target_pairs={{0,16},{16,32},{32,48},{48,64},{64,80},{80,96},{96,112},{112,0},{1... | collective-permute-start | bytes 589832 | tf_op jit(solution)/shard_map/panel/ppermute | solution.py:385
  59.9 21.9 %collective-permute-start.11 = (f32[384,128]{1,0:T(8,128)S(1)}, f32[384,128]{1,0:T(8,128)S(1)}, u32[]{:S(2)}, u32[]{:S(2)}) collective-permute-start(f32[384,128]{1,0:T(8,128)S(1)} %assemble_pivot_rows.1.across_refs_0_), channel_id=1, source_target_pairs={{0,0},{1,16},{2,32},{3,48},{4,64},{5,80},{6,96},{7,112},{8,8},{9,2... | collective-permute-start | bytes 589832 | tf_op jit(solution)/shard_map/panel/ppermute | solution.py:498
  63.1 18.8 %collective-permute-start.10 = (f32[384,128]{1,0:T(8,128)S(1)}, f32[384,128]{1,0:T(8,128)S(1)}, u32[]{:S(2)}, u32[]{:S(2)}) collective-permute-start(f32[384,128]{1,0:T(8,128)S(1)} %collective-permute-done.9.across_refs_2_), channel_id=1, source_target_pairs={{0,112},{16,0},{32,16},{48,32},{64,48},{80,64},{96,80},{112,96},{1... | collective-permute-start | bytes 589832 | tf_op jit(solution)/shard_map/panel/ppermute | solution.py:386
  69.0 12.9 %collective-permute-start.8 = (f32[384,128]{1,0:T(8,128)S(1)}, f32[384,128]{1,0:T(8,128)S(1)}, u32[]{:S(2)}, u32[]{:S(2)}) collective-permute-start(f32[384,128]{1,0:T(8,128)S(1)} %collective-permute-done.7.across_refs_1_), channel_id=1, source_target_pairs={{0,16},{16,32},{32,48},{48,64},{64,80},{80,96},{96,112},{112,0},{1... | collective-permute-start | bytes 589832 | tf_op jit(solution)/shard_map/panel/ppermute | solution.py:385
  69.0 22.7 %collective-permute-start.14 = (f32[384,128]{1,0:T(8,128)S(1)}, f32[384,128]{1,0:T(8,128)S(1)}, u32[]{:S(2)}, u32[]{:S(2)}) collective-permute-start(f32[384,128]{1,0:T(8,128)S(1)} %assemble_pivot_rows.1.across_refs_0_), channel_id=1, source_target_pairs={{0,128},{1,144},{2,160},{3,176},{4,192},{5,208},{6,224},{7,240},{8... | collective-permute-start | bytes 589832 | tf_op jit(solution)/shard_map/panel/ppermute | solution.py:498
  81.9 9.8 %collective-permute-start.12 = (f32[384,128]{1,0:T(8,128)S(1)}, f32[384,128]{1,0:T(8,128)S(1)}, u32[]{:S(2)}, u32[]{:S(2)}) collective-permute-start(f32[384,128]{1,0:T(8,128)S(1)} %collective-permute-done.8.across_refs_3_), channel_id=1, source_target_pairs={{0,16},{16,32},{32,48},{48,64},{64,80},{80,96},{96,112},{112,0},{1... | collective-permute-start | bytes 589832 | tf_op jit(solution)/shard_map/panel/ppermute | solution.py:385
  82.1 11.2 %collective-permute-start.13 = (f32[384,128]{1,0:T(8,128)S(1)}, f32[384,128]{1,0:T(8,128)S(1)}, u32[]{:S(2)}, u32[]{:S(2)}) collective-permute-start(f32[384,128]{1,0:T(8,128)S(1)} %collective-permute-done.10.across_refs_4_), channel_id=1, source_target_pairs={{0,112},{16,0},{32,16},{48,32},{64,48},{80,64},{96,80},{112,96},{1... | collective-permute-start | bytes 589832 | tf_op jit(solution)/shard_map/panel/ppermute | solution.py:386
  94.1 7.2 %collective-permute-start.15 = (f32[192,128]{1,0:T(8,128)S(1)}, f32[192,128]{1,0:T(8,128)S(1)}, u32[]{:S(2)}, u32[]{:S(2)}) collective-permute-start(f32[192,128]{1,0:T(8,128)S(1)} %slice.50), channel_id=1, source_target_pairs={{0,16},{16,32},{32,48},{48,64},{64,80},{80,96},{96,112},{112,0},{1... | collective-permute-start | bytes 294920 | tf_op jit(solution)/shard_map/panel/ppermute | solution.py:392
  99.0 5.2 %collective-permute-start.16 = (f32[192,128]{1,0:T(8,128)S(1)}, f32[192,128]{1,0:T(8,128)S(1)}, u32[]{:S(2)}, u32[]{:S(2)}) collective-permute-start(f32[192,128]{1,0:T(8,128)S(1)} %slice.51), channel_id=1, source_target_pairs={{0,112},{16,0},{32,16},{48,32},{64,48},{80,64},{96,80},{112,96},{1... | collective-permute-start | bytes 294920 | tf_op jit(solution)/shard_map/panel/ppermute | solution.py:392
  105.1 2.2 %copy-start = (f32[128,64,128]{2,1,0:T(8,128)S(1)}, f32[128,64,128]{2,1,0:T(8,128)}, u32[]{:S(2)}) copy-start(f32[128,64,128]{2,1,0:T(8,128)} %all-gather.6.cloned.1.call-done) | copy-start | bytes 12582916
  150.4 1.4 copy-start.1
  151.8 1.4 copy-start.2
  153.1 0.9 copy-start.3
  154.0 0.8 copy-start.5
  154.8 0.8 copy-start.7
  155.6 0.7 copy-start.9
  156.3 1.1 copy-start.4
  157.4 1.0 copy-start.6
  158.4 1.0 copy-start.8
  159.5 0.9 copy-start.10
Sparse Core Ops, SparseCore 0:
  50.5 54.5 all-gather.5
  106.9 45.9 all-gather.3

commit v7 on v6

--- a/solution.py
+++ b/solution.py
@@ -236,7 +236,7 @@
             pltpu.VMEM((8, width, TILE), jnp.float32),
             pltpu.VMEM((width, NPIV), jnp.float32),
         ],
-        compiler_params=pltpu.CompilerParams(vmem_limit_bytes=36 * 2**20),
+        compiler_params=pltpu.CompilerParams(vmem_limit_bytes=24 * 2**20),
         cost_estimate=pl.CostEstimate(
             flops=FACTOR_FLOPS, bytes_accessed=9 * 2**20, transcendentals=0
         ),
@@ -347,7 +347,7 @@
             pltpu.VMEM((2 * width, NPIV), jnp.float32),
             held(2 * width, NPIV),
         ],
-        compiler_params=pltpu.CompilerParams(vmem_limit_bytes=50 * 2**20),
+        compiler_params=pltpu.CompilerParams(vmem_limit_bytes=36 * 2**20),
         cost_estimate=pl.CostEstimate(
             flops=15 * 10**9, bytes_accessed=24 * 2**20, transcendentals=0
         ),

time: 192 us -> 203 us (1.057)
  the two profiles are of different devices: /device:TPU:2 before, /device:TPU:0 now
where the time goes in v7:
time: 203 us
  Pallas kernels  63.8 us (31%)
  waiting for transfers between devices  48.8 us (24%)
  starting transfers between devices  39.4 us (19%)
  local copies, waits for them, and re-layouts  30.3 us (15%)
  between operations  14.9 us (7%)
  other arithmetic  5.37 us (3%)
    pallas_call x1, Pallas kernels, factor(): pl.pallas_call(factor_kernel, out_shape=(halves(NPIV, NPIV), halves(PIVOT...  43.5 us
    ppermute x3, waiting for transfers between devices, ring_gather(): behind = lax.ppermute(behind, 'row', up)  27.8 us
    unnamed x56, local copies, waits for them, and re-layouts  26.4 us
    pallas_call x1, Pallas kernels, finish(): pl.pallas_call(finish_kernel, grid=(2,), out_shape=jax.ShapeDtypeStruct((...  19.6 us
    ppermute x3, starting transfers between devices, ring_gather(): ahead = lax.ppermute(ahead, 'row', down)  12.9 us
    ppermute x3, waiting for transfers between devices, body(): came = lax.ppermute(mine, 'row', [(i, i ^ bit) for i in range(8)])  10.3 us
    ppermute x3, starting transfers between devices, body(): came = lax.ppermute(mine, 'row', [(i, i ^ bit) for i in range(8)])  9.7 us
  transfers between devices with their start and end apart: 19, of which 12 were waited for; matrix products, arithmetic and copies ran while one was open for 3% of the time, Pallas kernels for 22%

profile of v7, /device:TPU:0, one launch (start us, length us, event | category | flops | bytes accessed | tf_op | source)
XLA Modules:
  0.0 202.6 jit_solution(3484426445006072305)
XLA Ops:
  9.2 0.9 fusion.2
  10.1 3.4 %collective-permute-start.1 = (f32[64,128]{1,0:T(8,128)S(1)}, f32[64,128]{1,0:T(8,128)S(1)}, u32[]{:S(2)}, u32[]{:S(2)}) collective-permute-start(f32[64,128]{1,0:T(8,128)S(1)} %get-tuple-element.62), channel_id=1, source_target_pairs={{0,8},{1,9},{2,10},{3,11},{4,12},{5,13},{6,14},{7,15},{16,24},{17,... | collective-permute-start | bytes 98312 | tf_op jit(solution)/shard_map/pivot_block/ppermute | solution.py:455
  13.5 3.8 %collective-permute-start.2 = (f32[64,128]{1,0:T(8,128)S(1)}, f32[64,128]{1,0:T(8,128)S(1)}, u32[]{:S(2)}, u32[]{:S(2)}) collective-permute-start(f32[64,128]{1,0:T(8,128)S(1)} %get-tuple-element.62), channel_id=1, source_target_pairs={{0,136},{1,137},{2,138},{3,139},{4,140},{5,141},{6,142},{7,143},{1... | collective-permute-start | bytes 98312 | tf_op jit(solution)/shard_map/pivot_block/ppermute | solution.py:456
  17.3 2.5 %collective-permute-start = (f32[64,128]{1,0:T(8,128)S(1)}, f32[64,128]{1,0:T(8,128)S(1)}, u32[]{:S(2)}, u32[]{:S(2)}) collective-permute-start(f32[64,128]{1,0:T(8,128)S(1)} %get-tuple-element.61), channel_id=1, source_target_pairs={{0,128},{1,129},{2,130},{3,131},{4,132},{5,133},{6,134},{7,135},{1... | collective-permute-start | bytes 98312 | tf_op jit(solution)/shard_map/pivot_block/ppermute | solution.py:454
  19.7 1.6 fusion.1
  21.4 1.0 pad_maximum_fusion
  22.5 2.1 %collective-permute-done = f32[64,128]{1,0:T(8,128)S(1)} collective-permute-done((f32[64,128]{1,0:T(8,128)S(1)}, f32[64,128]{1,0:T(8,128)S(1)}, u32[]{:S(2)}, u32[]{:S(2)}) %collective-permute-start) | collective-permute-done | bytes 32800 | tf_op jit(solution)/shard_map/pivot_block/ppermute | solution.py:454
  24.6 1.0 collective-permute-start.6
  25.5 7.2 %collective-permute-start.3 = (f32[1,64,128]{2,1,0:T(8,128)S(1)}, f32[1,64,128]{2,1,0:T(8,128)S(1)}, u32[]{:S(2)}, u32[]{:S(2)}) collective-permute-start(f32[1,64,128]{2,1,0:T(8,128)S(1)} %bitcast.26), channel_id=1, source_target_pairs={{0,64},{16,80},{32,96},{48,112},{64,0},{80,16},{96,32},{112,48},{1... | collective-permute-start | bytes 98312 | tf_op jit(solution)/shard_map/pivot_gather/ppermute | solution.py:468
  32.7 1.9 collective-permute-done.3
  34.6 2.0 collective-permute-start.4
  36.6 3.9 %collective-permute-done.4 = f32[2,64,128]{2,1,0:T(8,128)S(1)} collective-permute-done((f32[2,64,128]{2,1,0:T(8,128)S(1)}, f32[2,64,128]{2,1,0:T(8,128)S(1)}, u32[]{:S(2)}, u32[]{:S(2)}) %collective-permute-start.4) | collective-permute-done | bytes 65568 | tf_op jit(solution)/shard_map/pivot_gather/ppermute | solution.py:468
  41.0 4.6 %collective-permute-done.5 = f32[4,64,128]{2,1,0:T(8,128)S(1)} collective-permute-done((f32[4,64,128]{2,1,0:T(8,128)S(1)}, f32[4,64,128]{2,1,0:T(8,128)S(1)}, u32[]{:S(2)}, u32[]{:S(2)}) %collective-permute-start.5) | collective-permute-done | bytes 131104 | tf_op jit(solution)/shard_map/pivot_gather/ppermute | solution.py:468
  46.3 3.6 %collective-permute-done.6.came_ref = f32[2,1024,128]{2,1,0:T(8,128)S(1)} collective-permute-done((f32[2,1024,128]{2,1,0:T(8,128)}, f32[2,1024,128]{2,1,0:T(8,128)S(1)}, u32[]{:S(2)}, u32[]{:S(2)}) %collective-permute-start.6) | collective-permute-done | bytes 1048608 | tf_op jit(solution)/shard_map/siblings/ppermute | solution.py:463
  50.0 0.9 slice.47.front_ref
  52.5 5.9 %collective-permute-start.9 = (f32[384,128]{1,0:T(8,128)S(1)}, f32[384,128]{1,0:T(8,128)S(1)}, u32[]{:S(2)}, u32[]{:S(2)}) collective-permute-start(f32[384,128]{1,0:T(8,128)S(1)} %assemble_pivot_rows.1.across_refs_0_), channel_id=1, source_target_pairs={{0,112},{16,0},{32,16},{48,32},{64,48},{80,64},{96,80},{112,96},{1... | collective-permute-start | bytes 589832 | tf_op jit(solution)/shard_map/panel/ppermute | solution.py:386
  59.1 2.5 %collective-permute-done.9.across_refs_2_ = f32[384,128]{1,0:T(8,128)S(1)} collective-permute-done((f32[384,128]{1,0:T(8,128)S(1)}, f32[384,128]{1,0:T(8,128)S(1)}, u32[]{:S(2)}, u32[]{:S(2)}) %collective-permute-start.9) | collective-permute-done | bytes 196640 | tf_op jit(solution)/shard_map/panel/ppermute | solution.py:386
  61.7 3.7 %collective-permute-start.10 = (f32[384,128]{1,0:T(8,128)S(1)}, f32[384,128]{1,0:T(8,128)S(1)}, u32[]{:S(2)}, u32[]{:S(2)}) collective-permute-start(f32[384,128]{1,0:T(8,128)S(1)} %collective-permute-done.9.across_refs_2_), channel_id=1, source_target_pairs={{0,112},{16,0},{32,16},{48,32},{64,48},{80,64},{96,80},{112,96},{1... | collective-permute-start | bytes 589832 | tf_op jit(solution)/shard_map/panel/ppermute | solution.py:386
  66.0 13.3 %collective-permute-done.7.across_refs_1_ = f32[384,128]{1,0:T(8,128)S(1)} collective-permute-done((f32[384,128]{1,0:T(8,128)S(1)}, f32[384,128]{1,0:T(8,128)S(1)}, u32[]{:S(2)}, u32[]{:S(2)}) %collective-permute-start.7) | collective-permute-done | bytes 196640 | tf_op jit(solution)/shard_map/panel/ppermute | solution.py:385
  80.0 1.7 collective-permute-start.14
  81.7 11.1 %collective-permute-done.8.across_refs_3_ = f32[384,128]{1,0:T(8,128)S(1)} collective-permute-done((f32[384,128]{1,0:T(8,128)S(1)}, f32[384,128]{1,0:T(8,128)S(1)}, u32[]{:S(2)}, u32[]{:S(2)}) %collective-permute-start.8) | collective-permute-done | bytes 196640 | tf_op jit(solution)/shard_map/panel/ppermute | solution.py:385
  93.5 3.2 %collective-permute-start.13 = (f32[384,128]{1,0:T(8,128)S(1)}, f32[384,128]{1,0:T(8,128)}, u32[]{:S(2)}, u32[]{:S(2)}) collective-permute-start(f32[384,128]{1,0:T(8,128)S(1)} %collective-permute-done.10.across_refs_4_), channel_id=1, source_target_pairs={{0,112},{16,0},{32,16},{48,32},{64,48},{80,64},{96,80},{112,96},{1... | collective-permute-start | bytes 589832 | tf_op jit(solution)/shard_map/panel/ppermute | solution.py:386
  97.5 3.3 %collective-permute-done.12.across_refs_5_ = f32[384,128]{1,0:T(8,128)S(1)} collective-permute-done((f32[384,128]{1,0:T(8,128)S(1)}, f32[384,128]{1,0:T(8,128)S(1)}, u32[]{:S(2)}, u32[]{:S(2)}) %collective-permute-start.12) | collective-permute-done | bytes 196640 | tf_op jit(solution)/shard_map/panel/ppermute | solution.py:385
  101.0 0.8 maximum_select_fusion
  101.9 0.9 slice.51
  102.8 3.8 %collective-permute-start.16 = (f32[192,128]{1,0:T(8,128)S(1)}, f32[192,128]{1,0:T(8,128)S(1)}, u32[]{:S(2)}, u32[]{:S(2)}) collective-permute-start(f32[192,128]{1,0:T(8,128)S(1)} %slice.51), channel_id=1, source_target_pairs={{0,112},{16,0},{32,16},{48,32},{64,48},{80,64},{96,80},{112,96},{1... | collective-permute-start | bytes 294920 | tf_op jit(solution)/shard_map/panel/ppermute | solution.py:392
  106.6 1.7 collective-permute-done.15
  108.9 0.9 copy-done.2
  109.8 2.2 %copy-done.4 = f32[128,64,128]{2,1,0:T(8,128)S(1)} copy-done((f32[128,64,128]{2,1,0:T(8,128)S(1)}, f32[128,64,128]{2,1,0:T(8,128)}, u32[]{:S(2)}) %copy-start.4) | copy-done | bytes 4194328
  112.0 0.9 copy-done.6
  113.0 0.9 copy-done.8
  113.9 0.9 copy-done.10
  114.8 0.9 copy-done.12
  115.7 43.5 %factor_pivots.1 = (bf16[1024,1024]{1,0:T(8,128)(2,1)S(1)}, bf16[1024,1024]{1,0:T(8,128)(2,1)S(1)}, bf16[4,256,256]{2,1,0:T(8,128)(2,1)S(1)}, bf16[4,256,256]{2,...) custom-call(s32[24]{0:T(128)S(1)} %concatenate.31.meta_ref, ...), custom_call_target="tpu_custom_call" | custom-call | flops 49999998976 | bytes 9437184 | tf_op jit(solution)/shard_map/factor/factor_pivots/pallas_call | solution.py:223
  159.3 1.3 copy-done.13
  160.6 1.4 copy-done.15
  162.0 0.9 copy-done.17
  162.9 0.9 copy-done.19
  164.6 0.8 copy-done.23
  166.0 1.7 copy-done.3
  167.7 1.6 copy-done.14
  169.3 1.6 copy-done.16
  170.9 1.1 copy-done.18
  172.0 1.1 copy-done.20
  173.1 1.0 copy-done.22
  174.2 1.0 copy-done.24
  175.2 0.9 copy-done.26
  176.1 19.6 %solve_and_update.1 = f32[3,4,128,384]{3,2,1,0:T(8,128)} custom-call(s32[24]{0:T(128)S(1)} %concatenate.31.meta_ref, f32[3,4,128,384]{3,2,1,0:T(8,128)S(1)} %bitcast.24, f32[2,4,128,512]{3,2,1,0:T(8,128)S(1)} %bitcast.22, f32[2,2,4,128,128]{4,3,2,1,0:T(8,128)S(1)} %bitcast.23, f32[16,2,384,128]{3,2,1,0:T(8,128)} %all-gather.4.cloned.1.call-done.beneath_ref, ...), custom_call_target="tpu_custom_call" | custom-call | flops 15000000512 | bytes 25165824 | tf_op jit(solution)/shard_map/finish/solve_and_update/pallas_call | solution.py:330
  (77 shorter events, 10.1 us)
Async XLA Ops:
  6.5 102.4 %all-gather.6.cloned.1.call-start = ((), (), s32[]{:S(2)}) async-start(), calls=%async_computation.1 | async-start | bytes 4456448 | tf_op jit(solution)/shard_map/pivot_gather/all_gather | solution.py:471
  10.1 12.3 %collective-permute-start.1 = (f32[64,128]{1,0:T(8,128)S(1)}, f32[64,128]{1,0:T(8,128)S(1)}, u32[]{:S(2)}, u32[]{:S(2)}) collective-permute-start(f32[64,128]{1,0:T(8,128)S(1)} %get-tuple-element.62), channel_id=1, source_target_pairs={{0,8},{1,9},{2,10},{3,11},{4,12},{5,13},{6,14},{7,15},{16,24},{17,... | collective-permute-start | bytes 98312 | tf_op jit(solution)/shard_map/pivot_block/ppermute | solution.py:455
  13.5 9.0 %collective-permute-start.2 = (f32[64,128]{1,0:T(8,128)S(1)}, f32[64,128]{1,0:T(8,128)S(1)}, u32[]{:S(2)}, u32[]{:S(2)}) collective-permute-start(f32[64,128]{1,0:T(8,128)S(1)} %get-tuple-element.62), channel_id=1, source_target_pairs={{0,136},{1,137},{2,138},{3,139},{4,140},{5,141},{6,142},{7,143},{1... | collective-permute-start | bytes 98312 | tf_op jit(solution)/shard_map/pivot_block/ppermute | solution.py:456
  17.3 7.3 %collective-permute-start = (f32[64,128]{1,0:T(8,128)S(1)}, f32[64,128]{1,0:T(8,128)S(1)}, u32[]{:S(2)}, u32[]{:S(2)}) collective-permute-start(f32[64,128]{1,0:T(8,128)S(1)} %get-tuple-element.61), channel_id=1, source_target_pairs={{0,128},{1,129},{2,130},{3,131},{4,132},{5,133},{6,134},{7,135},{1... | collective-permute-start | bytes 98312 | tf_op jit(solution)/shard_map/pivot_block/ppermute | solution.py:454
  21.4 28.6 %copy-start.27 = (s32[2,64]{1,0:T(2,128)S(1)}, s32[2,64]{1,0:T(2,128)}, u32[]{:S(2)}) copy-start(s32[2,64]{1,0:T(2,128)} %param.5) | copy-start | bytes 1540
  21.4 30.4 %copy-start = (f32[1,1024,512]{2,1,0:T(8,128)S(1)}, f32[1,1024,512]{2,1,0:T(8,128)}, u32[]{:S(2)}) copy-start(f32[1,1024,512]{2,1,0:T(8,128)} %param.4) | copy-start | bytes 6291460
  24.6 25.3 %collective-permute-start.6 = (f32[2,1024,128]{2,1,0:T(8,128)}, f32[2,1024,128]{2,1,0:T(8,128)S(1)}, u32[]{:S(2)}, u32[]{:S(2)}) collective-permute-start(f32[2,1024,128]{2,1,0:T(8,128)} %pad_maximum_fusion), channel_id=1, source_target_pairs={{0,128},{128,0},{1,129},{129,1},{2,130},{130,2},{3,131},{131,3},{4... | collective-permute-start | bytes 3145736 | tf_op jit(solution)/shard_map/siblings/ppermute | solution.py:463
  25.5 9.1 %collective-permute-start.3 = (f32[1,64,128]{2,1,0:T(8,128)S(1)}, f32[1,64,128]{2,1,0:T(8,128)S(1)}, u32[]{:S(2)}, u32[]{:S(2)}) collective-permute-start(f32[1,64,128]{2,1,0:T(8,128)S(1)} %bitcast.26), channel_id=1, source_target_pairs={{0,64},{16,80},{32,96},{48,112},{64,0},{80,16},{96,32},{112,48},{1... | collective-permute-start | bytes 98312 | tf_op jit(solution)/shard_map/pivot_gather/ppermute | solution.py:468
  34.6 5.9 %collective-permute-start.4 = (f32[2,64,128]{2,1,0:T(8,128)S(1)}, f32[2,64,128]{2,1,0:T(8,128)S(1)}, u32[]{:S(2)}, u32[]{:S(2)}) collective-permute-start(f32[2,64,128]{2,1,0:T(8,128)S(1)} %pad_maximum_fusion.4), channel_id=1, source_target_pairs={{0,32},{16,48},{32,0},{48,16},{64,96},{80,112},{96,64},{112,80},{1... | collective-permute-start | bytes 196616 | tf_op jit(solution)/shard_map/pivot_gather/ppermute | solution.py:468
  40.5 5.1 %collective-permute-start.5 = (f32[4,64,128]{2,1,0:T(8,128)S(1)}, f32[4,64,128]{2,1,0:T(8,128)S(1)}, u32[]{:S(2)}, u32[]{:S(2)}) collective-permute-start(f32[4,64,128]{2,1,0:T(8,128)S(1)} %pad_maximum_fusion.3), channel_id=1, source_target_pairs={{0,16},{16,0},{32,48},{48,32},{64,80},{80,64},{96,112},{112,96},{1... | collective-permute-start | bytes 393224 | tf_op jit(solution)/shard_map/pivot_gather/ppermute | solution.py:468
  49.9 116.1 %all-gather.4.cloned.1.call-start = ((), (), s32[]{:S(2)}) async-start(), calls=%async_computation | async-start | bytes 6684672 | tf_op jit(solution)/shard_map/panel/all_gather | solution.py:504
  52.5 9.1 %collective-permute-start.9 = (f32[384,128]{1,0:T(8,128)S(1)}, f32[384,128]{1,0:T(8,128)S(1)}, u32[]{:S(2)}, u32[]{:S(2)}) collective-permute-start(f32[384,128]{1,0:T(8,128)S(1)} %assemble_pivot_rows.1.across_refs_0_), channel_id=1, source_target_pairs={{0,112},{16,0},{32,16},{48,32},{64,48},{80,64},{96,80},{112,96},{1... | collective-permute-start | bytes 589832 | tf_op jit(solution)/shard_map/panel/ppermute | solution.py:386
  58.5 20.9 %collective-permute-start.7 = (f32[384,128]{1,0:T(8,128)S(1)}, f32[384,128]{1,0:T(8,128)S(1)}, u32[]{:S(2)}, u32[]{:S(2)}) collective-permute-start(f32[384,128]{1,0:T(8,128)S(1)} %assemble_pivot_rows.1.across_refs_0_), channel_id=1, source_target_pairs={{0,16},{16,32},{32,48},{48,64},{64,80},{80,96},{96,112},{112,0},{1... | collective-permute-start | bytes 589832 | tf_op jit(solution)/shard_map/panel/ppermute | solution.py:385
  58.5 23.3 %collective-permute-start.11 = (f32[384,128]{1,0:T(8,128)S(1)}, f32[384,128]{1,0:T(8,128)S(1)}, u32[]{:S(2)}, u32[]{:S(2)}) collective-permute-start(f32[384,128]{1,0:T(8,128)S(1)} %assemble_pivot_rows.1.across_refs_0_), channel_id=1, source_target_pairs={{0,0},{1,16},{2,32},{3,48},{4,64},{5,80},{6,96},{7,112},{8,8},{9,2... | collective-permute-start | bytes 589832 | tf_op jit(solution)/shard_map/panel/ppermute | solution.py:498
  61.7 20.1 %collective-permute-start.10 = (f32[384,128]{1,0:T(8,128)S(1)}, f32[384,128]{1,0:T(8,128)S(1)}, u32[]{:S(2)}, u32[]{:S(2)}) collective-permute-start(f32[384,128]{1,0:T(8,128)S(1)} %collective-permute-done.9.across_refs_2_), channel_id=1, source_target_pairs={{0,112},{16,0},{32,16},{48,32},{64,48},{80,64},{96,80},{112,96},{1... | collective-permute-start | bytes 589832 | tf_op jit(solution)/shard_map/panel/ppermute | solution.py:386
  65.3 0.7 copy-start.5
  79.3 13.5 %collective-permute-start.8 = (f32[384,128]{1,0:T(8,128)S(1)}, f32[384,128]{1,0:T(8,128)S(1)}, u32[]{:S(2)}, u32[]{:S(2)}) collective-permute-start(f32[384,128]{1,0:T(8,128)S(1)} %collective-permute-done.7.across_refs_1_), channel_id=1, source_target_pairs={{0,16},{16,32},{32,48},{48,64},{64,80},{80,96},{96,112},{112,0},{1... | collective-permute-start | bytes 589832 | tf_op jit(solution)/shard_map/panel/ppermute | solution.py:385
  79.3 0.7 copy-start.7
  80.0 17.5 %collective-permute-start.14 = (f32[384,128]{1,0:T(8,128)S(1)}, f32[384,128]{1,0:T(8,128)S(1)}, u32[]{:S(2)}, u32[]{:S(2)}) collective-permute-start(f32[384,128]{1,0:T(8,128)S(1)} %assemble_pivot_rows.1.across_refs_0_), channel_id=1, source_target_pairs={{0,128},{1,144},{2,160},{3,176},{4,192},{5,208},{6,224},{7,240},{8... | collective-permute-start | bytes 589832 | tf_op jit(solution)/shard_map/panel/ppermute | solution.py:498
  92.9 7.9 %collective-permute-start.12 = (f32[384,128]{1,0:T(8,128)S(1)}, f32[384,128]{1,0:T(8,128)S(1)}, u32[]{:S(2)}, u32[]{:S(2)}) collective-permute-start(f32[384,128]{1,0:T(8,128)S(1)} %collective-permute-done.8.across_refs_3_), channel_id=1, source_target_pairs={{0,16},{16,32},{32,48},{48,64},{64,80},{80,96},{96,112},{112,0},{1... | collective-permute-start | bytes 589832 | tf_op jit(solution)/shard_map/panel/ppermute | solution.py:385
  92.9 0.7 copy-start.11
  93.5 7.5 %collective-permute-start.13 = (f32[384,128]{1,0:T(8,128)S(1)}, f32[384,128]{1,0:T(8,128)}, u32[]{:S(2)}, u32[]{:S(2)}) collective-permute-start(f32[384,128]{1,0:T(8,128)S(1)} %collective-permute-done.10.across_refs_4_), channel_id=1, source_target_pairs={{0,112},{16,0},{32,16},{48,32},{64,48},{80,64},{96,80},{112,96},{1... | collective-permute-start | bytes 589832 | tf_op jit(solution)/shard_map/panel/ppermute | solution.py:386
  96.8 0.7 copy-start.9
  100.8 7.5 %copy-start.1 = (f32[384,128]{1,0:T(8,128)}, f32[384,128]{1,0:T(8,128)S(1)}, u32[]{:S(2)}) copy-start(f32[384,128]{1,0:T(8,128)S(1)} %collective-permute-done.12.across_refs_5_) | copy-start | bytes 589828
  101.9 6.5 %collective-permute-start.15 = (f32[192,128]{1,0:T(8,128)S(1)}, f32[192,128]{1,0:T(8,128)S(1)}, u32[]{:S(2)}, u32[]{:S(2)}) collective-permute-start(f32[192,128]{1,0:T(8,128)S(1)} %slice.50), channel_id=1, source_target_pairs={{0,16},{16,32},{32,48},{48,64},{64,80},{80,96},{96,112},{112,0},{1... | collective-permute-start | bytes 294920 | tf_op jit(solution)/shard_map/panel/ppermute | solution.py:392
  102.8 6.0 %collective-permute-start.16 = (f32[192,128]{1,0:T(8,128)S(1)}, f32[192,128]{1,0:T(8,128)S(1)}, u32[]{:S(2)}, u32[]{:S(2)}) collective-permute-start(f32[192,128]{1,0:T(8,128)S(1)} %slice.51), channel_id=1, source_target_pairs={{0,112},{16,0},{32,16},{48,32},{64,48},{80,64},{96,80},{112,96},{1... | collective-permute-start | bytes 294920 | tf_op jit(solution)/shard_map/panel/ppermute | solution.py:392
  108.9 0.9 copy-start.2
  109.8 2.2 %copy-start.4 = (f32[128,64,128]{2,1,0:T(8,128)S(1)}, f32[128,64,128]{2,1,0:T(8,128)}, u32[]{:S(2)}) copy-start(f32[128,64,128]{2,1,0:T(8,128)} %all-gather.6.cloned.1.call-done) | copy-start | bytes 12582916
  112.0 0.9 copy-start.6
  113.0 0.9 copy-start.8
  113.9 0.9 copy-start.10
  114.8 0.9 copy-start.12
  159.3 1.3 copy-start.13
  160.6 1.4 copy-start.15
  162.0 0.9 copy-start.17
  162.9 0.9 copy-start.19
  163.8 0.8 copy-start.21
  164.6 0.8 copy-start.23
  165.3 0.7 copy-start.25
  166.0 1.7 copy-start.3
  167.7 1.6 copy-start.14
  169.3 1.6 copy-start.16
  170.9 1.1 copy-start.18
  172.0 1.1 copy-start.20
  173.1 1.0 copy-start.22
  174.2 1.0 copy-start.24
  175.2 0.9 copy-start.26
Sparse Core Ops, SparseCore 0:
  50.0 53.4 all-gather.5
  105.3 46.1 all-gather.3

commit v8 on v5

--- a/solution.py
+++ b/solution.py
@@ -364,10 +364,8 @@
     for turn in range(3):
         behind = lax.ppermute(behind, "row", up)
         ahead = lax.ppermute(ahead, "row", down)
-        if turn:
-            behind, ahead, beside[turn - 1] = lax.optimization_barrier(
-                (behind, ahead, beside[turn - 1])
-            )
+        if turn < len(beside):
+            behind, ahead, beside[turn] = lax.optimization_barrier((behind, ahead, beside[turn]))
         blocks += [behind, ahead]
     last = [lax.ppermute(behind[:half], "row", up), lax.ppermute(ahead[half:], "row", down)]
     return blocks + [jnp.concatenate(last)]

time: 187 us -> 187 us (level)
  waiting for transfers between devices: 49.7 us -> 47.4 us
    ppermute x3, waiting for transfers between devices: 2.14 us -> 8.41 us  [ring_gather(): behind = lax.ppermute(behind, 'row', up)]
    all_gather x1, waiting for transfers between devices: 5.35 us -> 0.01 us  [body(): beneath = lax.all_gather(turned, 'col')]
    ppermute x1, starting transfers between devices: 4.94 us -> 0.63 us  [ring_gather(): lax.ppermute(behind[:half], 'row', up)]
    ppermute x2, starting transfers between devices: 2.21 us -> 5.75 us  [body(): beside = [lax.ppermute(pivot_columns, ALL, route) for route in routes]]
    ppermute x1, waiting for transfers between devices: 3 us -> 0.16 us  [ring_gather(): lax.ppermute(ahead[half:], 'row', down)]
    ppermute x1, starting transfers between devices: 0.26 us -> 2.49 us  [ring_gather(): lax.ppermute(ahead[half:], 'row', down)]
    ppermute x3, waiting for transfers between devices: 2.61 us -> 0.45 us  [ring_gather(): ahead = lax.ppermute(ahead, 'row', down)]
    ppermute x2, waiting for transfers between devices: 19.4 us -> 21.6 us  [body(): beside = [lax.ppermute(pivot_columns, ALL, route) for route in routes]]
  transfers between devices with their start and end apart: 19 -> 19, of which waited for: 14 -> 11; matrix products, arithmetic and copies ran while one was open for 3% -> 3% of each run, Pallas kernels for 21% -> 21%
where the time goes in v8:
time: 187 us; the launch traced here: 184 us
  Pallas kernels  64.2 us (34%)
  waiting for transfers between devices  47.4 us (25%)
  starting transfers between devices  45.3 us (24%)
  between operations  14.9 us (8%)
  local copies, waits for them, and re-layouts  8.28 us (4%)
  other arithmetic  4.39 us (2%)
    pallas_call x1, Pallas kernels, factor(): pl.pallas_call(factor_kernel, out_shape=(jax.ShapeDtypeStruct((NPIV, NPIV...  38.3 us
    pallas_call x1, Pallas kernels, finish(): pl.pallas_call(finish_kernel, grid=(2,), out_shape=jax.ShapeDtypeStruct((...  25.3 us
    ppermute x2, waiting for transfers between devices, body(): beside = [lax.ppermute(pivot_columns, ALL, route) for route in routes]  21.6 us
    ppermute x3, starting transfers between devices, ring_gather(): ahead = lax.ppermute(ahead, 'row', down)  10.9 us
    ppermute x3, starting transfers between devices, body(): came = lax.ppermute(mine, 'row', [(i, i ^ bit) for i in range(8)])  10.6 us
    ppermute x3, waiting for transfers between devices, body(): came = lax.ppermute(mine, 'row', [(i, i ^ bit) for i in range(8)])  8.66 us
    ppermute x3, waiting for transfers between devices, ring_gather(): behind = lax.ppermute(behind, 'row', up)  8.41 us
    ppermute x2, starting transfers between devices, body(): beside = [lax.ppermute(pivot_columns, ALL, route) for route in routes]  5.75 us
  transfers between devices with their start and end apart: 19, of which 11 were waited for; matrix products, arithmetic and copies ran while one was open for 3% of the time, Pallas kernels for 21%

profile of v8, /device:TPU:2, one launch (start us, length us, event | category | flops | bytes accessed | tf_op | source)
XLA Modules:
  0.0 184.5 jit_solution(1645292046821913313)
XLA Ops:
  6.5 0.8 reshape.95
  7.3 0.7 constant_dynamic-slice_fusion
  9.3 0.9 fusion.2
  10.2 5.1 %collective-permute-start.1 = (f32[64,128]{1,0:T(8,128)S(1)}, f32[64,128]{1,0:T(8,128)S(1)}, u32[]{:S(2)}, u32[]{:S(2)}) collective-permute-start(f32[64,128]{1,0:T(8,128)S(1)} %get-tuple-element.52), channel_id=1, source_target_pairs={{0,8},{1,9},{2,10},{3,11},{4,12},{5,13},{6,14},{7,15},{16,24},{17,... | collective-permute-start | bytes 98312 | tf_op jit(solution)/shard_map/pivot_block/ppermute | solution.py:433
  15.3 2.9 %collective-permute-start.2 = (f32[64,128]{1,0:T(8,128)S(1)}, f32[64,128]{1,0:T(8,128)S(1)}, u32[]{:S(2)}, u32[]{:S(2)}) collective-permute-start(f32[64,128]{1,0:T(8,128)S(1)} %get-tuple-element.52), channel_id=1, source_target_pairs={{0,136},{1,137},{2,138},{3,139},{4,140},{5,141},{6,142},{7,143},{1... | collective-permute-start | bytes 98312 | tf_op jit(solution)/shard_map/pivot_block/ppermute | solution.py:434
  18.2 3.3 %collective-permute-start = (f32[64,128]{1,0:T(8,128)S(1)}, f32[64,128]{1,0:T(8,128)S(1)}, u32[]{:S(2)}, u32[]{:S(2)}) collective-permute-start(f32[64,128]{1,0:T(8,128)S(1)} %get-tuple-element.51), channel_id=1, source_target_pairs={{0,128},{1,129},{2,130},{3,131},{4,132},{5,133},{6,134},{7,135},{1... | collective-permute-start | bytes 98312 | tf_op jit(solution)/shard_map/pivot_block/ppermute | solution.py:432
  21.5 1.6 fusion.1
  23.2 0.1 pad_maximum_fusion
  23.3 2.2 %collective-permute-done = f32[64,128]{1,0:T(8,128)S(1)} collective-permute-done((f32[64,128]{1,0:T(8,128)S(1)}, f32[64,128]{1,0:T(8,128)S(1)}, u32[]{:S(2)}, u32[]{:S(2)}) %collective-permute-start) | collective-permute-done | bytes 32800 | tf_op jit(solution)/shard_map/pivot_block/ppermute | solution.py:432
  25.5 1.5 collective-permute-start.6
  27.0 7.2 %collective-permute-start.3 = (f32[1,64,128]{2,1,0:T(8,128)S(1)}, f32[1,64,128]{2,1,0:T(8,128)S(1)}, u32[]{:S(2)}, u32[]{:S(2)}) collective-permute-start(f32[1,64,128]{2,1,0:T(8,128)S(1)} %bitcast.25), channel_id=1, source_target_pairs={{0,64},{16,80},{32,96},{48,112},{64,0},{80,16},{96,32},{112,48},{1... | collective-permute-start | bytes 98312 | tf_op jit(solution)/shard_map/pivot_gather/ppermute | solution.py:446
  34.2 1.9 %collective-permute-done.3 = f32[1,64,128]{2,1,0:T(8,128)S(1)} collective-permute-done((f32[1,64,128]{2,1,0:T(8,128)S(1)}, f32[1,64,128]{2,1,0:T(8,128)S(1)}, u32[]{:S(2)}, u32[]{:S(2)}) %collective-permute-start.3) | collective-permute-done | bytes 32800 | tf_op jit(solution)/shard_map/pivot_gather/ppermute | solution.py:446
  36.1 2.0 %collective-permute-start.4 = (f32[2,64,128]{2,1,0:T(8,128)S(1)}, f32[2,64,128]{2,1,0:T(8,128)S(1)}, u32[]{:S(2)}, u32[]{:S(2)}) collective-permute-start(f32[2,64,128]{2,1,0:T(8,128)S(1)} %pad_maximum_fusion.4), channel_id=1, source_target_pairs={{0,32},{16,48},{32,0},{48,16},{64,96},{80,112},{96,64},{112,80},{1... | collective-permute-start | bytes 196616 | tf_op jit(solution)/shard_map/pivot_gather/ppermute | solution.py:446
  38.1 3.2 %collective-permute-done.4 = f32[2,64,128]{2,1,0:T(8,128)S(1)} collective-permute-done((f32[2,64,128]{2,1,0:T(8,128)S(1)}, f32[2,64,128]{2,1,0:T(8,128)S(1)}, u32[]{:S(2)}, u32[]{:S(2)}) %collective-permute-start.4) | collective-permute-done | bytes 65568 | tf_op jit(solution)/shard_map/pivot_gather/ppermute | solution.py:446
  41.3 1.4 collective-permute-start.5
  42.7 3.6 %collective-permute-done.5 = f32[4,64,128]{2,1,0:T(8,128)S(1)} collective-permute-done((f32[4,64,128]{2,1,0:T(8,128)S(1)}, f32[4,64,128]{2,1,0:T(8,128)S(1)}, u32[]{:S(2)}, u32[]{:S(2)}) %collective-permute-start.5) | collective-permute-done | bytes 131104 | tf_op jit(solution)/shard_map/pivot_gather/ppermute | solution.py:446
  46.3 0.7 pad_maximum_fusion.1
  47.0 3.5 %collective-permute-done.6.came_ref = f32[2,1024,128]{2,1,0:T(8,128)S(1)} collective-permute-done((f32[2,1024,128]{2,1,0:T(8,128)S(1)}, f32[2,1024,128]{2,1,0:T(8,128)S(1)}, u32[]{:S(2)}, u32[]{:S(2)}) %collective-permute-start.6) | collective-permute-done | bytes 1048608 | tf_op jit(solution)/shard_map/siblings/ppermute | solution.py:441
  50.7 0.1 reshape.93
  50.7 0.9 slice.47.front_ref
  51.7 0.2 dynamic-slice_reduce_fusion
  51.9 0.1 reshape.96
  52.0 0.2 fusion.4
  52.2 0.1 copy.6
  52.3 0.1 reshape.94
  52.4 0.1 concatenate.31.meta_ref
  52.5 1.0 slice_bitcast_fusion.child_ref
  53.5 0.7 assemble_pivot_rows.1.across_refs_0_
  54.2 2.0 %collective-permute-start.7 = (f32[384,128]{1,0:T(8,128)S(1)}, f32[384,128]{1,0:T(8,128)S(1)}, u32[]{:S(2)}, u32[]{:S(2)}) collective-permute-start(f32[384,128]{1,0:T(8,128)S(1)} %assemble_pivot_rows.1.across_refs_0_), channel_id=1, source_target_pairs={{0,16},{16,32},{32,48},{48,64},{64,80},{80,96},{96,112},{112,0},{1... | collective-permute-start | bytes 589832 | tf_op jit(solution)/shard_map/panel/ppermute | solution.py:365
  56.2 4.0 %collective-permute-start.8 = (f32[384,128]{1,0:T(8,128)S(1)}, f32[384,128]{1,0:T(8,128)S(1)}, u32[]{:S(2)}, u32[]{:S(2)}) collective-permute-start(f32[384,128]{1,0:T(8,128)S(1)} %assemble_pivot_rows.1.across_refs_0_), channel_id=1, source_target_pairs={{0,112},{16,0},{32,16},{48,32},{64,48},{80,64},{96,80},{112,96},{1... | collective-permute-start | bytes 589832 | tf_op jit(solution)/shard_map/panel/ppermute | solution.py:366
  60.2 2.1 %collective-permute-start.9 = (f32[384,128]{1,0:T(8,128)S(1)}, f32[384,128]{1,0:T(8,128)S(1)}, u32[]{:S(2)}, u32[]{:S(2)}) collective-permute-start(f32[384,128]{1,0:T(8,128)S(1)} %assemble_pivot_rows.1.across_refs_0_), channel_id=1, source_target_pairs={{0,0},{1,16},{2,32},{3,48},{4,64},{5,80},{6,96},{7,112},{8,8},{9,2... | collective-permute-start | bytes 589832 | tf_op jit(solution)/shard_map/panel/ppermute | solution.py:476
  62.3 3.6 %collective-permute-start.12 = (f32[384,128]{1,0:T(8,128)S(1)}, f32[384,128]{1,0:T(8,128)S(1)}, u32[]{:S(2)}, u32[]{:S(2)}) collective-permute-start(f32[384,128]{1,0:T(8,128)S(1)} %assemble_pivot_rows.1.across_refs_0_), channel_id=1, source_target_pairs={{0,128},{1,144},{2,160},{3,176},{4,192},{5,208},{6,224},{7,240},{8... | collective-permute-start | bytes 589832 | tf_op jit(solution)/shard_map/panel/ppermute | solution.py:476
  66.0 21.6 %collective-permute-done.9 = f32[384,128]{1,0:T(8,128)S(1)} collective-permute-done((f32[384,128]{1,0:T(8,128)S(1)}, f32[384,128]{1,0:T(8,128)S(1)}, u32[]{:S(2)}, u32[]{:S(2)}) %collective-permute-start.9) | collective-permute-done | bytes 196640 | tf_op jit(solution)/shard_map/panel/ppermute | solution.py:476
  87.5 3.2 %collective-permute-start.11 = (f32[384,128]{1,0:T(8,128)S(1)}, f32[384,128]{1,0:T(8,128)S(1)}, u32[]{:S(2)}, u32[]{:S(2)}) collective-permute-start(f32[384,128]{1,0:T(8,128)S(1)} %collective-permute-done.8.across_refs_2_), channel_id=1, source_target_pairs={{0,112},{16,0},{32,16},{48,32},{64,48},{80,64},{96,80},{112,96},{1... | collective-permute-start | bytes 589832 | tf_op jit(solution)/shard_map/panel/ppermute | solution.py:366
  90.8 4.9 %collective-permute-done.10.across_refs_3_ = f32[384,128]{1,0:T(8,128)S(1)} collective-permute-done((f32[384,128]{1,0:T(8,128)S(1)}, f32[384,128]{1,0:T(8,128)S(1)}, u32[]{:S(2)}, u32[]{:S(2)}) %collective-permute-start.10) | collective-permute-done | bytes 196640 | tf_op jit(solution)/shard_map/panel/ppermute | solution.py:365
  95.6 0.8 maximum_select_fusion
  96.4 0.1 collective-permute-start.13
  96.5 3.6 %collective-permute-start.14 = (f32[384,128]{1,0:T(8,128)S(1)}, f32[384,128]{1,0:T(8,128)S(1)}, u32[]{:S(2)}, u32[]{:S(2)}) collective-permute-start(f32[384,128]{1,0:T(8,128)S(1)} %collective-permute-done.11.across_refs_4_), channel_id=1, source_target_pairs={{0,112},{16,0},{32,16},{48,32},{64,48},{80,64},{96,80},{112,96},{1... | collective-permute-start | bytes 589832 | tf_op jit(solution)/shard_map/panel/ppermute | solution.py:366
  100.2 3.6 %collective-permute-done.13.across_refs_5_ = f32[384,128]{1,0:T(8,128)S(1)} collective-permute-done((f32[384,128]{1,0:T(8,128)S(1)}, f32[384,128]{1,0:T(8,128)S(1)}, u32[]{:S(2)}, u32[]{:S(2)}) %collective-permute-start.13) | collective-permute-done | bytes 196640 | tf_op jit(solution)/shard_map/panel/ppermute | solution.py:365
  103.7 0.6 collective-permute-start.15
  104.4 0.4 collective-permute-done.14.across_refs_6_
  104.8 2.5 %collective-permute-start.16 = (f32[192,128]{1,0:T(8,128)S(1)}, f32[192,128]{1,0:T(8,128)S(1)}, u32[]{:S(2)}, u32[]{:S(2)}) collective-permute-start(f32[192,128]{1,0:T(8,128)S(1)} %slice.60), channel_id=1, source_target_pairs={{0,112},{16,0},{32,16},{48,32},{64,48},{80,64},{96,80},{112,96},{1... | collective-permute-start | bytes 294920 | tf_op jit(solution)/shard_map/panel/ppermute | solution.py:370
  107.3 2.3 %collective-permute-done.15 = f32[192,128]{1,0:T(8,128)S(1)} collective-permute-done((f32[192,128]{1,0:T(8,128)S(1)}, f32[192,128]{1,0:T(8,128)S(1)}, u32[]{:S(2)}, u32[]{:S(2)}) %collective-permute-start.15) | collective-permute-done | bytes 98336 | tf_op jit(solution)/shard_map/panel/ppermute | solution.py:370
  109.6 0.2 collective-permute-done.16
  109.8 2.2 %copy-done = f32[128,64,128]{2,1,0:T(8,128)S(1)} copy-done((f32[128,64,128]{2,1,0:T(8,128)S(1)}, f32[128,64,128]{2,1,0:T(8,128)}, u32[]{:S(2)}) %copy-start) | copy-done | bytes 4194328
  112.0 38.3 %factor_pivots.1 = (f32[1024,1024]{1,0:T(8,128)S(1)}, f32[8,128,128]{2,1,0:T(8,128)S(1)}) custom-call(s32[1]{0:T(128)} %bitcast.1.row_ref, f32[16,8,64,128]{3,2,1,0:T(8,128)S(1)} %bitcast.21), custom_call_target="tpu_custom_call" | custom-call | flops 49999998976 | bytes 9437184 | tf_op jit(solution)/shard_map/factor/factor_pivots/pallas_call | solution.py:143
  150.3 2.0 %copy-done.1 = f32[1024,1024]{1,0:T(8,128)} copy-done((f32[1024,1024]{1,0:T(8,128)}, f32[1024,1024]{1,0:T(8,128)S(1)}, u32[]{:S(2)}) %copy-start.1) | copy-done | bytes 4194328
  152.4 25.3 %solve_and_update.1 = f32[3,4,128,384]{3,2,1,0:T(8,128)} custom-call(s32[24]{0:T(128)S(1)} %concatenate.31.meta_ref, f32[3,4,128,384]{3,2,1,0:T(8,128)} %bitcast.31, f32[2,4,128,512]{3,2,1,0:T(8,128)} %bitcast.24, f32[2,2,4,128,128]{4,3,2,1,0:T(8,128)S(1)} %bitcast.20, f32[384,128]{1,0:T(8,128)S(1)} %assemble_pivot_rows.1.across_refs_0_, ...), custom_call_target="tpu_custom_call" | custom-call | flops 15000000512 | bytes 25165824 | tf_op jit(solution)/shard_map/finish/solve_and_update/pallas_call | solution.py:309
  (27 shorter events, 0.2 us)
Async XLA Ops:
  6.5 103.3 %all-gather.6.cloned.1.call-start = ((), (), s32[]{:S(2)}) async-start(), calls=%async_computation.1 | async-start | bytes 4456448 | tf_op jit(solution)/shard_map/pivot_gather/all_gather | solution.py:449
  10.2 13.1 %collective-permute-start.1 = (f32[64,128]{1,0:T(8,128)S(1)}, f32[64,128]{1,0:T(8,128)S(1)}, u32[]{:S(2)}, u32[]{:S(2)}) collective-permute-start(f32[64,128]{1,0:T(8,128)S(1)} %get-tuple-element.52), channel_id=1, source_target_pairs={{0,8},{1,9},{2,10},{3,11},{4,12},{5,13},{6,14},{7,15},{16,24},{17,... | collective-permute-start | bytes 98312 | tf_op jit(solution)/shard_map/pivot_block/ppermute | solution.py:433
  15.3 8.0 %collective-permute-start.2 = (f32[64,128]{1,0:T(8,128)S(1)}, f32[64,128]{1,0:T(8,128)S(1)}, u32[]{:S(2)}, u32[]{:S(2)}) collective-permute-start(f32[64,128]{1,0:T(8,128)S(1)} %get-tuple-element.52), channel_id=1, source_target_pairs={{0,136},{1,137},{2,138},{3,139},{4,140},{5,141},{6,142},{7,143},{1... | collective-permute-start | bytes 98312 | tf_op jit(solution)/shard_map/pivot_block/ppermute | solution.py:434
  18.2 7.3 %collective-permute-start = (f32[64,128]{1,0:T(8,128)S(1)}, f32[64,128]{1,0:T(8,128)S(1)}, u32[]{:S(2)}, u32[]{:S(2)}) collective-permute-start(f32[64,128]{1,0:T(8,128)S(1)} %get-tuple-element.51), channel_id=1, source_target_pairs={{0,128},{1,129},{2,130},{3,131},{4,132},{5,133},{6,134},{7,135},{1... | collective-permute-start | bytes 98312 | tf_op jit(solution)/shard_map/pivot_block/ppermute | solution.py:432
  23.2 27.5 %copy-start.2 = (s32[2,64]{1,0:T(2,128)S(1)}, s32[2,64]{1,0:T(2,128)}, u32[]{:S(2)}) copy-start(s32[2,64]{1,0:T(2,128)} %param.5) | copy-start | bytes 1540
  25.5 25.1 %collective-permute-start.6 = (f32[2,1024,128]{2,1,0:T(8,128)S(1)}, f32[2,1024,128]{2,1,0:T(8,128)S(1)}, u32[]{:S(2)}, u32[]{:S(2)}) collective-permute-start(f32[2,1024,128]{2,1,0:T(8,128)S(1)} %pad_maximum_fusion), channel_id=1, source_target_pairs={{0,128},{128,0},{1,129},{129,1},{2,130},{130,2},{3,131},{131,3},{4... | collective-permute-start | bytes 3145736 | tf_op jit(solution)/shard_map/siblings/ppermute | solution.py:441
  27.0 9.1 %collective-permute-start.3 = (f32[1,64,128]{2,1,0:T(8,128)S(1)}, f32[1,64,128]{2,1,0:T(8,128)S(1)}, u32[]{:S(2)}, u32[]{:S(2)}) collective-permute-start(f32[1,64,128]{2,1,0:T(8,128)S(1)} %bitcast.25), channel_id=1, source_target_pairs={{0,64},{16,80},{32,96},{48,112},{64,0},{80,16},{96,32},{112,48},{1... | collective-permute-start | bytes 98312 | tf_op jit(solution)/shard_map/pivot_gather/ppermute | solution.py:446
  36.1 5.2 %collective-permute-start.4 = (f32[2,64,128]{2,1,0:T(8,128)S(1)}, f32[2,64,128]{2,1,0:T(8,128)S(1)}, u32[]{:S(2)}, u32[]{:S(2)}) collective-permute-start(f32[2,64,128]{2,1,0:T(8,128)S(1)} %pad_maximum_fusion.4), channel_id=1, source_target_pairs={{0,32},{16,48},{32,0},{48,16},{64,96},{80,112},{96,64},{112,80},{1... | collective-permute-start | bytes 196616 | tf_op jit(solution)/shard_map/pivot_gather/ppermute | solution.py:446
  41.3 5.1 %collective-permute-start.5 = (f32[4,64,128]{2,1,0:T(8,128)S(1)}, f32[4,64,128]{2,1,0:T(8,128)S(1)}, u32[]{:S(2)}, u32[]{:S(2)}) collective-permute-start(f32[4,64,128]{2,1,0:T(8,128)S(1)} %pad_maximum_fusion.3), channel_id=1, source_target_pairs={{0,16},{16,0},{32,48},{48,32},{64,80},{80,64},{96,112},{112,96},{1... | collective-permute-start | bytes 393224 | tf_op jit(solution)/shard_map/pivot_gather/ppermute | solution.py:446
  50.6 101.8 %all-gather.4.cloned.1.call-start = ((), (), s32[]{:S(2)}) async-start(), calls=%async_computation | async-start | bytes 6684672 | tf_op jit(solution)/shard_map/panel/all_gather | solution.py:482
  54.2 11.8 %collective-permute-start.7 = (f32[384,128]{1,0:T(8,128)S(1)}, f32[384,128]{1,0:T(8,128)S(1)}, u32[]{:S(2)}, u32[]{:S(2)}) collective-permute-start(f32[384,128]{1,0:T(8,128)S(1)} %assemble_pivot_rows.1.across_refs_0_), channel_id=1, source_target_pairs={{0,16},{16,32},{32,48},{48,64},{64,80},{80,96},{96,112},{112,0},{1... | collective-permute-start | bytes 589832 | tf_op jit(solution)/shard_map/panel/ppermute | solution.py:365
  56.2 9.8 %collective-permute-start.8 = (f32[384,128]{1,0:T(8,128)S(1)}, f32[384,128]{1,0:T(8,128)S(1)}, u32[]{:S(2)}, u32[]{:S(2)}) collective-permute-start(f32[384,128]{1,0:T(8,128)S(1)} %assemble_pivot_rows.1.across_refs_0_), channel_id=1, source_target_pairs={{0,112},{16,0},{32,16},{48,32},{64,48},{80,64},{96,80},{112,96},{1... | collective-permute-start | bytes 589832 | tf_op jit(solution)/shard_map/panel/ppermute | solution.py:366
  60.2 27.3 %collective-permute-start.9 = (f32[384,128]{1,0:T(8,128)S(1)}, f32[384,128]{1,0:T(8,128)S(1)}, u32[]{:S(2)}, u32[]{:S(2)}) collective-permute-start(f32[384,128]{1,0:T(8,128)S(1)} %assemble_pivot_rows.1.across_refs_0_), channel_id=1, source_target_pairs={{0,0},{1,16},{2,32},{3,48},{4,64},{5,80},{6,96},{7,112},{8,8},{9,2... | collective-permute-start | bytes 589832 | tf_op jit(solution)/shard_map/panel/ppermute | solution.py:476
  62.3 28.4 %collective-permute-start.12 = (f32[384,128]{1,0:T(8,128)S(1)}, f32[384,128]{1,0:T(8,128)S(1)}, u32[]{:S(2)}, u32[]{:S(2)}) collective-permute-start(f32[384,128]{1,0:T(8,128)S(1)} %assemble_pivot_rows.1.across_refs_0_), channel_id=1, source_target_pairs={{0,128},{1,144},{2,160},{3,176},{4,192},{5,208},{6,224},{7,240},{8... | collective-permute-start | bytes 589832 | tf_op jit(solution)/shard_map/panel/ppermute | solution.py:476
  87.5 8.1 %collective-permute-start.10 = (f32[384,128]{1,0:T(8,128)S(1)}, f32[384,128]{1,0:T(8,128)S(1)}, u32[]{:S(2)}, u32[]{:S(2)}) collective-permute-start(f32[384,128]{1,0:T(8,128)S(1)} %collective-permute-done.7.across_refs_1_), channel_id=1, source_target_pairs={{0,16},{16,32},{32,48},{48,64},{64,80},{80,96},{96,112},{112,0},{1... | collective-permute-start | bytes 589832 | tf_op jit(solution)/shard_map/panel/ppermute | solution.py:365
  87.5 8.1 %collective-permute-start.11 = (f32[384,128]{1,0:T(8,128)S(1)}, f32[384,128]{1,0:T(8,128)S(1)}, u32[]{:S(2)}, u32[]{:S(2)}) collective-permute-start(f32[384,128]{1,0:T(8,128)S(1)} %collective-permute-done.8.across_refs_2_), channel_id=1, source_target_pairs={{0,112},{16,0},{32,16},{48,32},{64,48},{80,64},{96,80},{112,96},{1... | collective-permute-start | bytes 589832 | tf_op jit(solution)/shard_map/panel/ppermute | solution.py:366
  96.4 7.3 %collective-permute-start.13 = (f32[384,128]{1,0:T(8,128)S(1)}, f32[384,128]{1,0:T(8,128)S(1)}, u32[]{:S(2)}, u32[]{:S(2)}) collective-permute-start(f32[384,128]{1,0:T(8,128)S(1)} %collective-permute-done.10.across_refs_3_), channel_id=1, source_target_pairs={{0,16},{16,32},{32,48},{48,64},{64,80},{80,96},{96,112},{112,0},{1... | collective-permute-start | bytes 589832 | tf_op jit(solution)/shard_map/panel/ppermute | solution.py:365
  96.5 8.3 %collective-permute-start.14 = (f32[384,128]{1,0:T(8,128)S(1)}, f32[384,128]{1,0:T(8,128)S(1)}, u32[]{:S(2)}, u32[]{:S(2)}) collective-permute-start(f32[384,128]{1,0:T(8,128)S(1)} %collective-permute-done.11.across_refs_4_), channel_id=1, source_target_pairs={{0,112},{16,0},{32,16},{48,32},{64,48},{80,64},{96,80},{112,96},{1... | collective-permute-start | bytes 589832 | tf_op jit(solution)/shard_map/panel/ppermute | solution.py:366
  103.7 5.9 %collective-permute-start.15 = (f32[192,128]{1,0:T(8,128)S(1)}, f32[192,128]{1,0:T(8,128)S(1)}, u32[]{:S(2)}, u32[]{:S(2)}) collective-permute-start(f32[192,128]{1,0:T(8,128)S(1)} %slice.59), channel_id=1, source_target_pairs={{0,16},{16,32},{32,48},{48,64},{64,80},{80,96},{96,112},{112,0},{1... | collective-permute-start | bytes 294920 | tf_op jit(solution)/shard_map/panel/ppermute | solution.py:370
  104.8 5.0 %collective-permute-start.16 = (f32[192,128]{1,0:T(8,128)S(1)}, f32[192,128]{1,0:T(8,128)S(1)}, u32[]{:S(2)}, u32[]{:S(2)}) collective-permute-start(f32[192,128]{1,0:T(8,128)S(1)} %slice.60), channel_id=1, source_target_pairs={{0,112},{16,0},{32,16},{48,32},{64,48},{80,64},{96,80},{112,96},{1... | collective-permute-start | bytes 294920 | tf_op jit(solution)/shard_map/panel/ppermute | solution.py:370
  109.8 2.2 %copy-start = (f32[128,64,128]{2,1,0:T(8,128)S(1)}, f32[128,64,128]{2,1,0:T(8,128)}, u32[]{:S(2)}) copy-start(f32[128,64,128]{2,1,0:T(8,128)} %all-gather.6.cloned.1.call-done) | copy-start | bytes 12582916
  150.3 2.1 %copy-start.1 = (f32[1024,1024]{1,0:T(8,128)}, f32[1024,1024]{1,0:T(8,128)S(1)}, u32[]{:S(2)}) copy-start(f32[1024,1024]{1,0:T(8,128)S(1)} %get-tuple-element.47.upper_ref) | copy-start | bytes 12582916
Sparse Core Ops, SparseCore 0:
  50.7 53.1 all-gather.5
  105.7 42.7 all-gather.3
